TPU v7x, 256 devices: a whole 4x4x8 slice. The times are simulated.
256 devices in a mesh: replica: 32 (over x, z), tensor: 8 (over y, core).
Axes of the slice: x: 4, y: 4, z: 8, core: 2. Of those that a mesh axis runs over, the one named last changes fastest.
Arguments:
- ssm_state: bfloat16 [128, 128, 4096], P('replica', None, 'tensor'), may hold values from -6 to 6
- kcache: bfloat16 [128, 1024, 1024], P('replica', None, 'tensor'), may hold values from -6 to 6
- vcache: bfloat16 [128, 1024, 1024], P('replica', None, 'tensor'), may hold values from -6 to 6
- lengths: int32 [32], replicated, may hold values from 128 to 1024, as said below
- parents: int32 [2, 128], replicated, may hold values from 0 to 127, as said below
- x_in: bfloat16 [2, 128, 4096], P(None, 'replica', 'tensor'), may hold values from -6 to 6
- z_in: bfloat16 [2, 128, 4096], P(None, 'replica', 'tensor'), may hold values from -6 to 6
- dt_in: bfloat16 [2, 128, 64], P(None, 'replica', 'tensor'), may hold values from -4 to 4
- b_in: bfloat16 [2, 128, 128], P(None, 'replica'), may hold values from -0.5 to 0.5
- c_in: bfloat16 [2, 128, 128], P(None, 'replica'), may hold values from -0.5 to 0.5
- q_in: bfloat16 [2, 128, 8192], P(None, 'replica', 'tensor'), may hold values from -100 to 100
- kv_new: bfloat16 [2, 128, 2, 1024], P(None, 'replica', None, 'tensor'), may hold values from -12 to 12
- a_rate: float32 [64], P('tensor'), may hold values from 0.05 to 8
- dt_bias: float32 [64], P('tensor'), may hold values from -3 to 0
- skip: float32 [64], P('tensor'), may hold values from 0.5 to 1.5
- gain: float32 [4096], P('tensor'), may hold values from 0.5 to 1.5
- out_proj: bfloat16 [4096, 4096], P('tensor'), may hold values from -0.09375 to 0.09375
Outputs:
- final_state: bfloat16 [128, 128, 4096], P('replica', None, 'tensor')
- mamba_out: bfloat16 [2, 128, 4096], P(None, 'replica', 'tensor')
- attn_out: bfloat16 [2, 128, 8192], P(None, 'replica', 'tensor')
Inputs may be any that keep to these rules, and one draw needn't show every extreme that they name: In each step the 4 slots of a prompt take their parents among the 4 slots of one prompt, and each prompt is that source for exactly one prompt. `lengths`: multiples of 128; some prompt's cache is full.
All inputs are finite; a program needn't handle non-finite values.
Results may differ from a plain program's by a relative error of at most 0.019.
Values may be sent and summed in bfloat16 or wider, within the bound.
No kernel may reach another device: no remote copies, remote signals or barrier semaphores. Data moves between devices by JAX's collectives and lax.ppermute only.
A program may use at most 64 MiB of HBM per device.

v0:
```python
import jax
import jax.numpy as jnp
from jax import lax
from jax.sharding import PartitionSpec as P

HEAD = 64
NORM_GROUP = 512
HD = 128
BEAM = 4


MASKED = -1e30


def gated_norm(ssm_out, z_row, gain):
    row_count = ssm_out.shape[0]
    gated_out = ssm_out * jax.nn.silu(z_row.astype(jnp.float32))
    grouped = gated_out.reshape(row_count, -1, NORM_GROUP)
    scaled = grouped * lax.rsqrt(jnp.mean(grouped * grouped, axis=-1, keepdims=True) + 1e-05)
    return (scaled.reshape(row_count, -1) * gain).astype(jnp.bfloat16)


def advance(carried, x_row, dt_row, b_part, a_rate, dt_bias):
    step_size = jax.nn.softplus(dt_row.astype(jnp.float32) + dt_bias)
    decay_rate = jnp.repeat(jnp.exp(-a_rate * step_size), HEAD, axis=1)
    drive_term = jnp.repeat(step_size, HEAD, axis=1) * x_row.astype(jnp.float32)
    return (
        decay_rate[:, None, :] * carried.astype(jnp.float32)
        + drive_term[:, None, :] * b_part.astype(jnp.float32)[:, :, None]
    )


def key_scores(queries, key_block):
    row_count = queries.shape[0]
    local_heads = key_block.shape[2] // HD
    query_view = queries.reshape(row_count, local_heads, -1, HD)
    key_view = key_block.reshape(row_count, key_block.shape[1], local_heads, HD)
    return jnp.einsum(
        "skgd,snkd->skgn", query_view, key_view, preferred_element_type=jnp.float32
    ) * HD ** (-0.5)


def weighted(weights, value_block):
    row_count = value_block.shape[0]
    local_heads = value_block.shape[2] // HD
    value_view = value_block.reshape(row_count, value_block.shape[1], local_heads, HD)
    return jnp.einsum(
        "skgn,snkd->skgd",
        weights.astype(jnp.bfloat16),
        value_view,
        preferred_element_type=jnp.float32,
    )


def attend_local(queries, key_block, value_block, live_mask, extra_keys, extra_values):
    row_count = queries.shape[0]
    cached = jnp.where(live_mask, key_scores(queries, key_block), MASKED)
    new_scores = key_scores(queries, extra_keys)
    row_max = jnp.maximum(jnp.max(cached, axis=-1), jnp.max(new_scores, axis=-1))[..., None]
    cache_weights = jnp.where(live_mask, jnp.exp(cached - row_max), 0.0)
    extra_weights = jnp.exp(new_scores - row_max)
    weight_sum = jnp.sum(cache_weights, axis=-1) + jnp.sum(extra_weights, axis=-1)
    mixture = weighted(cache_weights, value_block) + weighted(extra_weights, extra_values)
    return (mixture / weight_sum[..., None]).reshape(row_count, -1).astype(jnp.bfloat16)


def spread(carried, key_block, value_block):
    return (
        lax.all_to_all(carried, "replica", split_axis=1, concat_axis=0, tiled=True),
        lax.all_to_all(key_block, "replica", split_axis=1, concat_axis=0, tiled=True),
        lax.all_to_all(value_block, "replica", split_axis=1, concat_axis=0, tiled=True),
    )


def per_device(
    ssm_state,
    kcache,
    vcache,
    lengths,
    parents,
    x_in,
    z_in,
    dt_in,
    b_in,
    c_in,
    q_in,
    kv_new,
    a_rate,
    dt_bias,
    skip,
    gain,
    out_proj,
):
    slot_count = ssm_state.shape[0]
    replica_id = lax.axis_index("replica")
    first_slot = replica_id * slot_count
    own_first = lax.dynamic_slice_in_dim(parents[0], first_slot, slot_count)
    own_second = lax.dynamic_slice_in_dim(parents[1], first_slot, slot_count)
    skip_wide = jnp.repeat(skip, HEAD)
    projected = []
    attended = []
    carried, key_block, value_block = (ssm_state, kcache, vcache)
    earlier = lax.all_gather(kv_new[0], "replica", axis=0, tiled=True)
    positions = jnp.arange(kcache.shape[1], dtype=jnp.int32)
    roots = (own_first, parents[0][own_second])
    for step_id in range(2):
        rows_state, rows_keys, rows_values = spread(carried, key_block, value_block)
        parent_ids = parents[step_id]
        carried, key_block, value_block = (
            lax.all_to_all(
                rows_state[parent_ids], "replica", split_axis=0, concat_axis=1, tiled=True
            ),
            lax.all_to_all(
                rows_keys[parent_ids], "replica", split_axis=0, concat_axis=1, tiled=True
            ),
            lax.all_to_all(
                rows_values[parent_ids], "replica", split_axis=0, concat_axis=1, tiled=True
            ),
        )
        updated = advance(carried, x_in[step_id], dt_in[step_id], b_in[step_id], a_rate, dt_bias)
        ssm_out = jnp.sum(
            updated * c_in[step_id].astype(jnp.float32)[:, :, None], axis=1
        ) + skip_wide * x_in[step_id].astype(jnp.float32)
        carried = updated.astype(jnp.bfloat16)
        projected.append(
            jnp.dot(
                gated_norm(ssm_out, z_in[step_id], gain),
                out_proj,
                preferred_element_type=jnp.float32,
            )
        )
        cap_len = lengths[roots[step_id] // BEAM]
        live_mask = (positions[None, :] < cap_len[:, None])[:, None, None, :]
        if step_id == 0:
            extra_keys = kv_new[0][:, 0:1, :]
            extra_values = kv_new[0][:, 1:2, :]
        else:
            extra_keys = jnp.stack([earlier[own_second, 0], kv_new[1][:, 0]], axis=1)
            extra_values = jnp.stack([earlier[own_second, 1], kv_new[1][:, 1]], axis=1)
        attended.append(
            attend_local(q_in[step_id], key_block, value_block, live_mask, extra_keys, extra_values)
        )
    mamba_out = lax.psum_scatter(
        jnp.stack(projected).astype(jnp.bfloat16), "tensor", scatter_dimension=2, tiled=True
    )
    return (carried, mamba_out, jnp.stack(attended))


def solution(mesh):
    return jax.shard_map(
        per_device,
        mesh=mesh,
        in_specs=(
            P("replica", None, "tensor"),
            P("replica", None, "tensor"),
            P("replica", None, "tensor"),
            P(),
            P(),
            P(None, "replica", "tensor"),
            P(None, "replica", "tensor"),
            P(None, "replica", "tensor"),
            P(None, "replica", None),
            P(None, "replica", None),
            P(None, "replica", "tensor"),
            P(None, "replica", None, "tensor"),
            P("tensor"),
            P("tensor"),
            P("tensor"),
            P("tensor"),
            P("tensor", None),
        ),
        out_specs=(
            P("replica", None, "tensor"),
            P(None, "replica", "tensor"),
            P(None, "replica", "tensor"),
        ),
        check_vma=False,
    )
```

profile of v0, /device:TPU:56, one launch (start us, length us, event | category | flops | bytes accessed | tf_op | source)
XLA Modules:
  0.0 449.0 jit_solution(13502122596180195011)
XLA Ops:
  7.2 2.3 copy.81
  9.5 11.3 %all-to-all-start = ((bf16[4,128,512]{2,0,1:T(4,128)(2,1)}), bf16[4,128,512]{2,0,1:T(4,128)(2,1)S(1)}, u32[]{:S(2)}, u32[]{:S(2)}) async-start(bf16[4,128,512]{2,0,1:T(4,128)(2,1)} %copy.81), calls=%async_computation | async-start | bytes 1048576 | tf_op jit(solution)/shard_map/all_to_all | solution.py:69
  20.9 0.8 fusion.80
  21.7 16.8 %all-to-all-done = bf16[4,128,512]{2,0,1:T(4,128)(2,1)S(1)} async-done(((bf16[4,128,512]{2,0,1:T(4,128)(2,1)}), bf16[4,128,512]{2,0,1:T(4,128)(2,1)S(1)}, u32[]{:S(2)}, u32[]{:S(2)}) %all-to-all-start) | async-done | bytes 524320 | tf_op jit(solution)/shard_map/all_to_all | solution.py:69
  38.8 1.8 gather_fusion
  40.6 4.9 %all-to-all-start.1 = ((bf16[128,4,512]{2,1,0:T(4,128)(2,1)}), bf16[128,4,512]{2,1,0:T(4,128)(2,1)S(1)}, u32[]{:S(2)}, u32[]{:S(2)}) async-start(bf16[128,4,512]{2,1,0:T(4,128)(2,1)} %gather_fusion), calls=%async_computation.1 | async-start | bytes 1048576 | tf_op jit(solution)/shard_map/all_to_all | solution.py:110
  45.4 1.8 copy.92
  47.2 15.1 %all-to-all-done.1 = bf16[128,4,512]{2,1,0:T(4,128)(2,1)S(1)} async-done(((bf16[128,4,512]{2,1,0:T(4,128)(2,1)}), bf16[128,4,512]{2,1,0:T(4,128)(2,1)S(1)}, u32[]{:S(2)}, u32[]{:S(2)}) %all-to-all-start.1) | async-done | bytes 524320 | tf_op jit(solution)/shard_map/all_to_all | solution.py:110
  62.4 4.9 %all-to-all-start.4 = ((bf16[4,1024,128]{2,0,1:T(4,128)(2,1)}), bf16[4,1024,128]{2,0,1:T(4,128)(2,1)S(1)}, u32[]{:S(2)}, u32[]{:S(2)}) async-start(bf16[4,1024,128]{2,0,1:T(4,128)(2,1)} %copy.92), calls=%async_computation.4 | async-start | bytes 2097152 | tf_op jit(solution)/shard_map/all_to_all | solution.py:70
  68.5 1.2 fusion.22
  69.7 25.3 %all-to-all-done.4 = bf16[4,1024,128]{2,0,1:T(4,128)(2,1)S(1)} async-done(((bf16[4,1024,128]{2,0,1:T(4,128)(2,1)}), bf16[4,1024,128]{2,0,1:T(4,128)(2,1)S(1)}, u32[]{:S(2)}, u32[]{:S(2)}) %all-to-all-start.4) | async-done | bytes 1048608 | tf_op jit(solution)/shard_map/all_to_all | solution.py:70
  95.0 5.1 %all-to-all-start.2 = ((bf16[4,128,512]{2,0,1:T(4,128)(2,1)}), bf16[4,128,512]{2,0,1:T(4,128)(2,1)S(1)}, u32[]{:S(2)}, u32[]{:S(2)}) async-start(bf16[4,128,512]{2,0,1:T(4,128)(2,1)} %fusion.22), calls=%async_computation.2 | async-start | bytes 1048576 | tf_op jit(solution)/shard_map/all_to_all | solution.py:69
  100.1 1.8 copy.97
  101.9 15.2 %all-to-all-done.2 = bf16[4,128,512]{2,0,1:T(4,128)(2,1)S(1)} async-done(((bf16[4,128,512]{2,0,1:T(4,128)(2,1)}), bf16[4,128,512]{2,0,1:T(4,128)(2,1)S(1)}, u32[]{:S(2)}, u32[]{:S(2)}) %all-to-all-start.2) | async-done | bytes 524320 | tf_op jit(solution)/shard_map/all_to_all | solution.py:69
  117.2 4.9 %all-to-all-start.6 = ((bf16[4,1024,128]{2,0,1:T(4,128)(2,1)}), bf16[4,1024,128]{2,0,1:T(4,128)(2,1)S(1)}, u32[]{:S(2)}, u32[]{:S(2)}) async-start(bf16[4,1024,128]{2,0,1:T(4,128)(2,1)} %copy.97), calls=%async_computation.6 | async-start | bytes 2097152 | tf_op jit(solution)/shard_map/all_to_all | solution.py:71
  122.1 1.1 copy.85
  123.1 2.8 gather_fusion.1
  126.0 23.8 %all-to-all-done.6 = bf16[4,1024,128]{2,0,1:T(4,128)(2,1)S(1)} async-done(((bf16[4,1024,128]{2,0,1:T(4,128)(2,1)}), bf16[4,1024,128]{2,0,1:T(4,128)(2,1)S(1)}, u32[]{:S(2)}, u32[]{:S(2)}) %all-to-all-start.6) | async-done | bytes 1048608 | tf_op jit(solution)/shard_map/all_to_all | solution.py:71
  149.8 5.1 %all-to-all-start.3 = ((bf16[128,4,512]{2,1,0:T(4,128)(2,1)}), bf16[128,4,512]{2,1,0:T(4,128)(2,1)S(1)}, u32[]{:S(2)}, u32[]{:S(2)}) async-start(bf16[128,4,512]{2,1,0:T(4,128)(2,1)} %gather_fusion.1), calls=%async_computation.3 | async-start | bytes 1048576 | tf_op jit(solution)/shard_map/all_to_all | solution.py:110
  155.2 1.7 gather_fusion.3
  156.9 15.1 %all-to-all-done.3 = bf16[128,4,512]{2,1,0:T(4,128)(2,1)S(1)} async-done(((bf16[128,4,512]{2,1,0:T(4,128)(2,1)}), bf16[128,4,512]{2,1,0:T(4,128)(2,1)S(1)}, u32[]{:S(2)}, u32[]{:S(2)}) %all-to-all-start.3) | async-done | bytes 524320 | tf_op jit(solution)/shard_map/all_to_all | solution.py:110
  172.0 4.9 %all-to-all-start.5 = ((bf16[128,32,128]{2,1,0:T(8,128)(2,1)}), bf16[128,32,128]{2,1,0:T(8,128)(2,1)}, u32[]{:S(2)}, u32[]{:S(2)}) async-start(bf16[128,32,128]{2,1,0:T(8,128)(2,1)} %gather_fusion.3), calls=%async_computation.5 | async-start | bytes 2097152 | tf_op jit(solution)/shard_map/all_to_all | solution.py:113
  177.2 1.7 gather_fusion.4
  178.9 25.9 %all-to-all-done.5 = bf16[128,32,128]{2,1,0:T(8,128)(2,1)} async-done(((bf16[128,32,128]{2,1,0:T(8,128)(2,1)}), bf16[128,32,128]{2,1,0:T(8,128)(2,1)}, u32[]{:S(2)}, u32[]{:S(2)}) %all-to-all-start.5) | async-done | bytes 1048608 | tf_op jit(solution)/shard_map/all_to_all | solution.py:113
  204.8 5.1 %all-to-all-start.7 = ((bf16[128,32,128]{2,1,0:T(8,128)(2,1)}), bf16[128,32,128]{2,1,0:T(8,128)(2,1)S(1)}, u32[]{:S(2)}, u32[]{:S(2)}) async-start(bf16[128,32,128]{2,1,0:T(8,128)(2,1)} %gather_fusion.4), calls=%async_computation.7 | async-start | bytes 2097152 | tf_op jit(solution)/shard_map/all_to_all | solution.py:116
  209.9 1.3 copy.95
  211.2 1.8 copy.101
  213.0 24.9 %all-to-all-done.7 = bf16[128,32,128]{2,1,0:T(8,128)(2,1)S(1)} async-done(((bf16[128,32,128]{2,1,0:T(8,128)(2,1)}), bf16[128,32,128]{2,1,0:T(8,128)(2,1)S(1)}, u32[]{:S(2)}, u32[]{:S(2)}) %all-to-all-start.7) | async-done | bytes 1048608 | tf_op jit(solution)/shard_map/all_to_all | solution.py:116
  237.9 5.3 %all-to-all-start.8 = ((bf16[4,1024,128]{2,0,1:T(4,128)(2,1)}), bf16[4,1024,128]{2,0,1:T(4,128)(2,1)}, u32[]{:S(2)}, u32[]{:S(2)}) async-start(bf16[4,1024,128]{2,0,1:T(4,128)(2,1)} %copy.101), calls=%async_computation.8 | async-start | bytes 2097152 | tf_op jit(solution)/shard_map/all_to_all | solution.py:70
  244.0 1.2 gather_fusion.2
  245.3 1.1 gather_fusion.6
  247.2 0.7 mul.255
  248.1 1.3 copy.100
  249.4 1.8 copy.106
  251.2 20.0 %all-to-all-done.8 = bf16[4,1024,128]{2,0,1:T(4,128)(2,1)} async-done(((bf16[4,1024,128]{2,0,1:T(4,128)(2,1)}), bf16[4,1024,128]{2,0,1:T(4,128)(2,1)}, u32[]{:S(2)}, u32[]{:S(2)}) %all-to-all-start.8) | async-done | bytes 1048608 | tf_op jit(solution)/shard_map/all_to_all | solution.py:70
  271.2 5.2 %all-to-all-start.10 = ((bf16[4,1024,128]{2,0,1:T(4,128)(2,1)}), bf16[4,1024,128]{2,0,1:T(4,128)(2,1)}, u32[]{:S(2)}, u32[]{:S(2)}) async-start(bf16[4,1024,128]{2,0,1:T(4,128)(2,1)} %copy.106), calls=%async_computation.10 | async-start | bytes 2097152 | tf_op jit(solution)/shard_map/all_to_all | solution.py:71
  277.5 64.9 %all-gather = bf16[1,128,2,128]{3,2,0,1:T(2,128)(2,1)S(1)} all-gather(bf16[1,4,2,128]{3,2,0,1:T(2,128)(2,1)S(1)} %get-tuple-element.32), channel_id=2, replica_groups=mesh['replica'=32,'tensor'=8] {'replica'}, dimensions={1}, use_global_device_ids=true | all-gather | bytes 67584 | tf_op jit(solution)/shard_map/all_gather | solution.py:103
  344.9 0.8 iota_compare_fusion.1
  345.7 0.7 iota_compare_fusion
  347.0 0.7 slice_bitcast_fusion.1
  347.7 1.4 fusion.46
  349.1 2.0 fusion.96
  351.0 1.4 copy.102
  352.4 1.1 copy.103
  353.6 3.0 gather_fusion.7
  356.6 8.0 %all-to-all-start.9 = ((bf16[128,32,128]{2,1,0:T(8,128)(2,1)}), bf16[128,32,128]{2,1,0:T(8,128)(2,1)}, u32[]{:S(2)}, u32[]{:S(2)}) async-start(bf16[128,32,128]{2,1,0:T(8,128)(2,1)} %gather_fusion.7), calls=%async_computation.9 | async-start | bytes 2097152 | tf_op jit(solution)/shard_map/all_to_all | solution.py:113
  365.9 1.4 copy.86
  367.9 0.9 multiply_reduce_fusion.1
  368.8 0.7 fusion.1
  369.5 0.7 fusion
  370.2 1.4 copy.107
  371.6 1.1 copy.108
  372.7 3.0 gather_fusion.9
  375.7 9.5 %all-to-all-done.9 = bf16[128,32,128]{2,1,0:T(8,128)(2,1)} async-done(((bf16[128,32,128]{2,1,0:T(8,128)(2,1)}), bf16[128,32,128]{2,1,0:T(8,128)(2,1)}, u32[]{:S(2)}, u32[]{:S(2)}) %all-to-all-start.9) | async-done | bytes 1048608 | tf_op jit(solution)/shard_map/all_to_all | solution.py:113
  385.2 6.9 %all-to-all-start.11 = ((bf16[128,32,128]{2,1,0:T(8,128)(2,1)}), bf16[128,32,128]{2,1,0:T(8,128)(2,1)}, u32[]{:S(2)}, u32[]{:S(2)}) async-start(bf16[128,32,128]{2,1,0:T(8,128)(2,1)} %gather_fusion.9), calls=%async_computation.11 | async-start | bytes 2097152 | tf_op jit(solution)/shard_map/all_to_all | solution.py:116
  392.2 1.6 fusion.20
  393.8 0.9 copy.111
  394.8 3.9 copy.114
  398.7 4.8 %reshape.751 = bf16[4096,8]{1,0:T(8,128)(2,1)} reshape(bf16[4096,2,4]{2,1,0:T(2,128)(2,1)} %bitcast.210) | data formatting | bytes 131072
  404.5 31.4 %reduce-scatter.4.cloned.1.call-done = bf16[512,8]{1,0:T(8,128)(2,1)} async-done(((bf16[4096,8]{1,0:T(8,128)(2,1)}), bf16[512,8]{1,0:T(8,128)(2,1)}) %reduce-scatter.4.cloned.1.call-update) | async-done | bytes 8208
  435.9 1.0 reshape.752
  436.9 0.8 copy.115
  437.7 1.3 copy.104
  439.7 1.3 copy.109
  (128 shorter events, 12.7 us)
Async XLA Ops:
  7.2 236.9 %copy-start = (s32[32]{0:T(128)S(1)}, s32[32]{0:T(128)}, u32[]{:S(2)}) copy-start(s32[32]{0:T(128)} %param.20) | copy-start | bytes 388
  7.2 38.3 %copy-start.3 = (bf16[4,1024,128]{2,1,0:T(8,128)(2,1)S(1)}, bf16[4,1024,128]{2,1,0:T(8,128)(2,1)}, u32[]{:S(2)}) copy-start(bf16[4,1024,128]{2,1,0:T(8,128)(2,1)} %param.18) | copy-start | bytes 3145732
  9.5 57.7 %copy-start.27 = (f32[8]{0:T(128)S(1)}, f32[8]{0:T(128)}, u32[]{:S(2)}) copy-start(f32[8]{0:T(128)} %param.29) | copy-start | bytes 100
  9.5 57.7 %copy-start.23 = (bf16[2,4,8]{2,1,0:T(4,128)(2,1)S(1)}, bf16[2,4,8]{2,1,0:T(4,128)(2,1)}, u32[]{:S(2)}) copy-start(bf16[2,4,8]{2,1,0:T(4,128)(2,1)} %param.24) | copy-start | bytes 388
  9.5 57.8 %copy-start.25 = (f32[8]{0:T(128)S(1)}, f32[8]{0:T(128)}, u32[]{:S(2)}) copy-start(f32[8]{0:T(128)} %param.30) | copy-start | bytes 100
  9.5 58.2 %copy-start.19 = (bf16[2,4,128]{2,1,0:T(4,128)(2,1)S(1)}, bf16[2,4,128]{2,1,0:T(4,128)(2,1)}, u32[]{:S(2)}) copy-start(bf16[2,4,128]{2,1,0:T(4,128)(2,1)} %param.25) | copy-start | bytes 6148
  9.5 58.4 %copy-start.10 = (bf16[2,4,512]{2,1,0:T(4,128)(2,1)S(1)}, bf16[2,4,512]{2,1,0:T(4,128)(2,1)}, u32[]{:S(2)}) copy-start(bf16[2,4,512]{2,1,0:T(4,128)(2,1)} %param.22) | copy-start | bytes 24580
  9.5 29.0 %all-to-all-start = ((bf16[4,128,512]{2,0,1:T(4,128)(2,1)}), bf16[4,128,512]{2,0,1:T(4,128)(2,1)S(1)}, u32[]{:S(2)}, u32[]{:S(2)}) async-start(bf16[4,128,512]{2,0,1:T(4,128)(2,1)} %copy.81), calls=%async_computation | async-start | bytes 1048576 | tf_op jit(solution)/shard_map/all_to_all | solution.py:69
  40.6 21.8 %all-to-all-start.1 = ((bf16[128,4,512]{2,1,0:T(4,128)(2,1)}), bf16[128,4,512]{2,1,0:T(4,128)(2,1)S(1)}, u32[]{:S(2)}, u32[]{:S(2)}) async-start(bf16[128,4,512]{2,1,0:T(4,128)(2,1)} %gather_fusion), calls=%async_computation.1 | async-start | bytes 1048576 | tf_op jit(solution)/shard_map/all_to_all | solution.py:110
  47.2 52.9 %copy-start.4 = (bf16[4,1024,128]{2,1,0:T(8,128)(2,1)S(1)}, bf16[4,1024,128]{2,1,0:T(8,128)(2,1)}, u32[]{:S(2)}) copy-start(bf16[4,1024,128]{2,1,0:T(8,128)(2,1)} %param.19) | copy-start | bytes 3145732
  62.4 32.6 %all-to-all-start.4 = ((bf16[4,1024,128]{2,0,1:T(4,128)(2,1)}), bf16[4,1024,128]{2,0,1:T(4,128)(2,1)S(1)}, u32[]{:S(2)}, u32[]{:S(2)}) async-start(bf16[4,1024,128]{2,0,1:T(4,128)(2,1)} %copy.92), calls=%async_computation.4 | async-start | bytes 2097152 | tf_op jit(solution)/shard_map/all_to_all | solution.py:70
  67.6 34.3 %copy-start.5 = (f32[4,512]{1,0:T(4,128)}, f32[4,512]{1,0:T(4,128)S(1)}, u32[]{:S(2)}) copy-start(f32[4,512]{1,0:T(4,128)S(1)} %mul.258) | copy-start | bytes 24580
  67.9 34.0 %copy-start.7 = (f32[4,512]{1,0:T(4,128)}, f32[4,512]{1,0:T(4,128)S(1)}, u32[]{:S(2)}) copy-start(f32[4,512]{1,0:T(4,128)S(1)} %get-tuple-element.27) | copy-start | bytes 24580
  95.0 22.2 %all-to-all-start.2 = ((bf16[4,128,512]{2,0,1:T(4,128)(2,1)}), bf16[4,128,512]{2,0,1:T(4,128)(2,1)S(1)}, u32[]{:S(2)}, u32[]{:S(2)}) async-start(bf16[4,128,512]{2,0,1:T(4,128)(2,1)} %fusion.22), calls=%async_computation.2 | async-start | bytes 1048576 | tf_op jit(solution)/shard_map/all_to_all | solution.py:69
  117.2 32.6 %all-to-all-start.6 = ((bf16[4,1024,128]{2,0,1:T(4,128)(2,1)}), bf16[4,1024,128]{2,0,1:T(4,128)(2,1)S(1)}, u32[]{:S(2)}, u32[]{:S(2)}) async-start(bf16[4,1024,128]{2,0,1:T(4,128)(2,1)} %copy.97), calls=%async_computation.6 | async-start | bytes 2097152 | tf_op jit(solution)/shard_map/all_to_all | solution.py:71
  122.1 34.9 %copy-start.15 = (s32[1024]{0:T(1024)}, s32[1024]{0:T(1024)S(1)}, u32[]{:S(2)}) copy-start(s32[1024]{0:T(1024)S(1)} %pad_clamp_fusion.3) | copy-start | bytes 12292
  149.8 22.2 %all-to-all-start.3 = ((bf16[128,4,512]{2,1,0:T(4,128)(2,1)}), bf16[128,4,512]{2,1,0:T(4,128)(2,1)S(1)}, u32[]{:S(2)}, u32[]{:S(2)}) async-start(bf16[128,4,512]{2,1,0:T(4,128)(2,1)} %gather_fusion.1), calls=%async_computation.3 | async-start | bytes 1048576 | tf_op jit(solution)/shard_map/all_to_all | solution.py:110
  172.0 32.7 %all-to-all-start.5 = ((bf16[128,32,128]{2,1,0:T(8,128)(2,1)}), bf16[128,32,128]{2,1,0:T(8,128)(2,1)}, u32[]{:S(2)}, u32[]{:S(2)}) async-start(bf16[128,32,128]{2,1,0:T(8,128)(2,1)} %gather_fusion.3), calls=%async_computation.5 | async-start | bytes 2097152 | tf_op jit(solution)/shard_map/all_to_all | solution.py:113
  178.9 64.3 %copy-start.18 = (s32[2,128]{1,0:T(2,128)S(1)}, s32[2,128]{1,0:T(2,128)}, u32[]{:S(2)}) copy-start(s32[2,128]{1,0:T(2,128)} %param.21) | copy-start | bytes 3076
  204.8 33.1 %all-to-all-start.7 = ((bf16[128,32,128]{2,1,0:T(8,128)(2,1)}), bf16[128,32,128]{2,1,0:T(8,128)(2,1)S(1)}, u32[]{:S(2)}, u32[]{:S(2)}) async-start(bf16[128,32,128]{2,1,0:T(8,128)(2,1)} %gather_fusion.4), calls=%async_computation.7 | async-start | bytes 2097152 | tf_op jit(solution)/shard_map/all_to_all | solution.py:116
  209.9 36.5 %copy-start.26 = (f32[8]{0:T(128)S(1)}, f32[8]{0:T(128)}, u32[]{:S(2)}) copy-start(f32[8]{0:T(128)} %param.31) | copy-start | bytes 100
  237.9 10.2 %copy-start.2 = (bf16[128,32,128]{2,1,0:T(8,128)(2,1)}, bf16[128,32,128]{2,1,0:T(8,128)(2,1)S(1)}, u32[]{:S(2)}) copy-start(bf16[128,32,128]{2,1,0:T(8,128)(2,1)S(1)} %all-to-all-done.7) | copy-start | bytes 3145732
  237.9 33.3 %all-to-all-start.8 = ((bf16[4,1024,128]{2,0,1:T(4,128)(2,1)}), bf16[4,1024,128]{2,0,1:T(4,128)(2,1)}, u32[]{:S(2)}, u32[]{:S(2)}) async-start(bf16[4,1024,128]{2,0,1:T(4,128)(2,1)} %copy.101), calls=%async_computation.8 | async-start | bytes 2097152 | tf_op jit(solution)/shard_map/all_to_all | solution.py:70
  243.2 33.3 %copy-start.20 = (bf16[2,4,128]{2,1,0:T(4,128)(2,1)S(1)}, bf16[2,4,128]{2,1,0:T(4,128)(2,1)}, u32[]{:S(2)}) copy-start(bf16[2,4,128]{2,1,0:T(4,128)(2,1)} %param.26) | copy-start | bytes 6148
  243.3 33.6 %copy-start.16 = (bf16[2,4,2,128]{3,2,1,0:T(2,128)(2,1)S(1)}, bf16[2,4,2,128]{3,2,1,0:T(2,128)(2,1)}, u32[]{:S(2)}) copy-start(bf16[2,4,2,128]{3,2,1,0:T(2,128)(2,1)} %param.28) | copy-start | bytes 12292
  271.2 85.4 %all-to-all-start.10 = ((bf16[4,1024,128]{2,0,1:T(4,128)(2,1)}), bf16[4,1024,128]{2,0,1:T(4,128)(2,1)}, u32[]{:S(2)}, u32[]{:S(2)}) async-start(bf16[4,1024,128]{2,0,1:T(4,128)(2,1)} %copy.106), calls=%async_computation.10 | async-start | bytes 2097152 | tf_op jit(solution)/shard_map/all_to_all | solution.py:71
  351.0 13.6 %copy-start.14 = (bf16[4,2,128]{2,1,0:T(2,128)(2,1)S(1)}, bf16[4,2,128]{2,1,0:T(2,128)(2,1)}, u32[]{:S(2)}) copy-start(bf16[4,2,128]{2,1,0:T(2,128)(2,1)} %get-tuple-element.30) | copy-start | bytes 6148
  351.0 14.2 %copy-start.6 = (f32[4,512]{1,0:T(4,128)S(1)}, f32[4,512]{1,0:T(4,128)}, u32[]{:S(2)}) copy-start(f32[4,512]{1,0:T(4,128)} %copy-done.5) | copy-start | bytes 24580
  351.0 14.2 %copy-start.8 = (f32[4,512]{1,0:T(4,128)S(1)}, f32[4,512]{1,0:T(4,128)}, u32[]{:S(2)}) copy-start(f32[4,512]{1,0:T(4,128)} %copy-done.7) | copy-start | bytes 24580
  353.6 13.8 %copy-start.9 = (f32[4,512]{1,0:T(4,128)S(1)}, f32[4,512]{1,0:T(4,128)}, u32[]{:S(2)}) copy-start(f32[4,512]{1,0:T(4,128)} %mul.255) | copy-start | bytes 24580
  353.6 15.2 %copy-start.11 = (f32[512]{0:T(512)S(1)}, f32[512]{0:T(512)}, u32[]{:S(2)}) copy-start(f32[512]{0:T(512)} %param.32) | copy-start | bytes 6148
  356.6 28.6 %all-to-all-start.9 = ((bf16[128,32,128]{2,1,0:T(8,128)(2,1)}), bf16[128,32,128]{2,1,0:T(8,128)(2,1)}, u32[]{:S(2)}, u32[]{:S(2)}) async-start(bf16[128,32,128]{2,1,0:T(8,128)(2,1)} %gather_fusion.7), calls=%async_computation.9 | async-start | bytes 2097152 | tf_op jit(solution)/shard_map/all_to_all | solution.py:113
  364.6 4.2 copy-start.1
  385.2 54.4 %all-to-all-start.11 = ((bf16[128,32,128]{2,1,0:T(8,128)(2,1)}), bf16[128,32,128]{2,1,0:T(8,128)(2,1)}, u32[]{:S(2)}, u32[]{:S(2)}) async-start(bf16[128,32,128]{2,1,0:T(8,128)(2,1)} %gather_fusion.9), calls=%async_computation.11 | async-start | bytes 2097152 | tf_op jit(solution)/shard_map/all_to_all | solution.py:116
  392.2 43.7 %reduce-scatter.4.cloned.1.call-start = ((), (), s32[]{:S(2)}) async-start(), calls=%async_computation.13 | async-start | bytes 1179648
  393.8 10.1 %copy-start.13 = (f32[4,1,8]{2,1,0:T(1,128)S(1)}, f32[4,1,8]{2,1,0:T(1,128)}, u32[]{:S(2)}) copy-start(f32[4,1,8]{2,1,0:T(1,128)} %fusion.46) | copy-start | bytes 388
  393.8 10.3 %copy-start.12 = (f32[4,1,128]{2,1,0:T(1,128)S(1)}, f32[4,1,128]{2,1,0:T(1,128)}, u32[]{:S(2)}) copy-start(f32[4,1,128]{2,1,0:T(1,128)} %slice_convert_fusion) | copy-start | bytes 6148
  403.5 36.0 %copy-start.21 = (f32[4,8]{1,0:T(4,128)S(1)}, f32[4,8]{1,0:T(4,128)}, u32[]{:S(2)}) copy-start(f32[4,8]{1,0:T(4,128)} %get-tuple-element.50) | copy-start | bytes 388
  403.5 36.0 %copy-start.17 = (f32[4,8,2]{1,2,0:T(2,128)S(1)}, f32[4,8,2]{1,2,0:T(2,128)}, u32[]{:S(2)}) copy-start(f32[4,8,2]{1,2,0:T(2,128)} %get-tuple-element.51) | copy-start | bytes 772
  404.2 37.2 %copy-start.22 = (bf16[4,1,128]{2,1,0:T(2,128)(2,1)S(1)}, bf16[4,1,128]{2,1,0:T(2,128)(2,1)}, u32[]{:S(2)}) copy-start(bf16[4,1,128]{2,1,0:T(2,128)(2,1)} %copy.110) | copy-start | bytes 3076
  404.2 37.2 %copy-start.24 = (bf16[4,1,128]{2,1,0:T(2,128)(2,1)S(1)}, bf16[4,1,128]{2,1,0:T(2,128)(2,1)}, u32[]{:S(2)}) copy-start(bf16[4,1,128]{2,1,0:T(2,128)(2,1)} %get-tuple-element.35) | copy-start | bytes 3076
Sparse Core Ops, SparseCore 0:
  403.6 32.2 reduce-scatter.3
where the time goes:
time: 455 us; the launch traced here: 449 us
  waiting for transfers between devices  223 us (49%)
  starting transfers between devices  71.6 us (16%)
  blocking collectives  64.9 us (14%)
  local copies, waits for them, and re-layouts  59.1 us (13%)
  between operations  14.7 us (3%)
  other arithmetic  9.18 us (2%)
  matrix products  6.42 us (1%)
    all_gather x1, blocking collectives, per_device(): earlier = lax.all_gather(kv_new[0], 'replica', axis=0, tiled=True)  64.9 us
    all_to_all x2, waiting for transfers between devices, spread(): lax.all_to_all(key_block, 'replica', split_axis=1, concat_axis=0, tiled=T...  45.3 us
    all_to_all x2, waiting for transfers between devices, per_device(): lax.all_to_all(rows_keys[parent_ids], 'replica', split_axis=0, concat_axi...  35.4 us
    all_to_all x2, waiting for transfers between devices, spread(): lax.all_to_all(carried, 'replica', split_axis=1, concat_axis=0, tiled=True)  32.1 us
    unnamed x2, waiting for transfers between devices  31.4 us
    all_to_all x2, waiting for transfers between devices, per_device(): lax.all_to_all(rows_state[parent_ids], 'replica', split_axis=0, concat_ax...  30.2 us
    all_to_all x2, waiting for transfers between devices, per_device(): lax.all_to_all(rows_values[parent_ids], 'replica', split_axis=0, concat_a...  24.9 us
    all_to_all x2, waiting for transfers between devices, spread(): lax.all_to_all(value_block, 'replica', split_axis=1, concat_axis=0, tiled...  23.9 us
  transfers between devices with their start and end apart: 13, of which 11 were waited for; matrix products, arithmetic and copies ran while one was open for 15% of the time, Pallas kernels for 0%

commit v1 on v0

v1 whole, which is shorter than its diff:
```python
import functools

import jax
import jax.numpy as jnp
from jax import lax
from jax.experimental import pallas as pl
from jax.experimental.pallas import tpu as pltpu
from jax.sharding import PartitionSpec as P

F32 = jnp.float32
BF16 = jnp.bfloat16
HD = 128
STEP_LANES = 1408
CARRY_LANES = 384
ITEM_LANES = STEP_LANES + CARRY_LANES
BACK_LANES = 1536
MASKED = -1e30
VMEM_LIMIT = 40 * 1024 * 1024

SMEM = pl.BlockSpec(memory_space=pltpu.SMEM)
VMEM = pl.BlockSpec(memory_space=pltpu.VMEM)


def call(body, name, out_shape, in_specs, out_specs, scratch=(), cost=(1000000, 1000000)):
    return pl.pallas_call(
        body,
        name=name,
        out_shape=out_shape,
        in_specs=in_specs,
        out_specs=out_specs,
        scratch_shapes=list(scratch),
        compiler_params=pltpu.CompilerParams(vmem_limit_bytes=VMEM_LIMIT),
        cost_estimate=pl.CostEstimate(flops=cost[0], bytes_accessed=cost[1], transcendentals=0),
    )


def source_of(parents, step, prompt):
    return parents[step, prompt * 4] >> 2


def root_of(parents, prompt):
    return source_of(parents, 0, source_of(parents, 1, prompt))


def pack_body(parents, q, kv, c, x, b, dt, item, inverse, wide):
    def fill(prompt, _):
        inverse[0, source_of(parents, 0, prompt)] = prompt
        inverse[1, root_of(parents, prompt)] = prompt
        return 0

    lax.fori_loop(0, 32, fill, 0)
    wide[:, STEP_LANES:] = jnp.zeros((8, CARRY_LANES), F32)
    for t in range(2):
        rows = pl.ds(4 * t, 4)
        wide[rows, 0:1024] = q[t].astype(F32)
        for s in range(4):
            pair = kv[t, s].astype(F32)
            wide[pl.ds(4 * t + s, 1), 1024:1152] = pair[0:1]
            wide[pl.ds(4 * t + s, 1), 1152:1280] = pair[1:2]
        wide[rows, 1280:1408] = c[t].astype(F32)
    x0 = x[0].astype(F32)
    wide[pl.ds(0, 4), 1408:1792] = x0[:, 0:384]
    wide[pl.ds(4, 4), 1408:1536] = x0[:, 384:512]
    wide[pl.ds(4, 4), 1536:1664] = b[0].astype(F32)
    wide[pl.ds(4, 4), 1664:1672] = dt[0].astype(F32)
    item[...] = wide[...].astype(BF16)


def first_rows(shape):
    return lax.broadcasted_iota(jnp.int32, shape, 0) < 4


def sort_out_body(parents, inverse, *refs):
    rows, outs, held = refs[:4], refs[4:12], refs[12]
    me = lax.axis_index("replica")
    for k in range(4):
        held[k] = rows[k][...]
    first = first_rows((8, STEP_LANES))
    for k in range(8):
        dest = (me & 24) | ((me + k) & 7)
        pick = lambda source: ((me >> 3) - (source >> 3)) & 3
        for_child = held[pick(inverse[0, dest])].astype(F32)
        for_second = held[pick(inverse[1, dest])].astype(F32)
        carry = held[pick(source_of(parents, 1, dest))]
        outs[k][:, 0:STEP_LANES] = jnp.where(
            first, for_child[:, 0:STEP_LANES], for_second[:, 0:STEP_LANES]
        ).astype(BF16)
        outs[k][:, STEP_LANES:] = carry[:, STEP_LANES:]


def sort_back_body(parents, *refs):
    rows, outs, held = refs[:4], refs[4:12], refs[12]
    me = lax.axis_index("replica")
    for k in range(4):
        held[k] = rows[k][...]
    first = first_rows((8, BACK_LANES))
    for k in range(8):
        dest = (me & 24) | ((me + k) & 7)
        pick = lambda source: ((me >> 3) - (source >> 3)) & 3
        one = held[pick(source_of(parents, 0, dest))].astype(F32)
        two = held[pick(root_of(parents, dest))].astype(F32)
        outs[k][...] = jnp.where(first, one, two).astype(BF16)


def by_row(values, shape):
    row = lax.broadcasted_iota(jnp.int32, shape, 0)
    out = jnp.full(shape, values[-1], jnp.int32)
    for i in range(len(values) - 1):
        out = jnp.where(row == i, values[i], out)
    return out


def nt_dot(a, b):
    return lax.dot_general(a, b, (((1,), (1,)), ((), ())), preferred_element_type=F32)


def attend_body(parents, inverse, lengths, *refs):
    blocks = refs[:8]
    keys, values, state = refs[8:11]
    back, carry = refs[11:13]
    held = refs[13]
    me = lax.axis_index("replica")
    child = inverse[0, me]
    second = inverse[1, me]
    for k in range(8):
        held[k] = blocks[k][...]
    one = held[(me - child) & 7].astype(F32)
    two = held[(me - second) & 7].astype(F32)
    carry[...] = held[(me - source_of(parents, 1, me)) & 7][:, STEP_LANES:]
    item = jnp.where(
        first_rows((8, STEP_LANES)), one[:, 0:STEP_LANES], two[:, 0:STEP_LANES]
    )
    query = jnp.concatenate([item[:, h * HD : (h + 1) * HD] for h in range(8)], axis=0).astype(BF16)
    pads = jnp.zeros((120, HD), F32)
    new_keys = jnp.concatenate([item[:, 1024:1152], pads], axis=0).astype(BF16)
    new_values = jnp.concatenate([item[:, 1152:1280], pads], axis=0).astype(BF16)
    c_rows = item[:, 1280:1408].astype(BF16)
    ways = [parents[1, second * 4 + s] & 3 for s in range(4)]
    roots = [parents[0, child * 4 + s] & 3 for s in range(4)]
    roots += [parents[0, child * 4 + ways[s]] & 3 for s in range(4)]
    scale = HD ** (-0.5)

    root_rows = by_row(roots, (8, 1024))
    live = lax.broadcasted_iota(jnp.int32, (8, 1024), 1) < lengths[me]
    scores = jnp.zeros((8, 8, 1024), F32)
    for r in range(4):
        part = nt_dot(query, keys[r]).reshape(8, 8, 1024)
        scores = jnp.where((root_rows == r)[None], part, scores)
    scores = jnp.where(live[None], scores * scale, MASKED)

    row = lax.broadcasted_iota(jnp.int32, (8, HD), 0)
    column = lax.broadcasted_iota(jnp.int32, (8, HD), 1)
    way_rows = by_row([0, 1, 2, 3] + ways, (8, HD))
    seen = (column == row) | (column == way_rows)
    new_scores = nt_dot(query, new_keys).reshape(8, 8, HD) * scale
    new_scores = jnp.where(seen[None], new_scores, MASKED)

    top = jnp.maximum(
        jnp.max(scores, axis=-1, keepdims=True), jnp.max(new_scores, axis=-1, keepdims=True)
    )
    weights = jnp.exp(scores - top)
    new_weights = jnp.exp(new_scores - top)
    total = jnp.sum(weights, axis=-1, keepdims=True) + jnp.sum(new_weights, axis=-1, keepdims=True)
    mixed = jnp.dot(
        new_weights.reshape(64, HD).astype(BF16), new_values, preferred_element_type=F32
    )
    for r in range(4):
        mine = jnp.where((root_rows == r)[None], weights, 0.0).reshape(64, 1024).astype(BF16)
        mixed = mixed + jnp.dot(mine, values[r], preferred_element_type=F32)
    mixed = mixed / total.reshape(64, 1)
    for h in range(8):
        back[:, h * HD : (h + 1) * HD] = mixed[h * 8 : (h + 1) * 8].astype(BF16)

    root_wide = by_row(roots, (8, 512))
    read = jnp.zeros((8, 512), F32)
    for r in range(4):
        part = jnp.dot(c_rows, state[r], preferred_element_type=F32)
        read = jnp.where(root_wide == r, part, read)
    back[:, 1024:1536] = read.astype(BF16)


def per_head(ref, rows=8):
    head = lax.broadcasted_iota(jnp.int32, (rows, 512), 1) >> 6
    out = jnp.full((rows, 512), ref[7], F32)
    for h in range(7):
        out = jnp.where(head == h, ref[h], out)
    return out


def spread_heads(dt):
    head = lax.broadcasted_iota(jnp.int32, (HD, 512), 0)
    lane = lax.broadcasted_iota(jnp.int32, (HD, 512), 1) >> 6
    expand = (head == lane).astype(F32).astype(BF16)
    return jnp.dot(dt.astype(BF16), expand, preferred_element_type=F32)


def step_terms(dt, x, rate, bias):
    raw = spread_heads(dt) + bias
    step = jnp.maximum(raw, 0.0) + jnp.log1p(jnp.exp(-jnp.abs(raw)))
    return jnp.exp(-rate * step), step * x


def parent_rows(parents, me, carry, wide):
    folded = carry[...].astype(F32)
    wide[pl.ds(8, 4), 0:384] = folded[0:4]
    wide[pl.ds(8, 4), 384:768] = folded[4:8]
    wide[pl.ds(0, 4), :] = jnp.zeros((4, 768), F32)
    for s in range(4):
        way = parents[1, me * 4 + s] & 3
        wide[pl.ds(4 + s, 1), :] = wide[pl.ds(8 + way, 1), :]
    return wide[pl.ds(0, 8), :]


def stacked(ref, wide, lanes):
    wide[pl.ds(0, 4), 0:lanes] = ref[0].astype(F32)
    wide[pl.ds(4, 4), 0:lanes] = ref[1].astype(F32)
    return wide[pl.ds(0, 8), 0:lanes]


def mamba_body(parents, a_rate, dt_bias, skip, *refs):
    blocks = refs[:8]
    carry, x_in, z_in, dt_in, b_in, c_in, gain, proj = refs[8:16]
    attn, keep, send = refs[16:19]
    held, wide = refs[19:21]
    me = lax.axis_index("replica")
    core = lax.axis_index("tensor") & 1
    for k in range(8):
        held[k] = blocks[k][...]
    one = held[(me - source_of(parents, 0, me)) & 7].astype(F32)
    two = held[(me - root_of(parents, me)) & 7].astype(F32)
    attn[0] = one[0:4, 0:1024].astype(BF16)
    attn[1] = two[4:8, 0:1024].astype(BF16)
    first = first_rows((8, 512))
    read = jnp.where(first, one[:, 1024:1536], two[:, 1024:1536])

    rate = per_head(a_rate)
    bias = per_head(dt_bias)
    earlier = parent_rows(parents, me, carry, wide)
    decay_p, drive_p = step_terms(earlier[:, 640:768], earlier[:, 0:512], rate, bias)
    b_p = earlier[:, 512:640]
    wide[pl.ds(0, 8), 0:HD] = jnp.zeros((8, HD), F32)
    stacked(dt_in, wide, 8)
    dt = wide[pl.ds(0, 8), 0:HD]
    x = stacked(x_in, wide, 512)
    z = stacked(z_in, wide, 512)
    b = stacked(b_in, wide, HD)
    c = stacked(c_in, wide, HD)
    decay, drive = step_terms(dt, x, rate, bias)
    inner = decay_p * read + drive_p * jnp.sum(b_p * c, axis=-1, keepdims=True)
    inner = jnp.where(first, read, inner)
    out = decay * inner + drive * jnp.sum(b * c, axis=-1, keepdims=True) + per_head(skip) * x
    gated = out * (z / (1.0 + jnp.exp(-z)))
    mean = jnp.mean(gated * gated, axis=-1, keepdims=True)
    normed = (gated * lax.rsqrt(mean + 1e-05) * gain[...]).astype(BF16)
    for y in range(4):
        own = pl.multiple_of((2 * y + core) * 512, 512)
        other = pl.multiple_of((2 * y + 1 - core) * 512, 512)
        send[y] = jnp.dot(normed, proj[:, pl.ds(other, 512)], preferred_element_type=F32).astype(BF16)
        keep[y] = jnp.dot(normed, proj[:, pl.ds(own, 512)], preferred_element_type=F32).astype(BF16)


def core_sum_body(keep, came, *refs):
    outs, total = refs[:4], refs[4]
    y = lax.axis_index("tensor") >> 1
    total[...] = keep[...].astype(F32) + came[...].astype(F32)
    for k in range(4):
        outs[k][...] = total[(y + k) & 3].astype(BF16)


def last_sum_body(a, b, c, d, out):
    total = (a[...].astype(F32) + b[...].astype(F32)) + (c[...].astype(F32) + d[...].astype(F32))
    out[0] = total[0:4].astype(BF16)
    out[1] = total[4:8].astype(BF16)


def regroup_body(parents, came, out):
    for prompt in range(32):
        out[prompt] = came[root_of(parents, prompt)]


def advance_body(parents, a_rate, dt_bias, state, carry, x_in, dt_in, b_in, out, wide):
    me = lax.axis_index("replica")
    rate = per_head(a_rate)
    bias = per_head(dt_bias)
    earlier = parent_rows(parents, me, carry, wide)
    decay_p, drive_p = step_terms(earlier[:, 640:768], earlier[:, 0:512], rate, bias)
    b_p = earlier[:, 512:640]
    wide[pl.ds(0, 8), 0:HD] = jnp.zeros((8, HD), F32)
    stacked(dt_in, wide, 8)
    dt = wide[pl.ds(0, 8), 0:HD]
    x = stacked(x_in, wide, 512)
    b = stacked(b_in, wide, HD)
    decay, drive = step_terms(dt, x, rate, bias)
    columns_p = jnp.transpose(b_p)
    columns = jnp.transpose(b)
    source = source_of(parents, 1, me)
    for s in range(4):
        root = parents[0, source * 4 + (parents[1, me * 4 + s] & 3)] & 3
        r = 4 + s
        for i in range(8):
            rows = slice(i * 16, (i + 1) * 16)
            old = state[root * 8 + i].astype(F32)
            mid = decay_p[r : r + 1] * old + drive_p[r : r + 1] * columns_p[rows, r : r + 1]
            mid = mid.astype(BF16).astype(F32)
            new = decay[r : r + 1] * mid + drive[r : r + 1] * columns[rows, r : r + 1]
            out[s * 8 + i] = new.astype(BF16)


def along_x(array, k):
    return lax.ppermute(array, "replica", [(r, ((r + 8 * k) & 31)) for r in range(32)])


def along_z(array, k):
    return lax.ppermute(array, "replica", [(r, (r & 24) | ((r + k) & 7)) for r in range(32)])


def along_y(array, k):
    return lax.ppermute(array, "tensor", [(t, (t + 2 * k) & 7) for t in range(8)])


def across(array):
    return lax.ppermute(array, "tensor", [(t, t ^ 1) for t in range(8)])


def struct(shape, dtype=BF16):
    return jax.ShapeDtypeStruct(shape, dtype)


def per_device(
    ssm_state,
    kcache,
    vcache,
    lengths,
    parents,
    x_in,
    z_in,
    dt_in,
    b_in,
    c_in,
    q_in,
    kv_new,
    a_rate,
    dt_bias,
    skip,
    gain,
    out_proj,
):
    came = lax.all_to_all(ssm_state.reshape(32, 16, 512), "replica", 0, 0, tiled=True)

    item, inverse = call(
        pack_body,
        "pack",
        (struct((8, ITEM_LANES)), struct((2, 32), jnp.int32)),
        [SMEM] + [VMEM] * 6,
        (VMEM, SMEM),
        [pltpu.VMEM((8, ITEM_LANES), F32)],
    )(parents, q_in, kv_new, c_in, x_in, b_in, dt_in)
    rows = [item] + [along_x(item, k) for k in range(1, 4)]
    blocks = call(
        sort_out_body,
        "sort_out",
        (struct((8, ITEM_LANES)),) * 8,
        [SMEM, SMEM] + [VMEM] * 4,
        (VMEM,) * 8,
        [pltpu.VMEM((4, 8, ITEM_LANES), BF16)],
    )(parents, inverse, *rows)
    blocks = [blocks[0]] + [along_z(blocks[k], k) for k in range(1, 8)]
    back, carry = call(
        attend_body,
        "attend",
        (struct((8, BACK_LANES)), struct((8, CARRY_LANES))),
        [SMEM] * 3 + [VMEM] * 11,
        (VMEM, VMEM),
        [pltpu.VMEM((8, 8, ITEM_LANES), BF16)],
        (140000000, 3000000),
    )(parents, inverse, lengths, *blocks, kcache, vcache, ssm_state)
    rows = [back] + [along_x(back, k) for k in range(1, 4)]
    blocks = call(
        sort_back_body,
        "sort_back",
        (struct((8, BACK_LANES)),) * 8,
        [SMEM] + [VMEM] * 4,
        (VMEM,) * 8,
        [pltpu.VMEM((4, 8, BACK_LANES), BF16)],
    )(parents, *rows)
    blocks = [blocks[0]] + [along_z(blocks[k], k) for k in range(1, 8)]
    attn_out, keep, send = call(
        mamba_body,
        "mamba",
        (struct((2, 4, 1024)), struct((4, 8, 512)), struct((4, 8, 512))),
        [SMEM] * 4 + [VMEM] * 16,
        (VMEM,) * 3,
        [pltpu.VMEM((8, 8, BACK_LANES), BF16), pltpu.VMEM((16, 768), F32)],
        (40000000, 5000000),
    )(
        parents, a_rate, dt_bias, skip, *blocks, carry, x_in, z_in, dt_in, b_in, c_in,
        gain.reshape(1, 512), out_proj,
    )
    parts = call(
        core_sum_body,
        "core_sum",
        (struct((8, 512)),) * 4,
        [VMEM, VMEM],
        (VMEM,) * 4,
        [pltpu.VMEM((4, 8, 512), F32)],
    )(keep, across(send))
    mamba_out = call(last_sum_body, "last_sum", struct((2, 4, 512)), [VMEM] * 4, VMEM)(
        parts[0], *[along_y(parts[k], k) for k in range(1, 4)]
    )

    regrouped = call(
        regroup_body, "regroup", struct((32, 16, 512)), [SMEM, VMEM], VMEM
    )(parents, came)
    arrived = lax.all_to_all(regrouped, "replica", 0, 0, tiled=True)
    final_state = call(
        advance_body,
        "advance",
        struct((32, 16, 512)),
        [SMEM] * 3 + [VMEM] * 5,
        VMEM,
        [pltpu.VMEM((16, 768), F32)],
        (4000000, 1000000),
    )(parents, a_rate, dt_bias, arrived, carry, x_in, dt_in, b_in)
    return (final_state.reshape(4, 128, 512), mamba_out, attn_out)


def solution(mesh):
    return jax.shard_map(
        per_device,
        mesh=mesh,
        in_specs=(
            P("replica", None, "tensor"),
            P("replica", None, "tensor"),
            P("replica", None, "tensor"),
            P(),
            P(),
            P(None, "replica", "tensor"),
            P(None, "replica", "tensor"),
            P(None, "replica", "tensor"),
            P(None, "replica", None),
            P(None, "replica", None),
            P(None, "replica", "tensor"),
            P(None, "replica", None, "tensor"),
            P("tensor"),
            P("tensor"),
            P("tensor"),
            P("tensor"),
            P("tensor", None),
        ),
        out_specs=(
            P("replica", None, "tensor"),
            P(None, "replica", "tensor"),
            P(None, "replica", "tensor"),
        ),
        check_vma=False,
    )
```

time: 455 us -> 119 us (0.26)
  waiting for transfers between devices: 223 us -> 18.5 us
  local copies, waits for them, and re-layouts: 59.1 us -> 11.9 us
  blocking collectives: 64.9 us -> 28.9 us
  starting transfers between devices: 71.6 us -> 45.9 us
  between operations: 14.7 us -> 0.84 us
  Pallas kernels: 0 us -> 10.5 us
  other arithmetic: 9.18 us -> 0 us
  matrix products: 6.42 us -> 0 us
    all_to_all x12 -> x1, waiting for transfers between devices: 192 us -> 0.01 us  [per_device(): arrived = lax.all_to_all(regrouped, 'replica', 0, 0, tiled=True)]
    all_to_all x12 -> x1, starting transfers between devices: 71.6 us -> 4.99 us  [per_device(): arrived = lax.all_to_all(regrouped, 'replica', 0, 0, tiled=True)]
    all_gather x1 -> x0, blocking collectives: 64.9 us -> none  [per_device(): earlier = lax.all_gather(kv_new[0], 'replica', axis=0, tiled=True)]
    ppermute x0 -> x24, starting transfers between devices: none -> 40.9 us  [the longest x14 30.6 us: along_z(): lax.ppermute(array, 'replica', [(r, r & 24 | r + k & 7) for r in range(32)])]
    unnamed x2 -> x0, waiting for transfers between devices: 31.4 us -> none
    all_to_all x0 -> x1, blocking collectives: none -> 28.9 us  [per_device(): lax.all_to_all(ssm_state.reshape(32, 16, 512), 'replica', 0, 0, tiled=True)]
    ppermute x0 -> x24, waiting for transfers between devices: none -> 18.5 us  [the longest x6 8.03 us: along_x(): lax.ppermute(array, 'replica', [(r, r + 8 * k & 31) for r in range(32)])]
    gather x11 -> x0, local copies, waits for them, and re-layouts: 18.3 us -> none  [the longest x2 4.73 us: per_device(): rows_keys[parent_ids]]
  transfers between devices with their start and end apart: 13 -> 25, of which waited for: 11 -> 15; matrix products, arithmetic and copies ran while one was open for 15% -> 0% of each run, Pallas kernels for 0% -> 6%
where the time goes in v1:
time: 119 us; the launch traced here: 117 us
  starting transfers between devices  45.9 us (39%)
  blocking collectives  28.9 us (24%)
  waiting for transfers between devices  18.5 us (16%)
  local copies, waits for them, and re-layouts  11.9 us (10%)
  Pallas kernels  10.5 us (9%)
    ppermute x14, starting transfers between devices, along_z(): lax.ppermute(array, 'replica', [(r, r & 24 | r + k & 7) for r in range(32)])  30.6 us
    all_to_all x1, blocking collectives, per_device(): lax.all_to_all(ssm_state.reshape(32, 16, 512), 'replica', 0, 0, tiled=True)  28.9 us
    unnamed x46, local copies, waits for them, and re-layouts  11.9 us
    ppermute x6, waiting for transfers between devices, along_x(): lax.ppermute(array, 'replica', [(r, r + 8 * k & 31) for r in range(32)])  8.03 us
    ppermute x6, starting transfers between devices, along_x(): lax.ppermute(array, 'replica', [(r, r + 8 * k & 31) for r in range(32)])  7.48 us
    all_to_all x1, starting transfers between devices, per_device(): arrived = lax.all_to_all(regrouped, 'replica', 0, 0, tiled=True)  4.99 us
    ppermute x3, waiting for transfers between devices, along_y(): return lax.ppermute(array, 'tensor', [(t, t + 2 * k & 7) for t in range(8)])  4.86 us
    ppermute x14, waiting for transfers between devices, along_z(): lax.ppermute(array, 'replica', [(r, r & 24 | r + k & 7) for r in range(32)])  4.45 us
  transfers between devices with their start and end apart: 25, of which 15 were waited for; matrix products, arithmetic and copies ran while one was open for 0% of the time, Pallas kernels for 6%

profile of v1, /device:TPU:56, one launch (start us, length us, event | category | flops | bytes accessed | tf_op | source)
XLA Modules:
  0.0 116.6 jit_solution(17729073123800162623)
XLA Ops:
  0.6 0.0 copy-start.10
  0.6 0.0 copy-start.12
  0.7 0.0 copy-start.5
  0.7 0.0 copy-start.16
  0.7 28.9 %all_to_all.10.came = bf16[32,16,512]{2,1,0:T(8,128)(2,1)S(1)} all-to-all(bf16[32,16,512]{2,1,0:T(8,128)(2,1)} %bitcast.3), channel_id=1, replica_groups=mesh['replica'=32,'tensor'=8] {'replica'}, dimensions={0} | all-to-all | bytes 1048576 | tf_op jit(solution)/shard_map/all_to_all | solution.py:348
  29.7 0.7 copy-done.6
  30.4 1.4 %regroup.1 = bf16[32,16,512]{2,1,0:T(8,128)(2,1)} custom-call(s32[2,128]{1,0:T(2,128)S(1)} %copy-done.6, bf16[32,16,512]{2,1,0:T(8,128)(2,1)S(1)} %all_to_all.10.came), custom_call_target="tpu_custom_call" | custom-call | flops 1000000 | bytes 1000000 | tf_op jit(solution)/shard_map/regroup/pallas_call | solution.py:411
  31.8 5.0 %all-to-all-start.1 = ((bf16[32,16,512]{2,1,0:T(8,128)(2,1)}), bf16[32,16,512]{2,1,0:T(8,128)(2,1)S(1)}, u32[]{:S(2)}, u32[]{:S(2)}) async-start(bf16[32,16,512]{2,1,0:T(8,128)(2,1)} %regroup.1), calls=%async_computation.1 | async-start | bytes 1048576 | tf_op jit(solution)/shard_map/all_to_all | solution.py:414
  36.8 0.7 copy-done.4
  37.5 0.7 copy-done.7
  38.1 0.7 copy-done.9
  38.8 0.7 copy-done.11
  39.5 0.7 copy-done.13
  40.2 0.7 copy-done.15
  40.9 0.7 copy-done.17
  41.6 1.8 %pack.1 = (bf16[8,1792]{1,0:T(8,128)(2,1)S(1)}, s32[2,32]{1,0:T(2,128)S(1)}) custom-call(s32[2,128]{1,0:T(2,128)S(1)} %copy-done.7, bf16[2,4,1024]{2,1,0:T(4,128)(2,1)S(1)} %copy-done.13, bf16[2,4,2,128]{3,2,1,0:T(2,128)(2,1)S(1)} %copy-done.17, bf16[2,4,128]{2,1,0:T(4,128)(2,1)S(1)} %copy-done.15, bf16[2,4,512]{2,1,0:T(4,128)(2,1)S(1)} %copy-done.4, ...), custom_call_target="tpu_custom_call" | custom-call | flops 1000000 | bytes 1000000 | tf_op jit(solution)/shard_map/pack/pallas_call | solution.py:350
  43.4 2.8 %collective-permute-start.2 = (bf16[8,1792]{1,0:T(8,128)(2,1)S(1)}, bf16[8,1792]{1,0:T(8,128)(2,1)S(1)}, u32[]{:S(2)}, u32[]{:S(2)}) collective-permute-start(bf16[8,1792]{1,0:T(8,128)(2,1)S(1)} %get-tuple-element.31.refs_0_), channel_id=1, source_target_pairs={{0,192},{8,200},{16,208},{24,216},{32,224},{40,232},{48,240},{56,2... | collective-permute-start | bytes 86024 | tf_op jit(solution)/shard_map/ppermute | solution.py:310
  46.2 0.8 collective-permute-start.1
  47.0 0.9 collective-permute-start
  47.8 3.7 %collective-permute-done.1.refs_2_ = bf16[8,1792]{1,0:T(8,128)(2,1)S(1)} collective-permute-done((bf16[8,1792]{1,0:T(8,128)(2,1)S(1)}, bf16[8,1792]{1,0:T(8,128)(2,1)S(1)}, u32[]{:S(2)}, u32[]{:S(2)}) %collective-permute-start.1) | collective-permute-done | bytes 28704 | tf_op jit(solution)/shard_map/ppermute | solution.py:310
  51.5 0.5 collective-permute-done.refs_1_
  52.1 0.6 sort_out.1
  52.7 1.6 %collective-permute-start.3 = (bf16[8,1792]{1,0:T(8,128)(2,1)S(1)}, bf16[8,1792]{1,0:T(8,128)(2,1)S(1)}, u32[]{:S(2)}, u32[]{:S(2)}) collective-permute-start(bf16[8,1792]{1,0:T(8,128)(2,1)S(1)} %get-tuple-element.33), channel_id=1, source_target_pairs={{0,8},{8,16},{16,24},{24,32},{32,40},{40,48},{48,56},{56,0},{64,72... | collective-permute-start | bytes 86024 | tf_op jit(solution)/shard_map/ppermute | solution.py:314
  54.3 3.5 %collective-permute-start.4 = (bf16[8,1792]{1,0:T(8,128)(2,1)S(1)}, bf16[8,1792]{1,0:T(8,128)(2,1)S(1)}, u32[]{:S(2)}, u32[]{:S(2)}) collective-permute-start(bf16[8,1792]{1,0:T(8,128)(2,1)S(1)} %get-tuple-element.34), channel_id=1, source_target_pairs={{0,16},{8,24},{16,32},{24,40},{32,48},{40,56},{48,0},{56,8},{64,80... | collective-permute-start | bytes 86024 | tf_op jit(solution)/shard_map/ppermute | solution.py:314
  57.8 0.6 collective-permute-start.5
  58.4 3.3 %collective-permute-start.6 = (bf16[8,1792]{1,0:T(8,128)(2,1)S(1)}, bf16[8,1792]{1,0:T(8,128)(2,1)S(1)}, u32[]{:S(2)}, u32[]{:S(2)}) collective-permute-start(bf16[8,1792]{1,0:T(8,128)(2,1)S(1)} %get-tuple-element.36), channel_id=1, source_target_pairs={{0,32},{8,40},{16,48},{24,56},{32,0},{40,8},{48,16},{56,24},{64,96... | collective-permute-start | bytes 86024 | tf_op jit(solution)/shard_map/ppermute | solution.py:314
  61.7 1.8 %collective-permute-start.7 = (bf16[8,1792]{1,0:T(8,128)(2,1)S(1)}, bf16[8,1792]{1,0:T(8,128)(2,1)S(1)}, u32[]{:S(2)}, u32[]{:S(2)}) collective-permute-start(bf16[8,1792]{1,0:T(8,128)(2,1)S(1)} %get-tuple-element.37), channel_id=1, source_target_pairs={{0,40},{8,48},{16,56},{24,0},{32,8},{40,16},{48,24},{56,32},{64,10... | collective-permute-start | bytes 86024 | tf_op jit(solution)/shard_map/ppermute | solution.py:314
  63.5 2.5 %collective-permute-start.8 = (bf16[8,1792]{1,0:T(8,128)(2,1)S(1)}, bf16[8,1792]{1,0:T(8,128)(2,1)S(1)}, u32[]{:S(2)}, u32[]{:S(2)}) collective-permute-start(bf16[8,1792]{1,0:T(8,128)(2,1)S(1)} %get-tuple-element.38), channel_id=1, source_target_pairs={{0,48},{8,56},{16,0},{24,8},{32,16},{40,24},{48,32},{56,40},{64,11... | collective-permute-start | bytes 86024 | tf_op jit(solution)/shard_map/ppermute | solution.py:314
  66.0 2.4 %collective-permute-start.9 = (bf16[8,1792]{1,0:T(8,128)(2,1)S(1)}, bf16[8,1792]{1,0:T(8,128)(2,1)S(1)}, u32[]{:S(2)}, u32[]{:S(2)}) collective-permute-start(bf16[8,1792]{1,0:T(8,128)(2,1)S(1)} %get-tuple-element.39), channel_id=1, source_target_pairs={{0,56},{8,0},{16,8},{24,16},{32,24},{40,32},{48,40},{56,48},{64,12... | collective-permute-start | bytes 86024 | tf_op jit(solution)/shard_map/ppermute | solution.py:314
  68.5 0.2 collective-permute-done.7.refs_5_
  68.7 1.3 %collective-permute-done.9.refs_7_ = bf16[8,1792]{1,0:T(8,128)(2,1)S(1)} collective-permute-done((bf16[8,1792]{1,0:T(8,128)(2,1)S(1)}, bf16[8,1792]{1,0:T(8,128)(2,1)S(1)}, u32[]{:S(2)}, u32[]{:S(2)}) %collective-permute-start.9) | collective-permute-done | bytes 28704 | tf_op jit(solution)/shard_map/ppermute | solution.py:314
  70.0 1.0 copy-done.1
  71.1 1.2 %copy-done.2 = bf16[4,1024,128]{2,1,0:T(8,128)(2,1)S(1)} copy-done((bf16[4,1024,128]{2,1,0:T(8,128)(2,1)S(1)}, bf16[4,1024,128]{2,1,0:T(8,128)(2,1)}, u32[]{:S(2)}) %copy-start.2) | copy-done | bytes 1048600
  72.3 1.2 %copy-done.3 = bf16[4,1024,128]{2,1,0:T(8,128)(2,1)S(1)} copy-done((bf16[4,1024,128]{2,1,0:T(8,128)(2,1)S(1)}, bf16[4,1024,128]{2,1,0:T(8,128)(2,1)}, u32[]{:S(2)}) %copy-start.3) | copy-done | bytes 1048600
  73.5 0.7 copy-done.22
  74.2 1.5 %attend.1 = (bf16[8,1536]{1,0:T(8,128)(2,1)S(1)}, bf16[8,384]{1,0:T(8,128)(2,1)S(1)}) custom-call(s32[2,128]{1,0:T(2,128)S(1)} %copy-done.7, s32[2,32]{1,0:T(2,128)S(1)} %get-tuple-element.30.inverse, s32[32]{0:T(128)S(1)} %copy-done.22, bf16[8,1792]{1,0:T(8,128)(2,1)S(1)} %get-tuple-element.32.refs_0_, bf16[8,1792]{1,0:T(8,128)(2,1)S(1)} %collective-permute-done.3.refs_1_, ...), custom_call_target="tpu_custom_call" | custom-call | flops 140000000 | bytes 3000000 | tf_op jit(solution)/shard_map/attend/pallas_call | solution.py:368
  75.7 0.5 collective-permute-start.12
  76.2 1.3 %collective-permute-start.11 = (bf16[8,1536]{1,0:T(8,128)(2,1)S(1)}, bf16[8,1536]{1,0:T(8,128)(2,1)S(1)}, u32[]{:S(2)}, u32[]{:S(2)}) collective-permute-start(bf16[8,1536]{1,0:T(8,128)(2,1)S(1)} %get-tuple-element.41.refs_0_), channel_id=1, source_target_pairs={{0,128},{8,136},{16,144},{24,152},{32,160},{40,168},{48,176},{56,1... | collective-permute-start | bytes 73736 | tf_op jit(solution)/shard_map/ppermute | solution.py:310
  77.5 1.2 %collective-permute-start.10 = (bf16[8,1536]{1,0:T(8,128)(2,1)S(1)}, bf16[8,1536]{1,0:T(8,128)(2,1)S(1)}, u32[]{:S(2)}, u32[]{:S(2)}) collective-permute-start(bf16[8,1536]{1,0:T(8,128)(2,1)S(1)} %get-tuple-element.41.refs_0_), channel_id=1, source_target_pairs={{0,64},{8,72},{16,80},{24,88},{32,96},{40,104},{48,112},{56,120},{... | collective-permute-start | bytes 73736 | tf_op jit(solution)/shard_map/ppermute | solution.py:310
  78.7 0.9 collective-permute-done.12.refs_3_
  79.5 2.0 %collective-permute-done.11.refs_2_ = bf16[8,1536]{1,0:T(8,128)(2,1)S(1)} collective-permute-done((bf16[8,1536]{1,0:T(8,128)(2,1)S(1)}, bf16[8,1536]{1,0:T(8,128)(2,1)S(1)}, u32[]{:S(2)}, u32[]{:S(2)}) %collective-permute-start.11) | collective-permute-done | bytes 24608 | tf_op jit(solution)/shard_map/ppermute | solution.py:310
  81.5 1.0 collective-permute-done.10.refs_1_
  82.5 0.6 sort_back.1
  83.1 1.9 %collective-permute-start.13 = (bf16[8,1536]{1,0:T(8,128)(2,1)S(1)}, bf16[8,1536]{1,0:T(8,128)(2,1)S(1)}, u32[]{:S(2)}, u32[]{:S(2)}) collective-permute-start(bf16[8,1536]{1,0:T(8,128)(2,1)S(1)} %get-tuple-element.43), channel_id=1, source_target_pairs={{0,8},{8,16},{16,24},{24,32},{32,40},{40,48},{48,56},{56,0},{64,72... | collective-permute-start | bytes 73736 | tf_op jit(solution)/shard_map/ppermute | solution.py:314
  85.0 1.3 %collective-permute-start.14 = (bf16[8,1536]{1,0:T(8,128)(2,1)S(1)}, bf16[8,1536]{1,0:T(8,128)(2,1)S(1)}, u32[]{:S(2)}, u32[]{:S(2)}) collective-permute-start(bf16[8,1536]{1,0:T(8,128)(2,1)S(1)} %get-tuple-element.44), channel_id=1, source_target_pairs={{0,16},{8,24},{16,32},{24,40},{32,48},{40,56},{48,0},{56,8},{64,80... | collective-permute-start | bytes 73736 | tf_op jit(solution)/shard_map/ppermute | solution.py:314
  86.3 4.2 %collective-permute-start.15 = (bf16[8,1536]{1,0:T(8,128)(2,1)S(1)}, bf16[8,1536]{1,0:T(8,128)(2,1)S(1)}, u32[]{:S(2)}, u32[]{:S(2)}) collective-permute-start(bf16[8,1536]{1,0:T(8,128)(2,1)S(1)} %get-tuple-element.45), channel_id=1, source_target_pairs={{0,24},{8,32},{16,40},{24,48},{32,56},{40,0},{48,8},{56,16},{64,88... | collective-permute-start | bytes 73736 | tf_op jit(solution)/shard_map/ppermute | solution.py:314
  90.5 1.5 %collective-permute-start.16 = (bf16[8,1536]{1,0:T(8,128)(2,1)S(1)}, bf16[8,1536]{1,0:T(8,128)(2,1)S(1)}, u32[]{:S(2)}, u32[]{:S(2)}) collective-permute-start(bf16[8,1536]{1,0:T(8,128)(2,1)S(1)} %get-tuple-element.46), channel_id=1, source_target_pairs={{0,32},{8,40},{16,48},{24,56},{32,0},{40,8},{48,16},{56,24},{64,96... | collective-permute-start | bytes 73736 | tf_op jit(solution)/shard_map/ppermute | solution.py:314
  92.0 3.6 %collective-permute-start.17 = (bf16[8,1536]{1,0:T(8,128)(2,1)S(1)}, bf16[8,1536]{1,0:T(8,128)(2,1)S(1)}, u32[]{:S(2)}, u32[]{:S(2)}) collective-permute-start(bf16[8,1536]{1,0:T(8,128)(2,1)S(1)} %get-tuple-element.47), channel_id=1, source_target_pairs={{0,40},{8,48},{16,56},{24,0},{32,8},{40,16},{48,24},{56,32},{64,10... | collective-permute-start | bytes 73736 | tf_op jit(solution)/shard_map/ppermute | solution.py:314
  95.6 0.9 collective-permute-start.18
  96.5 1.5 %collective-permute-start.19 = (bf16[8,1536]{1,0:T(8,128)(2,1)S(1)}, bf16[8,1536]{1,0:T(8,128)(2,1)S(1)}, u32[]{:S(2)}, u32[]{:S(2)}) collective-permute-start(bf16[8,1536]{1,0:T(8,128)(2,1)S(1)} %get-tuple-element.49), channel_id=1, source_target_pairs={{0,56},{8,0},{16,8},{24,16},{32,24},{40,32},{48,40},{56,48},{64,12... | collective-permute-start | bytes 73736 | tf_op jit(solution)/shard_map/ppermute | solution.py:314
  98.0 0.3 collective-permute-done.16.refs_4_
  98.3 0.6 collective-permute-done.17.refs_5_
  98.8 1.6 %collective-permute-done.18.refs_6_ = bf16[8,1536]{1,0:T(8,128)(2,1)S(1)} collective-permute-done((bf16[8,1536]{1,0:T(8,128)(2,1)S(1)}, bf16[8,1536]{1,0:T(8,128)(2,1)S(1)}, u32[]{:S(2)}, u32[]{:S(2)}) %collective-permute-start.18) | collective-permute-done | bytes 24608 | tf_op jit(solution)/shard_map/ppermute | solution.py:314
  100.4 0.4 collective-permute-done.19.refs_7_
  100.9 2.2 %copy-done = bf16[512,4096]{1,0:T(8,128)(2,1)S(1)} copy-done((bf16[512,4096]{1,0:T(8,128)(2,1)S(1)}, bf16[512,4096]{1,0:T(8,128)(2,1)}, u32[]{:S(2)}) %copy-start) | copy-done | bytes 4194328
  103.1 2.0 %mamba.1 = (bf16[2,4,1024]{2,1,0:T(4,128)(2,1)}, bf16[4,8,512]{2,1,0:T(8,128)(2,1)S(1)}, bf16[4,8,512]{2,1,0:T(8,128)(2,1)S(1)}) custom-call(s32[2,128]{1,0:T(2,128)S(1)} %copy-done.7, f32[8]{0:T(128)S(1)} %copy-done.19, f32[8]{0:T(128)S(1)} %copy-done.20, f32[8]{0:T(128)S(1)} %copy-done.21, bf16[8,1536]{1,0:T(8,128)(2,1)S(1)} %get-tuple-element.42.refs_0_, ...), custom_call_target="tpu_custom_call" | custom-call | flops 40000000 | bytes 5000000 | tf_op jit(solution)/shard_map/mamba/pallas_call | solution.py:387
  105.1 1.2 %collective-permute-done.20.came = bf16[4,8,512]{2,1,0:T(8,128)(2,1)S(1)} collective-permute-done((bf16[4,8,512]{2,1,0:T(8,128)(2,1)S(1)}, bf16[4,8,512]{2,1,0:T(8,128)(2,1)S(1)}, u32[]{:S(2)}, u32[]{:S(2)}) %collective-permute-start.20) | collective-permute-done | bytes 32800 | tf_op jit(solution)/shard_map/ppermute | solution.py:322
  106.4 0.3 collective-permute-start.21
  106.7 2.6 %collective-permute-start.22 = (bf16[8,512]{1,0:T(8,128)(2,1)S(1)}, bf16[8,512]{1,0:T(8,128)(2,1)S(1)}, u32[]{:S(2)}, u32[]{:S(2)}) collective-permute-start(bf16[8,512]{1,0:T(8,128)(2,1)S(1)} %get-tuple-element.54), channel_id=1, source_target_pairs={{0,4},{1,5},{2,6},{3,7},{4,0},{5,1},{6,2},{7,3},{8,12},{9,13},{10,... | collective-permute-start | bytes 24584 | tf_op jit(solution)/shard_map/ppermute | solution.py:318
  109.3 0.8 collective-permute-done.21.b
  110.1 1.7 %collective-permute-done.22.c = bf16[8,512]{1,0:T(8,128)(2,1)S(1)} collective-permute-done((bf16[8,512]{1,0:T(8,128)(2,1)S(1)}, bf16[8,512]{1,0:T(8,128)(2,1)S(1)}, u32[]{:S(2)}, u32[]{:S(2)}) %collective-permute-start.22) | collective-permute-done | bytes 8224 | tf_op jit(solution)/shard_map/ppermute | solution.py:318
  111.8 2.3 %collective-permute-done.23.d = bf16[8,512]{1,0:T(8,128)(2,1)S(1)} collective-permute-done((bf16[8,512]{1,0:T(8,128)(2,1)S(1)}, bf16[8,512]{1,0:T(8,128)(2,1)S(1)}, u32[]{:S(2)}, u32[]{:S(2)}) %collective-permute-start.23) | collective-permute-done | bytes 8224 | tf_op jit(solution)/shard_map/ppermute | solution.py:318
  114.1 0.6 last_sum.1
  114.7 1.9 %advance.1 = bf16[32,16,512]{2,1,0:T(8,128)(2,1)} custom-call(s32[2,128]{1,0:T(2,128)S(1)} %copy-done.8, f32[8]{0:T(128)S(1)} %copy-done.19, f32[8]{0:T(128)S(1)} %copy-done.20, bf16[32,16,512]{2,1,0:T(8,128)(2,1)S(1)} %all-to-all-done.1.state, bf16[8,384]{1,0:T(8,128)(2,1)S(1)} %get-tuple-element.40.carry.refs_8_, bf16[2,4,512]{2,1,0:T(4,128)(2,1)S(1)} %copy-done.5, ...), custom_call_target="tpu_custom_call" | custom-call | flops 4000000 | bytes 1000000 | tf_op jit(solution)/shard_map/advance/pallas_call | solution.py:415
  (42 shorter events, 0.1 us)
Async XLA Ops:
  0.6 100.2 %copy-start.10 = (bf16[2,4,128]{2,1,0:T(4,128)(2,1)S(1)}, bf16[2,4,128]{2,1,0:T(4,128)(2,1)}, u32[]{:S(2)}) copy-start(bf16[2,4,128]{2,1,0:T(4,128)(2,1)} %refs_12_.1) | copy-start | bytes 6148
  0.6 100.2 %copy-start.12 = (bf16[2,4,8]{2,1,0:T(4,128)(2,1)S(1)}, bf16[2,4,8]{2,1,0:T(4,128)(2,1)}, u32[]{:S(2)}) copy-start(bf16[2,4,8]{2,1,0:T(4,128)(2,1)} %refs_11_.1) | copy-start | bytes 388
  0.7 100.2 %copy-start.5 = (bf16[2,4,512]{2,1,0:T(4,128)(2,1)S(1)}, bf16[2,4,512]{2,1,0:T(4,128)(2,1)}, u32[]{:S(2)}) copy-start(bf16[2,4,512]{2,1,0:T(4,128)(2,1)} %refs_9_.3) | copy-start | bytes 24580
  0.7 100.2 %copy-start.16 = (bf16[2,4,128]{2,1,0:T(4,128)(2,1)S(1)}, bf16[2,4,128]{2,1,0:T(4,128)(2,1)}, u32[]{:S(2)}) copy-start(bf16[2,4,128]{2,1,0:T(4,128)(2,1)} %refs_13_.1) | copy-start | bytes 6148
  0.7 100.2 %copy-start.20 = (f32[8]{0:T(128)S(1)}, f32[8]{0:T(128)}, u32[]{:S(2)}) copy-start(f32[8]{0:T(128)} %dt_bias.3) | copy-start | bytes 100
  0.7 100.2 %copy-start.19 = (f32[8]{0:T(128)S(1)}, f32[8]{0:T(128)}, u32[]{:S(2)}) copy-start(f32[8]{0:T(128)} %a_rate.3) | copy-start | bytes 100
  0.7 100.2 %copy-start.18 = (f32[512]{0:T(512)S(1)}, f32[512]{0:T(512)}, u32[]{:S(2)}) copy-start(f32[512]{0:T(512)} %param.32) | copy-start | bytes 6148
  0.7 100.2 %copy-start.21 = (f32[8]{0:T(128)S(1)}, f32[8]{0:T(128)}, u32[]{:S(2)}) copy-start(f32[8]{0:T(128)} %skip.1) | copy-start | bytes 100
  0.7 100.2 %copy-start.14 = (bf16[2,4,512]{2,1,0:T(4,128)(2,1)S(1)}, bf16[2,4,512]{2,1,0:T(4,128)(2,1)}, u32[]{:S(2)}) copy-start(bf16[2,4,512]{2,1,0:T(4,128)(2,1)} %refs_10_.3) | copy-start | bytes 24580
  29.7 0.7 copy-start.6
  31.8 83.0 %copy-start.8 = (s32[2,128]{1,0:T(2,128)S(1)}, s32[2,128]{1,0:T(2,128)}, u32[]{:S(2)}) copy-start(s32[2,128]{1,0:T(2,128)} %parents.13) | copy-start | bytes 3076
  31.8 83.0 %all-to-all-start.1 = ((bf16[32,16,512]{2,1,0:T(8,128)(2,1)}), bf16[32,16,512]{2,1,0:T(8,128)(2,1)S(1)}, u32[]{:S(2)}, u32[]{:S(2)}) async-start(bf16[32,16,512]{2,1,0:T(8,128)(2,1)} %regroup.1), calls=%async_computation.1 | async-start | bytes 1048576 | tf_op jit(solution)/shard_map/all_to_all | solution.py:414
  36.8 0.7 copy-start.4
  37.5 0.7 copy-start.7
  38.1 0.7 copy-start.9
  38.8 0.7 copy-start.11
  39.5 0.7 copy-start.13
  40.2 0.7 copy-start.15
  40.9 0.7 copy-start.17
  43.4 4.5 %collective-permute-start.2 = (bf16[8,1792]{1,0:T(8,128)(2,1)S(1)}, bf16[8,1792]{1,0:T(8,128)(2,1)S(1)}, u32[]{:S(2)}, u32[]{:S(2)}) collective-permute-start(bf16[8,1792]{1,0:T(8,128)(2,1)S(1)} %get-tuple-element.31.refs_0_), channel_id=1, source_target_pairs={{0,192},{8,200},{16,208},{24,216},{32,224},{40,232},{48,240},{56,2... | collective-permute-start | bytes 86024 | tf_op jit(solution)/shard_map/ppermute | solution.py:310
  46.2 5.4 %collective-permute-start.1 = (bf16[8,1792]{1,0:T(8,128)(2,1)S(1)}, bf16[8,1792]{1,0:T(8,128)(2,1)S(1)}, u32[]{:S(2)}, u32[]{:S(2)}) collective-permute-start(bf16[8,1792]{1,0:T(8,128)(2,1)S(1)} %get-tuple-element.31.refs_0_), channel_id=1, source_target_pairs={{0,128},{8,136},{16,144},{24,152},{32,160},{40,168},{48,176},{56,1... | collective-permute-start | bytes 86024 | tf_op jit(solution)/shard_map/ppermute | solution.py:310
  47.0 5.1 %collective-permute-start = (bf16[8,1792]{1,0:T(8,128)(2,1)S(1)}, bf16[8,1792]{1,0:T(8,128)(2,1)S(1)}, u32[]{:S(2)}, u32[]{:S(2)}) collective-permute-start(bf16[8,1792]{1,0:T(8,128)(2,1)S(1)} %get-tuple-element.31.refs_0_), channel_id=1, source_target_pairs={{0,64},{8,72},{16,80},{24,88},{32,96},{40,104},{48,112},{56,120},{... | collective-permute-start | bytes 86024 | tf_op jit(solution)/shard_map/ppermute | solution.py:310
  52.7 10.8 %collective-permute-start.3 = (bf16[8,1792]{1,0:T(8,128)(2,1)S(1)}, bf16[8,1792]{1,0:T(8,128)(2,1)S(1)}, u32[]{:S(2)}, u32[]{:S(2)}) collective-permute-start(bf16[8,1792]{1,0:T(8,128)(2,1)S(1)} %get-tuple-element.33), channel_id=1, source_target_pairs={{0,8},{8,16},{16,24},{24,32},{32,40},{40,48},{48,56},{56,0},{64,72... | collective-permute-start | bytes 86024 | tf_op jit(solution)/shard_map/ppermute | solution.py:314
  54.3 11.7 %collective-permute-start.4 = (bf16[8,1792]{1,0:T(8,128)(2,1)S(1)}, bf16[8,1792]{1,0:T(8,128)(2,1)S(1)}, u32[]{:S(2)}, u32[]{:S(2)}) collective-permute-start(bf16[8,1792]{1,0:T(8,128)(2,1)S(1)} %get-tuple-element.34), channel_id=1, source_target_pairs={{0,16},{8,24},{16,32},{24,40},{32,48},{40,56},{48,0},{56,8},{64,80... | collective-permute-start | bytes 86024 | tf_op jit(solution)/shard_map/ppermute | solution.py:314
  57.8 10.6 %collective-permute-start.5 = (bf16[8,1792]{1,0:T(8,128)(2,1)S(1)}, bf16[8,1792]{1,0:T(8,128)(2,1)S(1)}, u32[]{:S(2)}, u32[]{:S(2)}) collective-permute-start(bf16[8,1792]{1,0:T(8,128)(2,1)S(1)} %get-tuple-element.35), channel_id=1, source_target_pairs={{0,24},{8,32},{16,40},{24,48},{32,56},{40,0},{48,8},{56,16},{64,88... | collective-permute-start | bytes 86024 | tf_op jit(solution)/shard_map/ppermute | solution.py:314
  58.4 10.1 %collective-permute-start.6 = (bf16[8,1792]{1,0:T(8,128)(2,1)S(1)}, bf16[8,1792]{1,0:T(8,128)(2,1)S(1)}, u32[]{:S(2)}, u32[]{:S(2)}) collective-permute-start(bf16[8,1792]{1,0:T(8,128)(2,1)S(1)} %get-tuple-element.36), channel_id=1, source_target_pairs={{0,32},{8,40},{16,48},{24,56},{32,0},{40,8},{48,16},{56,24},{64,96... | collective-permute-start | bytes 86024 | tf_op jit(solution)/shard_map/ppermute | solution.py:314
  61.7 7.0 %collective-permute-start.7 = (bf16[8,1792]{1,0:T(8,128)(2,1)S(1)}, bf16[8,1792]{1,0:T(8,128)(2,1)S(1)}, u32[]{:S(2)}, u32[]{:S(2)}) collective-permute-start(bf16[8,1792]{1,0:T(8,128)(2,1)S(1)} %get-tuple-element.37), channel_id=1, source_target_pairs={{0,40},{8,48},{16,56},{24,0},{32,8},{40,16},{48,24},{56,32},{64,10... | collective-permute-start | bytes 86024 | tf_op jit(solution)/shard_map/ppermute | solution.py:314
  63.5 5.2 %collective-permute-start.8 = (bf16[8,1792]{1,0:T(8,128)(2,1)S(1)}, bf16[8,1792]{1,0:T(8,128)(2,1)S(1)}, u32[]{:S(2)}, u32[]{:S(2)}) collective-permute-start(bf16[8,1792]{1,0:T(8,128)(2,1)S(1)} %get-tuple-element.38), channel_id=1, source_target_pairs={{0,48},{8,56},{16,0},{24,8},{32,16},{40,24},{48,32},{56,40},{64,11... | collective-permute-start | bytes 86024 | tf_op jit(solution)/shard_map/ppermute | solution.py:314
  66.0 4.0 %collective-permute-start.9 = (bf16[8,1792]{1,0:T(8,128)(2,1)S(1)}, bf16[8,1792]{1,0:T(8,128)(2,1)S(1)}, u32[]{:S(2)}, u32[]{:S(2)}) collective-permute-start(bf16[8,1792]{1,0:T(8,128)(2,1)S(1)} %get-tuple-element.39), channel_id=1, source_target_pairs={{0,56},{8,0},{16,8},{24,16},{32,24},{40,32},{48,40},{56,48},{64,12... | collective-permute-start | bytes 86024 | tf_op jit(solution)/shard_map/ppermute | solution.py:314
  70.0 1.0 copy-start.1
  71.1 1.2 %copy-start.2 = (bf16[4,1024,128]{2,1,0:T(8,128)(2,1)S(1)}, bf16[4,1024,128]{2,1,0:T(8,128)(2,1)}, u32[]{:S(2)}) copy-start(bf16[4,1024,128]{2,1,0:T(8,128)(2,1)} %refs_8_.1) | copy-start | bytes 3145732
  72.3 1.2 %copy-start.3 = (bf16[4,1024,128]{2,1,0:T(8,128)(2,1)S(1)}, bf16[4,1024,128]{2,1,0:T(8,128)(2,1)}, u32[]{:S(2)}) copy-start(bf16[4,1024,128]{2,1,0:T(8,128)(2,1)} %refs_9_.2) | copy-start | bytes 3145732
  73.5 0.7 copy-start.22
  75.7 3.9 %collective-permute-start.12 = (bf16[8,1536]{1,0:T(8,128)(2,1)S(1)}, bf16[8,1536]{1,0:T(8,128)(2,1)S(1)}, u32[]{:S(2)}, u32[]{:S(2)}) collective-permute-start(bf16[8,1536]{1,0:T(8,128)(2,1)S(1)} %get-tuple-element.41.refs_0_), channel_id=1, source_target_pairs={{0,192},{8,200},{16,208},{24,216},{32,224},{40,232},{48,240},{56,2... | collective-permute-start | bytes 73736 | tf_op jit(solution)/shard_map/ppermute | solution.py:310
  76.2 5.3 %collective-permute-start.11 = (bf16[8,1536]{1,0:T(8,128)(2,1)S(1)}, bf16[8,1536]{1,0:T(8,128)(2,1)S(1)}, u32[]{:S(2)}, u32[]{:S(2)}) collective-permute-start(bf16[8,1536]{1,0:T(8,128)(2,1)S(1)} %get-tuple-element.41.refs_0_), channel_id=1, source_target_pairs={{0,128},{8,136},{16,144},{24,152},{32,160},{40,168},{48,176},{56,1... | collective-permute-start | bytes 73736 | tf_op jit(solution)/shard_map/ppermute | solution.py:310
  77.5 5.0 %collective-permute-start.10 = (bf16[8,1536]{1,0:T(8,128)(2,1)S(1)}, bf16[8,1536]{1,0:T(8,128)(2,1)S(1)}, u32[]{:S(2)}, u32[]{:S(2)}) collective-permute-start(bf16[8,1536]{1,0:T(8,128)(2,1)S(1)} %get-tuple-element.41.refs_0_), channel_id=1, source_target_pairs={{0,64},{8,72},{16,80},{24,88},{32,96},{40,104},{48,112},{56,120},{... | collective-permute-start | bytes 73736 | tf_op jit(solution)/shard_map/ppermute | solution.py:310
  83.1 12.5 %collective-permute-start.13 = (bf16[8,1536]{1,0:T(8,128)(2,1)S(1)}, bf16[8,1536]{1,0:T(8,128)(2,1)S(1)}, u32[]{:S(2)}, u32[]{:S(2)}) collective-permute-start(bf16[8,1536]{1,0:T(8,128)(2,1)S(1)} %get-tuple-element.43), channel_id=1, source_target_pairs={{0,8},{8,16},{16,24},{24,32},{32,40},{40,48},{48,56},{56,0},{64,72... | collective-permute-start | bytes 73736 | tf_op jit(solution)/shard_map/ppermute | solution.py:314
  85.0 11.5 %collective-permute-start.14 = (bf16[8,1536]{1,0:T(8,128)(2,1)S(1)}, bf16[8,1536]{1,0:T(8,128)(2,1)S(1)}, u32[]{:S(2)}, u32[]{:S(2)}) collective-permute-start(bf16[8,1536]{1,0:T(8,128)(2,1)S(1)} %get-tuple-element.44), channel_id=1, source_target_pairs={{0,16},{8,24},{16,32},{24,40},{32,48},{40,56},{48,0},{56,8},{64,80... | collective-permute-start | bytes 73736 | tf_op jit(solution)/shard_map/ppermute | solution.py:314
  86.3 11.6 %collective-permute-start.15 = (bf16[8,1536]{1,0:T(8,128)(2,1)S(1)}, bf16[8,1536]{1,0:T(8,128)(2,1)S(1)}, u32[]{:S(2)}, u32[]{:S(2)}) collective-permute-start(bf16[8,1536]{1,0:T(8,128)(2,1)S(1)} %get-tuple-element.45), channel_id=1, source_target_pairs={{0,24},{8,32},{16,40},{24,48},{32,56},{40,0},{48,8},{56,16},{64,88... | collective-permute-start | bytes 73736 | tf_op jit(solution)/shard_map/ppermute | solution.py:314
  90.5 7.7 %collective-permute-start.16 = (bf16[8,1536]{1,0:T(8,128)(2,1)S(1)}, bf16[8,1536]{1,0:T(8,128)(2,1)S(1)}, u32[]{:S(2)}, u32[]{:S(2)}) collective-permute-start(bf16[8,1536]{1,0:T(8,128)(2,1)S(1)} %get-tuple-element.46), channel_id=1, source_target_pairs={{0,32},{8,40},{16,48},{24,56},{32,0},{40,8},{48,16},{56,24},{64,96... | collective-permute-start | bytes 73736 | tf_op jit(solution)/shard_map/ppermute | solution.py:314
  92.0 6.8 %collective-permute-start.17 = (bf16[8,1536]{1,0:T(8,128)(2,1)S(1)}, bf16[8,1536]{1,0:T(8,128)(2,1)S(1)}, u32[]{:S(2)}, u32[]{:S(2)}) collective-permute-start(bf16[8,1536]{1,0:T(8,128)(2,1)S(1)} %get-tuple-element.47), channel_id=1, source_target_pairs={{0,40},{8,48},{16,56},{24,0},{32,8},{40,16},{48,24},{56,32},{64,10... | collective-permute-start | bytes 73736 | tf_op jit(solution)/shard_map/ppermute | solution.py:314
  95.6 4.8 %collective-permute-start.18 = (bf16[8,1536]{1,0:T(8,128)(2,1)S(1)}, bf16[8,1536]{1,0:T(8,128)(2,1)S(1)}, u32[]{:S(2)}, u32[]{:S(2)}) collective-permute-start(bf16[8,1536]{1,0:T(8,128)(2,1)S(1)} %get-tuple-element.48), channel_id=1, source_target_pairs={{0,48},{8,56},{16,0},{24,8},{32,16},{40,24},{48,32},{56,40},{64,11... | collective-permute-start | bytes 73736 | tf_op jit(solution)/shard_map/ppermute | solution.py:314
  96.5 4.3 %collective-permute-start.19 = (bf16[8,1536]{1,0:T(8,128)(2,1)S(1)}, bf16[8,1536]{1,0:T(8,128)(2,1)S(1)}, u32[]{:S(2)}, u32[]{:S(2)}) collective-permute-start(bf16[8,1536]{1,0:T(8,128)(2,1)S(1)} %get-tuple-element.49), channel_id=1, source_target_pairs={{0,56},{8,0},{16,8},{24,16},{32,24},{40,32},{48,40},{56,48},{64,12... | collective-permute-start | bytes 73736 | tf_op jit(solution)/shard_map/ppermute | solution.py:314
  100.9 2.2 %copy-start = (bf16[512,4096]{1,0:T(8,128)(2,1)S(1)}, bf16[512,4096]{1,0:T(8,128)(2,1)}, u32[]{:S(2)}) copy-start(bf16[512,4096]{1,0:T(8,128)(2,1)} %refs_15_.1) | copy-start | bytes 12582916
  105.1 1.2 %collective-permute-start.20 = (bf16[4,8,512]{2,1,0:T(8,128)(2,1)S(1)}, bf16[4,8,512]{2,1,0:T(8,128)(2,1)S(1)}, u32[]{:S(2)}, u32[]{:S(2)}) collective-permute-start(bf16[4,8,512]{2,1,0:T(8,128)(2,1)S(1)} %get-tuple-element.51), channel_id=1, source_target_pairs={{0,1},{1,0},{2,3},{3,2},{4,5},{5,4},{6,7},{7,6},{8,9},{9,8},{10,11... | collective-permute-start | bytes 98312 | tf_op jit(solution)/shard_map/ppermute | solution.py:322
  106.4 3.7 %collective-permute-start.21 = (bf16[8,512]{1,0:T(8,128)(2,1)S(1)}, bf16[8,512]{1,0:T(8,128)(2,1)S(1)}, u32[]{:S(2)}, u32[]{:S(2)}) collective-permute-start(bf16[8,512]{1,0:T(8,128)(2,1)S(1)} %get-tuple-element.53), channel_id=1, source_target_pairs={{0,2},{1,3},{2,4},{3,5},{4,6},{5,7},{6,0},{7,1},{8,10},{9,11},{10,... | collective-permute-start | bytes 24584 | tf_op jit(solution)/shard_map/ppermute | solution.py:318
  106.7 5.2 %collective-permute-start.22 = (bf16[8,512]{1,0:T(8,128)(2,1)S(1)}, bf16[8,512]{1,0:T(8,128)(2,1)S(1)}, u32[]{:S(2)}, u32[]{:S(2)}) collective-permute-start(bf16[8,512]{1,0:T(8,128)(2,1)S(1)} %get-tuple-element.54), channel_id=1, source_target_pairs={{0,4},{1,5},{2,6},{3,7},{4,0},{5,1},{6,2},{7,3},{8,12},{9,13},{10,... | collective-permute-start | bytes 24584 | tf_op jit(solution)/shard_map/ppermute | solution.py:318
  109.3 4.9 %collective-permute-start.23 = (bf16[8,512]{1,0:T(8,128)(2,1)S(1)}, bf16[8,512]{1,0:T(8,128)(2,1)S(1)}, u32[]{:S(2)}, u32[]{:S(2)}) collective-permute-start(bf16[8,512]{1,0:T(8,128)(2,1)S(1)} %get-tuple-element.55), channel_id=1, source_target_pairs={{0,6},{1,7},{2,0},{3,1},{4,2},{5,3},{6,4},{7,5},{8,14},{9,15},{10,... | collective-permute-start | bytes 24584 | tf_op jit(solution)/shard_map/ppermute | solution.py:318

commit v2 on v1

v2 whole, which is shorter than its diff:
```python
import functools

import jax
import jax.numpy as jnp
from jax import lax
from jax.experimental import pallas as pl
from jax.experimental.pallas import tpu as pltpu
from jax.sharding import PartitionSpec as P

F32 = jnp.float32
BF16 = jnp.bfloat16
HD = 128
ITEM_LANES = 1408
RESULT_LANES = 1536
CARRY_LANES = 384
BACK_LANES = RESULT_LANES + CARRY_LANES
MASKED = -1e30
MIB = 1024 * 1024

SMEM = pl.BlockSpec(memory_space=pltpu.SMEM)
VMEM = pl.BlockSpec(memory_space=pltpu.VMEM)
HBM = pl.BlockSpec(memory_space=pltpu.HBM)


def call(body, name, out_shape, in_specs, out_specs, scratch=(), flops=1000000, limit=32):
    return pl.pallas_call(
        body,
        name=name,
        out_shape=out_shape,
        in_specs=in_specs,
        out_specs=out_specs,
        scratch_shapes=list(scratch),
        compiler_params=pltpu.CompilerParams(vmem_limit_bytes=int(limit * MIB)),
        cost_estimate=pl.CostEstimate(flops=flops, bytes_accessed=0, transcendentals=0),
    )


def source_of(parents, step, prompt):
    return parents[step, prompt * 4] >> 2


def root_of(parents, prompt):
    return source_of(parents, 0, source_of(parents, 1, prompt))


def fetch(pairs, sems):
    copies = [pltpu.make_async_copy(src, dst, sems.at[i]) for i, (src, dst) in enumerate(pairs)]
    for copy in copies:
        copy.start()
    return copies


def pack_body(*refs):
    sources, (item, carry), wide, sems = refs[:6], refs[6:8], refs[14], refs[15]
    q, kv, c, x, b, dt = refs[8:14]
    copies = fetch(list(zip(sources, refs[8:14])), sems)
    for copy in copies:
        copy.wait()
    for t in range(2):
        rows = pl.ds(4 * t, 4)
        wide[rows, 0:1024] = q[t].astype(F32)
        for s in range(4):
            pair = kv[t, s].astype(F32)
            wide[pl.ds(4 * t + s, 1), 1024:1152] = pair[0:1]
            wide[pl.ds(4 * t + s, 1), 1152:1280] = pair[1:2]
        wide[rows, 1280:1408] = c[t].astype(F32)
    item[...] = wide[...].astype(BF16)
    wide[:, 0:CARRY_LANES] = jnp.zeros((8, CARRY_LANES), F32)
    x0 = x[0].astype(F32)
    wide[pl.ds(0, 4), 0:384] = x0[:, 0:384]
    wide[pl.ds(4, 4), 0:128] = x0[:, 384:512]
    wide[pl.ds(4, 4), 128:256] = b[0].astype(F32)
    wide[pl.ds(4, 4), 256:264] = dt[0].astype(F32)
    carry[...] = wide[:, 0:CARRY_LANES].astype(BF16)


def table_body(parents, lengths, table):
    for slot in range(128):
        table[0, slot] = parents[0, slot]
        table[1, slot] = parents[1, slot]
    for prompt in range(32):
        table[2, source_of(parents, 0, prompt)] = prompt
        table[3, root_of(parents, prompt)] = prompt
        table[4, prompt] = lengths[prompt]


def first_rows(shape):
    return lax.broadcasted_iota(jnp.int32, shape, 0) < 4


def bundle_body(own, up, down, out):
    out[0] = own[...]
    out[1] = up[...]
    out[2] = down[...]


def hold(held, own, up, down):
    for d, (ref, i) in enumerate(
        ((own, 0), (up, 0), (down, 1), (own, 1), (up, 1), (own, 2), (up, 2), (down, 0))
    ):
        held[d] = ref[i]


def stage_body(*refs):
    half = (len(refs) - 1) // 2
    for copy in fetch(list(zip(refs[:half], refs[half : 2 * half])), refs[-1]):
        copy.wait()


def sort_out_body(table, own, up, down, *refs):
    outs, held = refs[:4], refs[4]
    me = lax.axis_index("replica")
    hold(held, own, up, down)
    first = first_rows((8, ITEM_LANES))
    for k in range(4):
        dest = (me + 8 * k) & 31
        for_child = held[(me - table[2, dest]) & 7].astype(F32)
        for_second = held[(me - table[3, dest]) & 7].astype(F32)
        outs[k][...] = jnp.where(first, for_child, for_second).astype(BF16)


def bundle_back_body(own, one, two, three, out):
    for k, ref in enumerate((own, one, two, three)):
        out[k] = ref[...]


def sort_back_body(parents, own, up, down, *refs):
    outs, held = refs[:3], refs[3]
    me = lax.axis_index("replica")
    held[0], held[1], held[2] = own[...], up[...], down[...]
    first = first_rows((8, RESULT_LANES))
    for k, step in enumerate((0, 3, 5)):
        dest = (me & 24) | ((me + step) & 7)

        def pick(source):
            away = (me - source) & 7
            ring = jnp.where(away == 1, 1, jnp.where(away == 7, 2, 0))
            return held[ring, column(me, source)].astype(F32)

        one = pick(source_of(parents, 0, dest))[:, 0:RESULT_LANES]
        two = pick(root_of(parents, dest))[:, 0:RESULT_LANES]
        outs[k][:, 0:RESULT_LANES] = jnp.where(first, one, two).astype(BF16)
        outs[k][:, RESULT_LANES:] = pick(source_of(parents, 1, dest))[:, RESULT_LANES:].astype(BF16)


def came_by(me, source):
    away = (me - source) & 7
    up = (away >= 2) & (away <= 4)
    down = (away == 5) | (away == 6)
    return jnp.where(up, 1, jnp.where(down, 2, 0))


def column(me, source):
    return ((me >> 3) - (source >> 3)) & 3


def by_row(values, shape):
    row = lax.broadcasted_iota(jnp.int32, shape, 0)
    out = jnp.full(shape, values[-1], jnp.int32)
    for i in range(len(values) - 1):
        out = jnp.where(row == i, values[i], out)
    return out


def nt_dot(a, b):
    return lax.dot_general(a, b, (((1,), (1,)), ((), ())), preferred_element_type=F32)


def attend_body(parents, *refs):
    blocks = refs[:4]
    carry, keys, values, state, back, held = refs[4:10]
    me = lax.axis_index("replica")
    child = parents[2, me]
    second = parents[3, me]
    for k in range(4):
        held[k] = blocks[k][...]
    one = held[column(me, child)].astype(F32)
    two = held[column(me, second)].astype(F32)
    item = jnp.where(first_rows((8, ITEM_LANES)), one, two)
    back[:, RESULT_LANES:] = carry[...]

    query = jnp.concatenate([item[:, h * HD : (h + 1) * HD] for h in range(8)], axis=0).astype(BF16)
    pads = jnp.zeros((120, HD), F32)
    new_keys = jnp.concatenate([item[:, 1024:1152], pads], axis=0).astype(BF16)
    new_values = jnp.concatenate([item[:, 1152:1280], pads], axis=0).astype(BF16)
    c_rows = item[:, 1280:1408].astype(BF16)
    ways = [parents[1, second * 4 + s] & 3 for s in range(4)]
    roots = [parents[0, child * 4 + s] & 3 for s in range(4)]
    roots += [parents[0, child * 4 + ways[s]] & 3 for s in range(4)]
    scale = HD ** (-0.5)

    root_rows = by_row(roots, (8, 1024))
    live = lax.broadcasted_iota(jnp.int32, (8, 1024), 1) < parents[4, me]
    scores = jnp.zeros((8, 8, 1024), F32)
    for r in range(4):
        part = nt_dot(query, keys[r]).reshape(8, 8, 1024)
        scores = jnp.where((root_rows == r)[None], part, scores)
    scores = jnp.where(live[None], scores * scale, MASKED)

    row = lax.broadcasted_iota(jnp.int32, (8, HD), 0)
    key_at = lax.broadcasted_iota(jnp.int32, (8, HD), 1)
    way_rows = by_row([0, 1, 2, 3] + ways, (8, HD))
    seen = (key_at == row) | (key_at == way_rows)
    new_scores = nt_dot(query, new_keys).reshape(8, 8, HD) * scale
    new_scores = jnp.where(seen[None], new_scores, MASKED)

    top = jnp.maximum(
        jnp.max(scores, axis=-1, keepdims=True), jnp.max(new_scores, axis=-1, keepdims=True)
    )
    weights = jnp.exp(scores - top)
    new_weights = jnp.exp(new_scores - top)
    total = jnp.sum(weights, axis=-1, keepdims=True) + jnp.sum(new_weights, axis=-1, keepdims=True)
    mixed = jnp.dot(
        new_weights.reshape(64, HD).astype(BF16), new_values, preferred_element_type=F32
    )
    for r in range(4):
        mine = jnp.where((root_rows == r)[None], weights, 0.0).reshape(64, 1024).astype(BF16)
        mixed = mixed + jnp.dot(mine, values[r], preferred_element_type=F32)
    mixed = mixed / total.reshape(64, 1)
    for h in range(8):
        back[:, h * HD : (h + 1) * HD] = mixed[h * 8 : (h + 1) * 8].astype(BF16)

    root_wide = by_row(roots, (8, 512))
    read = jnp.zeros((8, 512), F32)
    for r in range(4):
        part = jnp.dot(c_rows, state[r], preferred_element_type=F32)
        read = jnp.where(root_wide == r, part, read)
    back[:, 1024:1536] = read.astype(BF16)


def per_head(ref, rows=8):
    head = lax.broadcasted_iota(jnp.int32, (rows, 512), 1) >> 6
    out = jnp.full((rows, 512), ref[7], F32)
    for h in range(7):
        out = jnp.where(head == h, ref[h], out)
    return out


def spread_heads(dt):
    head = lax.broadcasted_iota(jnp.int32, (HD, 512), 0)
    lane = lax.broadcasted_iota(jnp.int32, (HD, 512), 1) >> 6
    expand = (head == lane).astype(F32).astype(BF16)
    return jnp.dot(dt.astype(BF16), expand, preferred_element_type=F32)


def step_terms(dt, x, rate, bias):
    raw = spread_heads(dt) + bias
    step = jnp.maximum(raw, 0.0) + jnp.log1p(jnp.exp(-jnp.abs(raw)))
    return jnp.exp(-rate * step), step * x


def parent_rows(parents, me, carry, wide):
    folded = carry.astype(F32)
    wide[pl.ds(8, 4), 0:384] = folded[0:4]
    wide[pl.ds(8, 4), 384:768] = folded[4:8]
    wide[pl.ds(0, 4), :] = jnp.zeros((4, 768), F32)
    for s in range(4):
        way = parents[1, me * 4 + s] & 3
        wide[pl.ds(4 + s, 1), :] = wide[pl.ds(8 + way, 1), :]
    return wide[pl.ds(0, 8), :]


def stacked(ref, wide, lanes):
    wide[pl.ds(0, 4), 0:lanes] = ref[0].astype(F32)
    wide[pl.ds(4, 4), 0:lanes] = ref[1].astype(F32)
    return wide[pl.ds(0, 8), 0:lanes]


def mamba_body(parents, a_rate, dt_bias, skip, *refs):
    blocks = refs[:3]
    x_in, z_in, dt_in, b_in, c_in, gain, proj = refs[3:10]
    attn, keep, send, carry, held, wide = refs[10:16]
    me = lax.axis_index("replica")
    core = lax.axis_index("tensor") & 1
    for k in range(3):
        held[k] = blocks[k][...]
    one = held[came_by(me, source_of(parents, 0, me))].astype(F32)
    two = held[came_by(me, root_of(parents, me))].astype(F32)
    mine = held[came_by(me, source_of(parents, 1, me))][:, RESULT_LANES:]
    carry[...] = mine
    attn[0] = one[0:4, 0:1024].astype(BF16)
    attn[1] = two[4:8, 0:1024].astype(BF16)
    first = first_rows((8, 512))
    read = jnp.where(first, one[:, 1024:RESULT_LANES], two[:, 1024:RESULT_LANES])

    rate = per_head(a_rate)
    bias = per_head(dt_bias)
    earlier = parent_rows(parents, me, mine, wide)
    decay_p, drive_p = step_terms(earlier[:, 640:768], earlier[:, 0:512], rate, bias)
    b_p = earlier[:, 512:640]
    wide[pl.ds(0, 8), 0:HD] = jnp.zeros((8, HD), F32)
    stacked(dt_in, wide, 8)
    dt = wide[pl.ds(0, 8), 0:HD]
    x = stacked(x_in, wide, 512)
    z = stacked(z_in, wide, 512)
    b = stacked(b_in, wide, HD)
    c = stacked(c_in, wide, HD)
    decay, drive = step_terms(dt, x, rate, bias)
    inner = decay_p * read + drive_p * jnp.sum(b_p * c, axis=-1, keepdims=True)
    inner = jnp.where(first, read, inner)
    out = decay * inner + drive * jnp.sum(b * c, axis=-1, keepdims=True) + per_head(skip) * x
    gated = out * (z / (1.0 + jnp.exp(-z)))
    mean = jnp.mean(gated * gated, axis=-1, keepdims=True)
    normed = (gated * lax.rsqrt(mean + 1e-05) * gain[...]).astype(BF16)
    for y in range(4):
        for target, parity in ((send, 1 - core), (keep, core)):
            span = pl.ds(pl.multiple_of((2 * y + parity) * 512, 512), 512)
            part = jnp.dot(normed, proj[:, span], preferred_element_type=F32)
            target[y] = part.astype(BF16)


def core_sum_body(keep, came, *refs):
    outs, total = refs[:4], refs[4]
    y = lax.axis_index("tensor") >> 1
    total[...] = keep[...].astype(F32) + came[...].astype(F32)
    for k in range(4):
        outs[k][...] = total[(y + k) & 3].astype(BF16)


def last_sum_body(a, b, c, d, out):
    total = (a[...].astype(F32) + b[...].astype(F32)) + (c[...].astype(F32) + d[...].astype(F32))
    out[0] = total[0:4].astype(BF16)
    out[1] = total[4:8].astype(BF16)


def regroup_body(parents, came, _, out):
    for prompt in range(32):
        out[prompt] = came[root_of(parents, prompt)]


def advance_body(parents, a_rate, dt_bias, state, carry, x_in, dt_in, b_in, out, wide):
    me = lax.axis_index("replica")
    rate = per_head(a_rate)
    bias = per_head(dt_bias)
    earlier = parent_rows(parents, me, carry[...], wide)
    decay_p, drive_p = step_terms(earlier[:, 640:768], earlier[:, 0:512], rate, bias)
    b_p = earlier[:, 512:640]
    wide[pl.ds(0, 8), 0:HD] = jnp.zeros((8, HD), F32)
    stacked(dt_in, wide, 8)
    dt = wide[pl.ds(0, 8), 0:HD]
    x = stacked(x_in, wide, 512)
    b = stacked(b_in, wide, HD)
    decay, drive = step_terms(dt, x, rate, bias)
    columns_p = jnp.transpose(b_p)
    columns = jnp.transpose(b)
    source = source_of(parents, 1, me)
    for s in range(4):
        root = parents[0, source * 4 + (parents[1, me * 4 + s] & 3)] & 3
        r = 4 + s
        for i in range(8):
            rows = slice(i * 16, (i + 1) * 16)
            old = state[root * 8 + i].astype(F32)
            mid = decay_p[r : r + 1] * old + drive_p[r : r + 1] * columns_p[rows, r : r + 1]
            mid = mid.astype(BF16).astype(F32)
            new = decay[r : r + 1] * mid + drive[r : r + 1] * columns[rows, r : r + 1]
            out[s * 8 + i] = new.astype(BF16)


def along_x(array, k):
    return lax.ppermute(array, "replica", [(r, ((r + 8 * k) & 31)) for r in range(32)])


def along_z(array, k):
    return lax.ppermute(array, "replica", [(r, (r & 24) | ((r + k) & 7)) for r in range(32)])


def along_y(array, k):
    return lax.ppermute(array, "tensor", [(t, (t + 2 * k) & 7) for t in range(8)])


def across(array):
    return lax.ppermute(array, "tensor", [(t, t ^ 1) for t in range(8)])


def struct(shape, dtype=BF16):
    return jax.ShapeDtypeStruct(shape, dtype)


def per_device(
    ssm_state,
    kcache,
    vcache,
    lengths,
    parents,
    x_in,
    z_in,
    dt_in,
    b_in,
    c_in,
    q_in,
    kv_new,
    a_rate,
    dt_bias,
    skip,
    gain,
    out_proj,
):
    item, carry = call(
        pack_body,
        "pack",
        (struct((8, ITEM_LANES)), struct((8, CARRY_LANES))),
        [HBM] * 6,
        (VMEM,) * 2,
        [
            pltpu.VMEM((2, 4, 1024), BF16),
            pltpu.VMEM((2, 4, 2, 128), BF16),
            pltpu.VMEM((2, 4, 128), BF16),
            pltpu.VMEM((2, 4, 512), BF16),
            pltpu.VMEM((2, 4, 128), BF16),
            pltpu.VMEM((2, 4, 8), BF16),
            pltpu.VMEM((8, ITEM_LANES), F32),
            pltpu.SemaphoreType.DMA((6,)),
        ],
        limit=60,
    )(q_in, kv_new, c_in, x_in, b_in, dt_in)
    item, parents = lax.optimization_barrier((item, parents))
    table = call(table_body, "table", struct((8, 128), jnp.int32), [SMEM] * 2, SMEM)(
        parents, lengths
    )
    came_up, came_down = along_z(item, 3), along_z(item, 5)
    item, table, *staged = lax.optimization_barrier((item, table, kcache, vcache, ssm_state))
    bundle = call(
        bundle_body, "bundle", struct((3, 8, ITEM_LANES)), [VMEM] * 3, VMEM
    )(item, came_up, came_down)
    up, down = along_z(bundle, 1), along_z(bundle, 7)
    keys, values, state = call(
        stage_body,
        "stage",
        (struct((4, 1024, 128)), struct((4, 1024, 128)), struct((4, 128, 512))),
        [HBM] * 3,
        (VMEM,) * 3,
        [pltpu.SemaphoreType.DMA((3,))],
    )(*staged)
    bundle, keys, values, state = lax.optimization_barrier((bundle, keys, values, state))
    blocks = call(
        sort_out_body,
        "sort_out",
        (struct((8, ITEM_LANES)),) * 4,
        [SMEM] + [VMEM] * 3,
        (VMEM,) * 4,
        [pltpu.VMEM((8, 8, ITEM_LANES), BF16)],
    )(table, bundle, up, down)
    own_block, moving = lax.optimization_barrier((blocks[0], ssm_state))
    blocks = [own_block] + list(blocks[1:])
    came = lax.all_to_all(moving.reshape(32, 16, 512), "replica", 0, 0, tiled=True)
    blocks = [blocks[0]] + [along_x(blocks[k], k) for k in range(1, 4)]
    back = call(
        attend_body,
        "attend",
        struct((8, BACK_LANES)),
        [SMEM] + [VMEM] * 8,
        VMEM,
        [pltpu.VMEM((4, 8, ITEM_LANES), BF16)],
        flops=50000000000,
    )(table, *blocks, carry, keys, values, state)
    rows = call(
        bundle_back_body, "bundle_back", struct((4, 8, BACK_LANES)), [VMEM] * 4, VMEM
    )(back, *[along_x(back, k) for k in range(1, 4)])
    up, down = along_z(rows, 1), along_z(rows, 7)
    blocks = call(
        sort_back_body,
        "sort_back",
        (struct((8, BACK_LANES)),) * 3,
        [SMEM] + [VMEM] * 3,
        (VMEM,) * 3,
        [pltpu.VMEM((3, 4, 8, BACK_LANES), BF16)],
    )(table, rows, up, down)
    regrouped = call(
        regroup_body, "regroup", struct((32, 16, 512)), [SMEM, VMEM, HBM], VMEM
    )(table, came, rows)
    own_block, regrouped, weights = lax.optimization_barrier((blocks[0], regrouped, out_proj))
    weights = call(
        stage_body,
        "stage_proj",
        struct((512, 4096)),
        [HBM],
        VMEM,
        [pltpu.SemaphoreType.DMA((1,))],
    )(weights)
    arrived = lax.all_to_all(regrouped, "replica", 0, 0, tiled=True)
    blocks = [own_block, along_z(blocks[1], 3), along_z(blocks[2], 5)]
    attn_out, keep, send, carry = call(
        mamba_body,
        "mamba",
        (
            struct((2, 4, 1024)),
            struct((4, 8, 512)),
            struct((4, 8, 512)),
            struct((8, CARRY_LANES)),
        ),
        [SMEM] * 4 + [VMEM] * 10,
        (VMEM,) * 4,
        [
            pltpu.VMEM((3, 8, BACK_LANES), BF16),
            pltpu.VMEM((16, 768), F32),
        ],
        flops=50000000000,
    )(
        table, a_rate, dt_bias, skip, *blocks, x_in, z_in, dt_in, b_in, c_in,
        gain.reshape(1, 512), weights,
    )
    parts = call(
        core_sum_body,
        "core_sum",
        (struct((8, 512)),) * 4,
        [VMEM, VMEM],
        (VMEM,) * 4,
        [pltpu.VMEM((4, 8, 512), F32)],
    )(keep, across(send))
    final_state = call(
        advance_body,
        "advance",
        struct((32, 16, 512)),
        [SMEM] * 3 + [VMEM] * 5,
        VMEM,
        [pltpu.VMEM((16, 768), F32)],
    )(table, a_rate, dt_bias, arrived, carry, x_in, dt_in, b_in)
    own_part, final_state = lax.optimization_barrier((parts[0], final_state))
    mamba_out = call(last_sum_body, "last_sum", struct((2, 4, 512)), [VMEM] * 4, VMEM)(
        own_part, *[along_y(parts[k], k) for k in range(1, 4)]
    )
    return (final_state.reshape(4, 128, 512), mamba_out, attn_out)


def solution(mesh):
    return jax.shard_map(
        per_device,
        mesh=mesh,
        in_specs=(
            P("replica", None, "tensor"),
            P("replica", None, "tensor"),
            P("replica", None, "tensor"),
            P(),
            P(),
            P(None, "replica", "tensor"),
            P(None, "replica", "tensor"),
            P(None, "replica", "tensor"),
            P(None, "replica", None),
            P(None, "replica", None),
            P(None, "replica", "tensor"),
            P(None, "replica", None, "tensor"),
            P("tensor"),
            P("tensor"),
            P("tensor"),
            P("tensor"),
            P("tensor", None),
        ),
        out_specs=(
            P("replica", None, "tensor"),
            P(None, "replica", "tensor"),
            P(None, "replica", "tensor"),
        ),
        check_vma=False,
    )
```

time: 119 us -> 83 us (0.70); the launches traced: 117 us -> 82.4 us
  blocking collectives: 28.9 us -> 0 us
  starting transfers between devices: 45.9 us -> 41.8 us
  local copies, waits for them, and re-layouts: 11.9 us -> 8.85 us
  Pallas kernels: 10.5 us -> 12.4 us
    all_to_all x1 -> x0, blocking collectives: 28.9 us -> none  [per_device(): lax.all_to_all(ssm_state.reshape(32, 16, 512), 'replica', 0, 0, tiled=True)]
    ppermute x14 -> x8, starting transfers between devices: 30.6 us -> 16.2 us  [along_z(): lax.ppermute(array, 'replica', [(r, r & 24 | r + k & 7) for r in range(32)])]
    ppermute x3, waiting for transfers between devices: 4.86 us -> 0.01 us  [along_y(): return lax.ppermute(array, 'tensor', [(t, t + 2 * k & 7) for t in range(8)])]
    all_to_all x0 -> x1, starting transfers between devices: none -> 4.58 us  [per_device(): lax.all_to_all(moving.reshape(32, 16, 512), 'replica', 0, 0, tiled=True)]
    all_to_all x1, waiting for transfers between devices: 0.01 us -> 4.44 us  [per_device(): arrived = lax.all_to_all(regrouped, 'replica', 0, 0, tiled=True)]
    ppermute x14 -> x8, waiting for transfers between devices: 4.45 us -> 8.17 us  [along_z(): lax.ppermute(array, 'replica', [(r, r & 24 | r + k & 7) for r in range(32)])]
    ppermute x6, waiting for transfers between devices: 8.03 us -> 4.59 us  [along_x(): lax.ppermute(array, 'replica', [(r, r + 8 * k & 31) for r in range(32)])]
    unnamed x46 -> x34, local copies, waits for them, and re-layouts: 11.9 us -> 8.85 us
  transfers between devices with their start and end apart: 25 -> 20, of which waited for: 15 -> 8; matrix products, arithmetic and copies ran while one was open for 0% -> 0% of each run, Pallas kernels for 6% -> 12%
where the time goes in v2:
time: 83 us; the launch traced here: 82.4 us
  starting transfers between devices  41.8 us (50%)
  waiting for transfers between devices  18.4 us (22%)
  Pallas kernels  12.4 us (15%)
  local copies, waits for them, and re-layouts  8.85 us (11%)
  between operations  0.85 us (1%)
    ppermute x8, starting transfers between devices, along_z(): lax.ppermute(array, 'replica', [(r, r & 24 | r + k & 7) for r in range(32)])  16.2 us
    ppermute x6, starting transfers between devices, along_x(): lax.ppermute(array, 'replica', [(r, r + 8 * k & 31) for r in range(32)])  10.3 us
    unnamed x34, local copies, waits for them, and re-layouts  8.85 us
    ppermute x8, waiting for transfers between devices, along_z(): lax.ppermute(array, 'replica', [(r, r & 24 | r + k & 7) for r in range(32)])  8.17 us
    all_to_all x1, starting transfers between devices, per_device(): arrived = lax.all_to_all(regrouped, 'replica', 0, 0, tiled=True)  7.92 us
    ppermute x6, waiting for transfers between devices, along_x(): lax.ppermute(array, 'replica', [(r, r + 8 * k & 31) for r in range(32)])  4.59 us
    all_to_all x1, starting transfers between devices, per_device(): lax.all_to_all(moving.reshape(32, 16, 512), 'replica', 0, 0, tiled=True)  4.58 us
    all_to_all x1, waiting for transfers between devices, per_device(): arrived = lax.all_to_all(regrouped, 'replica', 0, 0, tiled=True)  4.44 us
  transfers between devices with their start and end apart: 20, of which 8 were waited for; matrix products, arithmetic and copies ran while one was open for 0% of the time, Pallas kernels for 12%

profile of v2, /device:TPU:56, one launch (start us, length us, event | category | flops | bytes accessed | tf_op | source)
XLA Modules:
  0.0 82.4 jit_solution(17672550194012443219)
XLA Ops:
  0.6 1.4 %pack.1 = (bf16[8,1408]{1,0:T(8,128)(2,1)}, bf16[8,384]{1,0:T(8,128)(2,1)}) custom-call(bf16[2,4,1024]{2,1,0:T(4,128)(2,1)} %refs_0_.1, bf16[2,4,2,128]{3,2,1,0:T(2,128)(2,1)} %refs_1_.1, bf16[2,4,128]{2,1,0:T(4,128)(2,1)} %refs_7_.1, bf16[2,4,512]{2,1,0:T(4,128)(2,1)} %x_in.1, bf16[2,4,128]{2,1,0:T(4,128)(2,1)} %b_in.1, bf16[2,4,8]{2,1,0:T(4,128)(2,1)} %dt_in.1), custom_call_target="tpu_custom_call" | custom-call | flops 1000000 | tf_op jit(solution)/shard_map/pack/pallas_call | solution.py:398
  2.1 5.9 %collective-permute-start.1 = (bf16[8,1408]{1,0:T(8,128)(2,1)}, bf16[8,1408]{1,0:T(8,128)(2,1)S(1)}, u32[]{:S(2)}, u32[]{:S(2)}) collective-permute-start(bf16[8,1408]{1,0:T(8,128)(2,1)} %get-tuple-element.45.own), channel_id=1, source_target_pairs={{0,40},{8,48},{16,56},{24,0},{32,8},{40,16},{48,24},{56,32},{64,10... | collective-permute-start | bytes 67592 | tf_op jit(solution)/shard_map/ppermute | solution.py:364
  8.0 0.1 collective-permute-start
  8.1 0.7 copy-done.9
  8.8 0.7 copy-done.12
  9.4 1.5 %table.1.parents = s32[8,128]{1,0:T(8,128)S(1)} custom-call(s32[2,128]{1,0:T(2,128)S(1)} %copy-done.9, s32[32]{0:T(128)S(1)} %copy-done.12), custom_call_target="tpu_custom_call" | custom-call | flops 1000000 | tf_op jit(solution)/shard_map/table/pallas_call | solution.py:417
  11.0 0.0 collective-permute-done.1.down
  11.0 4.0 %collective-permute-done.up = bf16[8,1408]{1,0:T(8,128)(2,1)S(1)} collective-permute-done((bf16[8,1408]{1,0:T(8,128)(2,1)}, bf16[8,1408]{1,0:T(8,128)(2,1)S(1)}, u32[]{:S(2)}, u32[]{:S(2)}) %collective-permute-start) | collective-permute-done | bytes 22560 | tf_op jit(solution)/shard_map/ppermute | solution.py:364
  15.0 0.7 copy-done.5
  15.8 1.0 %collective-permute-start.3 = (bf16[3,8,1408]{2,1,0:T(8,128)(2,1)S(1)}, bf16[3,8,1408]{2,1,0:T(8,128)(2,1)S(1)}, u32[]{:S(2)}, u32[]{:S(2)}) collective-permute-start(bf16[3,8,1408]{2,1,0:T(8,128)(2,1)S(1)} %bundle.1.own), channel_id=1, source_target_pairs={{0,56},{8,0},{16,8},{24,16},{32,24},{40,32},{48,40},{56,48},{64,12... | collective-permute-start | bytes 202760 | tf_op jit(solution)/shard_map/ppermute | solution.py:364
  16.8 1.0 %collective-permute-start.2 = (bf16[3,8,1408]{2,1,0:T(8,128)(2,1)S(1)}, bf16[3,8,1408]{2,1,0:T(8,128)(2,1)S(1)}, u32[]{:S(2)}, u32[]{:S(2)}) collective-permute-start(bf16[3,8,1408]{2,1,0:T(8,128)(2,1)S(1)} %bundle.1.own), channel_id=1, source_target_pairs={{0,8},{8,16},{16,24},{24,32},{32,40},{40,48},{48,56},{56,0},{64,72... | collective-permute-start | bytes 202760 | tf_op jit(solution)/shard_map/ppermute | solution.py:364
  17.8 1.0 %copy-done.1 = bf16[4,128,512]{2,1,0:T(8,128)(2,1)S(1)} copy-done((bf16[4,128,512]{2,1,0:T(8,128)(2,1)S(1)}, bf16[4,128,512]{2,1,0:T(8,128)(2,1)}, u32[]{:S(2)}) %copy-start.1) | copy-done | bytes 524312
  18.8 1.2 %copy-done.2 = bf16[4,1024,128]{2,1,0:T(8,128)(2,1)S(1)} copy-done((bf16[4,1024,128]{2,1,0:T(8,128)(2,1)S(1)}, bf16[4,1024,128]{2,1,0:T(8,128)(2,1)}, u32[]{:S(2)}) %copy-start.2) | copy-done | bytes 1048600
  20.1 1.2 %copy-done.3 = bf16[4,1024,128]{2,1,0:T(8,128)(2,1)S(1)} copy-done((bf16[4,1024,128]{2,1,0:T(8,128)(2,1)S(1)}, bf16[4,1024,128]{2,1,0:T(8,128)(2,1)}, u32[]{:S(2)}) %copy-start.3) | copy-done | bytes 1048600
  21.3 0.2 stage.1
  21.5 0.0 collective-permute-done.3.down
  21.5 0.0 collective-permute-done.2.up
  21.5 0.6 sort_out.1
  22.2 1.6 %collective-permute-start.4 = (bf16[8,1408]{1,0:T(8,128)(2,1)S(1)}, bf16[8,1408]{1,0:T(8,128)(2,1)S(1)}, u32[]{:S(2)}, u32[]{:S(2)}) collective-permute-start(bf16[8,1408]{1,0:T(8,128)(2,1)S(1)} %get-tuple-element.55), channel_id=1, source_target_pairs={{0,64},{8,72},{16,80},{24,88},{32,96},{40,104},{48,112},{56,120},{... | collective-permute-start | bytes 67592 | tf_op jit(solution)/shard_map/ppermute | solution.py:360
  23.7 2.7 %collective-permute-start.5 = (bf16[8,1408]{1,0:T(8,128)(2,1)S(1)}, bf16[8,1408]{1,0:T(8,128)(2,1)S(1)}, u32[]{:S(2)}, u32[]{:S(2)}) collective-permute-start(bf16[8,1408]{1,0:T(8,128)(2,1)S(1)} %get-tuple-element.56), channel_id=1, source_target_pairs={{0,128},{8,136},{16,144},{24,152},{32,160},{40,168},{48,176},{56,1... | collective-permute-start | bytes 67592 | tf_op jit(solution)/shard_map/ppermute | solution.py:360
  26.5 1.4 %collective-permute-start.6 = (bf16[8,1408]{1,0:T(8,128)(2,1)S(1)}, bf16[8,1408]{1,0:T(8,128)(2,1)S(1)}, u32[]{:S(2)}, u32[]{:S(2)}) collective-permute-start(bf16[8,1408]{1,0:T(8,128)(2,1)S(1)} %get-tuple-element.57), channel_id=1, source_target_pairs={{0,192},{8,200},{16,208},{24,216},{32,224},{40,232},{48,240},{56,2... | collective-permute-start | bytes 67592 | tf_op jit(solution)/shard_map/ppermute | solution.py:360
  27.9 4.6 %all-to-all-start = ((bf16[32,16,512]{2,1,0:T(8,128)(2,1)}), bf16[32,16,512]{2,1,0:T(8,128)(2,1)S(1)}, u32[]{:S(2)}, u32[]{:S(2)}) async-start(bf16[32,16,512]{2,1,0:T(8,128)(2,1)} %bitcast.3), calls=%async_computation | async-start | bytes 1048576 | tf_op jit(solution)/shard_map/all_to_all | solution.py:445
  32.5 0.0 collective-permute-done.4.refs_1_
  32.5 0.0 collective-permute-done.5.refs_2_
  32.5 0.0 copy-start.14
  32.5 0.7 copy-done.14
  33.2 1.5 %attend.1.own = bf16[8,1920]{1,0:T(8,128)(2,1)S(1)} custom-call(s32[8,128]{1,0:T(8,128)S(1)} %table.1.parents, bf16[8,1408]{1,0:T(8,128)(2,1)S(1)} %get-tuple-element.54.refs_0_, bf16[8,1408]{1,0:T(8,128)(2,1)S(1)} %collective-permute-done.4.refs_1_, bf16[8,1408]{1,0:T(8,128)(2,1)S(1)} %collective-permute-done.5.refs_2_, ...), custom_call_target="tpu_custom_call" | custom-call | flops 49999998976 | tf_op jit(solution)/shard_map/attend/pallas_call | solution.py:447
  34.8 2.9 %collective-permute-start.9 = (bf16[8,1920]{1,0:T(8,128)(2,1)S(1)}, bf16[8,1920]{1,0:T(8,128)(2,1)S(1)}, u32[]{:S(2)}, u32[]{:S(2)}) collective-permute-start(bf16[8,1920]{1,0:T(8,128)(2,1)S(1)} %attend.1.own), channel_id=1, source_target_pairs={{0,192},{8,200},{16,208},{24,216},{32,224},{40,232},{48,240},{56,2... | collective-permute-start | bytes 92168 | tf_op jit(solution)/shard_map/ppermute | solution.py:360
  37.6 0.7 collective-permute-start.8
  38.4 0.9 %collective-permute-start.7 = (bf16[8,1920]{1,0:T(8,128)(2,1)S(1)}, bf16[8,1920]{1,0:T(8,128)(2,1)S(1)}, u32[]{:S(2)}, u32[]{:S(2)}) collective-permute-start(bf16[8,1920]{1,0:T(8,128)(2,1)S(1)} %attend.1.own), channel_id=1, source_target_pairs={{0,64},{8,72},{16,80},{24,88},{32,96},{40,104},{48,112},{56,120},{... | collective-permute-start | bytes 92168 | tf_op jit(solution)/shard_map/ppermute | solution.py:360
  39.3 0.5 collective-permute-done.9.three
  39.8 3.5 %collective-permute-done.8.two = bf16[8,1920]{1,0:T(8,128)(2,1)S(1)} collective-permute-done((bf16[8,1920]{1,0:T(8,128)(2,1)S(1)}, bf16[8,1920]{1,0:T(8,128)(2,1)S(1)}, u32[]{:S(2)}, u32[]{:S(2)}) %collective-permute-start.8) | collective-permute-done | bytes 30752 | tf_op jit(solution)/shard_map/ppermute | solution.py:360
  43.3 0.6 collective-permute-done.7.one
  43.9 0.5 collective-permute-start.11
  44.4 1.6 %collective-permute-start.10 = (bf16[4,8,1920]{2,1,0:T(8,128)(2,1)S(1)}, bf16[4,8,1920]{2,1,0:T(8,128)(2,1)S(1)}, u32[]{:S(2)}, u32[]{:S(2)}) collective-permute-start(bf16[4,8,1920]{2,1,0:T(8,128)(2,1)S(1)} %bundle_back.1.own._), channel_id=1, source_target_pairs={{0,8},{8,16},{16,24},{24,32},{32,40},{40,48},{48,56},{56,0},{64,72... | collective-permute-start | bytes 368648 | tf_op jit(solution)/shard_map/ppermute | solution.py:364
  46.0 2.9 %collective-permute-done.11.down = bf16[4,8,1920]{2,1,0:T(8,128)(2,1)S(1)} collective-permute-done((bf16[4,8,1920]{2,1,0:T(8,128)(2,1)S(1)}, bf16[4,8,1920]{2,1,0:T(8,128)(2,1)S(1)}, u32[]{:S(2)}, u32[]{:S(2)}) %collective-permute-start.11) | collective-permute-done | bytes 122912 | tf_op jit(solution)/shard_map/ppermute | solution.py:364
  48.8 1.3 %collective-permute-done.10.up = bf16[4,8,1920]{2,1,0:T(8,128)(2,1)S(1)} collective-permute-done((bf16[4,8,1920]{2,1,0:T(8,128)(2,1)S(1)}, bf16[4,8,1920]{2,1,0:T(8,128)(2,1)S(1)}, u32[]{:S(2)}, u32[]{:S(2)}) %collective-permute-start.10) | collective-permute-done | bytes 122912 | tf_op jit(solution)/shard_map/ppermute | solution.py:364
  50.1 0.7 sort_back.1
  50.8 6.0 %collective-permute-start.12 = (bf16[8,1920]{1,0:T(8,128)(2,1)S(1)}, bf16[8,1920]{1,0:T(8,128)(2,1)S(1)}, u32[]{:S(2)}, u32[]{:S(2)}) collective-permute-start(bf16[8,1920]{1,0:T(8,128)(2,1)S(1)} %get-tuple-element.65), channel_id=1, source_target_pairs={{0,24},{8,32},{16,40},{24,48},{32,56},{40,0},{48,8},{56,16},{64,88... | collective-permute-start | bytes 92168 | tf_op jit(solution)/shard_map/ppermute | solution.py:364
  56.8 0.0 collective-permute-start.13
  56.8 0.0 all-to-all-done.came
  56.8 1.5 %regroup.1 = bf16[32,16,512]{2,1,0:T(8,128)(2,1)} custom-call(s32[8,128]{1,0:T(8,128)S(1)} %table.1.parents, bf16[32,16,512]{2,1,0:T(8,128)(2,1)S(1)} %all-to-all-done.came, bf16[4,8,1920]{2,1,0:T(8,128)(2,1)S(1)} %bundle_back.1.own._), custom_call_target="tpu_custom_call" | custom-call | flops 1000000 | tf_op jit(solution)/shard_map/regroup/pallas_call | solution.py:468
  58.3 7.9 %all-to-all-start.1 = ((bf16[32,16,512]{2,1,0:T(8,128)(2,1)}), bf16[32,16,512]{2,1,0:T(8,128)(2,1)S(1)}, u32[]{:S(2)}, u32[]{:S(2)}) async-start(bf16[32,16,512]{2,1,0:T(8,128)(2,1)} %regroup.1), calls=%async_computation.1 | async-start | bytes 1048576 | tf_op jit(solution)/shard_map/all_to_all | solution.py:480
  66.2 0.0 copy-start
  66.2 2.2 %copy-done = bf16[512,4096]{1,0:T(8,128)(2,1)S(1)} copy-done((bf16[512,4096]{1,0:T(8,128)(2,1)S(1)}, bf16[512,4096]{1,0:T(8,128)(2,1)}, u32[]{:S(2)}) %copy-start) | copy-done | bytes 4194328
  68.4 0.0 copy-start.10
  68.4 0.0 copy-start.11
  68.4 0.0 copy-start.13
  68.4 0.0 copy-start.15
  68.4 0.0 copy-start.16
  68.5 0.3 stage_proj.1.refs_9_
  68.8 0.0 collective-permute-done.13.refs_2_
  68.8 0.3 copy-done.4
  69.1 0.0 copy-done.7
  69.1 0.0 copy-done.8
  69.1 0.1 copy-done.13
  69.2 2.1 %mamba.1 = (bf16[2,4,1024]{2,1,0:T(4,128)(2,1)}, bf16[4,8,512]{2,1,0:T(8,128)(2,1)S(1)}, bf16[4,8,512]{2,1,0:T(8,128)(2,1)S(1)}, bf16[8,384]{1,0:T(8,128)(2,1)S(1)}) custom-call(s32[8,128]{1,0:T(8,128)S(1)} %table.1.parents, f32[8]{0:T(128)S(1)} %copy-done.10, f32[8]{0:T(128)S(1)} %copy-done.11, f32[8]{0:T(128)S(1)} %copy-done.16, ...), custom_call_target="tpu_custom_call" | custom-call | flops 49999998976 | tf_op jit(solution)/shard_map/mamba/pallas_call | solution.py:482
  71.2 0.0 collective-permute-start.14
  71.3 1.2 %collective-permute-done.14.came = bf16[4,8,512]{2,1,0:T(8,128)(2,1)S(1)} collective-permute-done((bf16[4,8,512]{2,1,0:T(8,128)(2,1)S(1)}, bf16[4,8,512]{2,1,0:T(8,128)(2,1)S(1)}, u32[]{:S(2)}, u32[]{:S(2)}) %collective-permute-start.14) | collective-permute-done | bytes 32800 | tf_op jit(solution)/shard_map/ppermute | solution.py:372
  72.5 0.3 collective-permute-start.15
  72.8 2.6 %collective-permute-start.16 = (bf16[8,512]{1,0:T(8,128)(2,1)S(1)}, bf16[8,512]{1,0:T(8,128)(2,1)S(1)}, u32[]{:S(2)}, u32[]{:S(2)}) collective-permute-start(bf16[8,512]{1,0:T(8,128)(2,1)S(1)} %get-tuple-element.76), channel_id=1, source_target_pairs={{0,4},{1,5},{2,6},{3,7},{4,0},{5,1},{6,2},{7,3},{8,12},{9,13},{10,... | collective-permute-start | bytes 24584 | tf_op jit(solution)/shard_map/ppermute | solution.py:368
  75.4 4.4 %all-to-all-done.1.state = bf16[32,16,512]{2,1,0:T(8,128)(2,1)S(1)} async-done(((bf16[32,16,512]{2,1,0:T(8,128)(2,1)}), bf16[32,16,512]{2,1,0:T(8,128)(2,1)S(1)}, u32[]{:S(2)}, u32[]{:S(2)}) %all-to-all-start.1) | async-done | bytes 524320 | tf_op jit(solution)/shard_map/all_to_all | solution.py:480
  79.8 1.9 %advance.1 = bf16[32,16,512]{2,1,0:T(8,128)(2,1)} custom-call(s32[8,128]{1,0:T(8,128)S(1)} %table.1.parents, f32[8]{0:T(128)S(1)} %copy-done.10, f32[8]{0:T(128)S(1)} %copy-done.11, bf16[32,16,512]{2,1,0:T(8,128)(2,1)S(1)} %all-to-all-done.1.state, bf16[8,384]{1,0:T(8,128)(2,1)S(1)} %get-tuple-element.72.carry, bf16[2,4,512]{2,1,0:T(4,128)(2,1)S(1)} %copy-done.4, ...), custom_call_target="tpu_custom_call" | custom-call | flops 1000000 | tf_op jit(solution)/shard_map/advance/pallas_call | solution.py:510
  81.8 0.6 last_sum.1
  (24 shorter events, 0.1 us)
Async XLA Ops:
  2.1 8.9 %collective-permute-start.1 = (bf16[8,1408]{1,0:T(8,128)(2,1)}, bf16[8,1408]{1,0:T(8,128)(2,1)S(1)}, u32[]{:S(2)}, u32[]{:S(2)}) collective-permute-start(bf16[8,1408]{1,0:T(8,128)(2,1)} %get-tuple-element.45.own), channel_id=1, source_target_pairs={{0,40},{8,48},{16,56},{24,0},{32,8},{40,16},{48,24},{56,32},{64,10... | collective-permute-start | bytes 67592 | tf_op jit(solution)/shard_map/ppermute | solution.py:364
  8.0 7.0 %collective-permute-start = (bf16[8,1408]{1,0:T(8,128)(2,1)}, bf16[8,1408]{1,0:T(8,128)(2,1)S(1)}, u32[]{:S(2)}, u32[]{:S(2)}) collective-permute-start(bf16[8,1408]{1,0:T(8,128)(2,1)} %get-tuple-element.45.own), channel_id=1, source_target_pairs={{0,24},{8,32},{16,40},{24,48},{32,56},{40,0},{48,8},{56,16},{64,88... | collective-permute-start | bytes 67592 | tf_op jit(solution)/shard_map/ppermute | solution.py:364
  8.1 0.7 copy-start.9
  8.8 0.7 copy-start.12
  15.0 0.7 copy-start.5
  15.8 5.7 %collective-permute-start.3 = (bf16[3,8,1408]{2,1,0:T(8,128)(2,1)S(1)}, bf16[3,8,1408]{2,1,0:T(8,128)(2,1)S(1)}, u32[]{:S(2)}, u32[]{:S(2)}) collective-permute-start(bf16[3,8,1408]{2,1,0:T(8,128)(2,1)S(1)} %bundle.1.own), channel_id=1, source_target_pairs={{0,56},{8,0},{16,8},{24,16},{32,24},{40,32},{48,40},{56,48},{64,12... | collective-permute-start | bytes 202760 | tf_op jit(solution)/shard_map/ppermute | solution.py:364
  16.8 4.7 %collective-permute-start.2 = (bf16[3,8,1408]{2,1,0:T(8,128)(2,1)S(1)}, bf16[3,8,1408]{2,1,0:T(8,128)(2,1)S(1)}, u32[]{:S(2)}, u32[]{:S(2)}) collective-permute-start(bf16[3,8,1408]{2,1,0:T(8,128)(2,1)S(1)} %bundle.1.own), channel_id=1, source_target_pairs={{0,8},{8,16},{16,24},{24,32},{32,40},{40,48},{48,56},{56,0},{64,72... | collective-permute-start | bytes 202760 | tf_op jit(solution)/shard_map/ppermute | solution.py:364
  17.8 1.0 %copy-start.1 = (bf16[4,128,512]{2,1,0:T(8,128)(2,1)S(1)}, bf16[4,128,512]{2,1,0:T(8,128)(2,1)}, u32[]{:S(2)}) copy-start(bf16[4,128,512]{2,1,0:T(8,128)(2,1)} %refs_2_.2) | copy-start | bytes 1572868
  18.8 1.2 %copy-start.2 = (bf16[4,1024,128]{2,1,0:T(8,128)(2,1)S(1)}, bf16[4,1024,128]{2,1,0:T(8,128)(2,1)}, u32[]{:S(2)}) copy-start(bf16[4,1024,128]{2,1,0:T(8,128)(2,1)} %refs_0_.2) | copy-start | bytes 3145732
  20.1 1.2 %copy-start.3 = (bf16[4,1024,128]{2,1,0:T(8,128)(2,1)S(1)}, bf16[4,1024,128]{2,1,0:T(8,128)(2,1)}, u32[]{:S(2)}) copy-start(bf16[4,1024,128]{2,1,0:T(8,128)(2,1)} %refs_1_.2) | copy-start | bytes 3145732
  22.2 10.3 %collective-permute-start.4 = (bf16[8,1408]{1,0:T(8,128)(2,1)S(1)}, bf16[8,1408]{1,0:T(8,128)(2,1)S(1)}, u32[]{:S(2)}, u32[]{:S(2)}) collective-permute-start(bf16[8,1408]{1,0:T(8,128)(2,1)S(1)} %get-tuple-element.55), channel_id=1, source_target_pairs={{0,64},{8,72},{16,80},{24,88},{32,96},{40,104},{48,112},{56,120},{... | collective-permute-start | bytes 67592 | tf_op jit(solution)/shard_map/ppermute | solution.py:360
  23.7 8.8 %collective-permute-start.5 = (bf16[8,1408]{1,0:T(8,128)(2,1)S(1)}, bf16[8,1408]{1,0:T(8,128)(2,1)S(1)}, u32[]{:S(2)}, u32[]{:S(2)}) collective-permute-start(bf16[8,1408]{1,0:T(8,128)(2,1)S(1)} %get-tuple-element.56), channel_id=1, source_target_pairs={{0,128},{8,136},{16,144},{24,152},{32,160},{40,168},{48,176},{56,1... | collective-permute-start | bytes 67592 | tf_op jit(solution)/shard_map/ppermute | solution.py:360
  26.5 6.0 %collective-permute-start.6 = (bf16[8,1408]{1,0:T(8,128)(2,1)S(1)}, bf16[8,1408]{1,0:T(8,128)(2,1)S(1)}, u32[]{:S(2)}, u32[]{:S(2)}) collective-permute-start(bf16[8,1408]{1,0:T(8,128)(2,1)S(1)} %get-tuple-element.57), channel_id=1, source_target_pairs={{0,192},{8,200},{16,208},{24,216},{32,224},{40,232},{48,240},{56,2... | collective-permute-start | bytes 67592 | tf_op jit(solution)/shard_map/ppermute | solution.py:360
  27.9 28.9 %all-to-all-start = ((bf16[32,16,512]{2,1,0:T(8,128)(2,1)}), bf16[32,16,512]{2,1,0:T(8,128)(2,1)S(1)}, u32[]{:S(2)}, u32[]{:S(2)}) async-start(bf16[32,16,512]{2,1,0:T(8,128)(2,1)} %bitcast.3), calls=%async_computation | async-start | bytes 1048576 | tf_op jit(solution)/shard_map/all_to_all | solution.py:445
  32.5 0.7 copy-start.14
  34.8 5.0 %collective-permute-start.9 = (bf16[8,1920]{1,0:T(8,128)(2,1)S(1)}, bf16[8,1920]{1,0:T(8,128)(2,1)S(1)}, u32[]{:S(2)}, u32[]{:S(2)}) collective-permute-start(bf16[8,1920]{1,0:T(8,128)(2,1)S(1)} %attend.1.own), channel_id=1, source_target_pairs={{0,192},{8,200},{16,208},{24,216},{32,224},{40,232},{48,240},{56,2... | collective-permute-start | bytes 92168 | tf_op jit(solution)/shard_map/ppermute | solution.py:360
  37.6 5.6 %collective-permute-start.8 = (bf16[8,1920]{1,0:T(8,128)(2,1)S(1)}, bf16[8,1920]{1,0:T(8,128)(2,1)S(1)}, u32[]{:S(2)}, u32[]{:S(2)}) collective-permute-start(bf16[8,1920]{1,0:T(8,128)(2,1)S(1)} %attend.1.own), channel_id=1, source_target_pairs={{0,128},{8,136},{16,144},{24,152},{32,160},{40,168},{48,176},{56,1... | collective-permute-start | bytes 92168 | tf_op jit(solution)/shard_map/ppermute | solution.py:360
  38.4 5.5 %collective-permute-start.7 = (bf16[8,1920]{1,0:T(8,128)(2,1)S(1)}, bf16[8,1920]{1,0:T(8,128)(2,1)S(1)}, u32[]{:S(2)}, u32[]{:S(2)}) collective-permute-start(bf16[8,1920]{1,0:T(8,128)(2,1)S(1)} %attend.1.own), channel_id=1, source_target_pairs={{0,64},{8,72},{16,80},{24,88},{32,96},{40,104},{48,112},{56,120},{... | collective-permute-start | bytes 92168 | tf_op jit(solution)/shard_map/ppermute | solution.py:360
  43.9 5.0 %collective-permute-start.11 = (bf16[4,8,1920]{2,1,0:T(8,128)(2,1)S(1)}, bf16[4,8,1920]{2,1,0:T(8,128)(2,1)S(1)}, u32[]{:S(2)}, u32[]{:S(2)}) collective-permute-start(bf16[4,8,1920]{2,1,0:T(8,128)(2,1)S(1)} %bundle_back.1.own._), channel_id=1, source_target_pairs={{0,56},{8,0},{16,8},{24,16},{32,24},{40,32},{48,40},{56,48},{64,12... | collective-permute-start | bytes 368648 | tf_op jit(solution)/shard_map/ppermute | solution.py:364
  44.4 5.7 %collective-permute-start.10 = (bf16[4,8,1920]{2,1,0:T(8,128)(2,1)S(1)}, bf16[4,8,1920]{2,1,0:T(8,128)(2,1)S(1)}, u32[]{:S(2)}, u32[]{:S(2)}) collective-permute-start(bf16[4,8,1920]{2,1,0:T(8,128)(2,1)S(1)} %bundle_back.1.own._), channel_id=1, source_target_pairs={{0,8},{8,16},{16,24},{24,32},{32,40},{40,48},{48,56},{56,0},{64,72... | collective-permute-start | bytes 368648 | tf_op jit(solution)/shard_map/ppermute | solution.py:364
  50.8 18.0 %collective-permute-start.12 = (bf16[8,1920]{1,0:T(8,128)(2,1)S(1)}, bf16[8,1920]{1,0:T(8,128)(2,1)S(1)}, u32[]{:S(2)}, u32[]{:S(2)}) collective-permute-start(bf16[8,1920]{1,0:T(8,128)(2,1)S(1)} %get-tuple-element.65), channel_id=1, source_target_pairs={{0,24},{8,32},{16,40},{24,48},{32,56},{40,0},{48,8},{56,16},{64,88... | collective-permute-start | bytes 92168 | tf_op jit(solution)/shard_map/ppermute | solution.py:364
  56.8 12.0 %collective-permute-start.13 = (bf16[8,1920]{1,0:T(8,128)(2,1)S(1)}, bf16[8,1920]{1,0:T(8,128)(2,1)S(1)}, u32[]{:S(2)}, u32[]{:S(2)}) collective-permute-start(bf16[8,1920]{1,0:T(8,128)(2,1)S(1)} %get-tuple-element.66), channel_id=1, source_target_pairs={{0,40},{8,48},{16,56},{24,0},{32,8},{40,16},{48,24},{56,32},{64,10... | collective-permute-start | bytes 92168 | tf_op jit(solution)/shard_map/ppermute | solution.py:364
  58.3 21.5 %all-to-all-start.1 = ((bf16[32,16,512]{2,1,0:T(8,128)(2,1)}), bf16[32,16,512]{2,1,0:T(8,128)(2,1)S(1)}, u32[]{:S(2)}, u32[]{:S(2)}) async-start(bf16[32,16,512]{2,1,0:T(8,128)(2,1)} %regroup.1), calls=%async_computation.1 | async-start | bytes 1048576 | tf_op jit(solution)/shard_map/all_to_all | solution.py:480
  66.2 2.2 %copy-start = (bf16[512,4096]{1,0:T(8,128)(2,1)S(1)}, bf16[512,4096]{1,0:T(8,128)(2,1)}, u32[]{:S(2)}) copy-start(bf16[512,4096]{1,0:T(8,128)(2,1)} %refs_0_.3) | copy-start | bytes 12582916
  68.4 0.7 copy-start.4
  68.4 0.7 copy-start.6
  68.4 0.7 copy-start.7
  68.4 0.7 copy-start.8
  68.4 0.7 copy-start.10
  68.4 0.7 copy-start.11
  68.4 0.8 copy-start.13
  68.4 0.7 copy-start.15
  68.4 0.7 copy-start.16
  71.2 1.2 %collective-permute-start.14 = (bf16[4,8,512]{2,1,0:T(8,128)(2,1)S(1)}, bf16[4,8,512]{2,1,0:T(8,128)(2,1)S(1)}, u32[]{:S(2)}, u32[]{:S(2)}) collective-permute-start(bf16[4,8,512]{2,1,0:T(8,128)(2,1)S(1)} %get-tuple-element.69), channel_id=1, source_target_pairs={{0,1},{1,0},{2,3},{3,2},{4,5},{5,4},{6,7},{7,6},{8,9},{9,8},{10,11... | collective-permute-start | bytes 98312 | tf_op jit(solution)/shard_map/ppermute | solution.py:372
  72.5 9.3 %collective-permute-start.15 = (bf16[8,512]{1,0:T(8,128)(2,1)S(1)}, bf16[8,512]{1,0:T(8,128)(2,1)S(1)}, u32[]{:S(2)}, u32[]{:S(2)}) collective-permute-start(bf16[8,512]{1,0:T(8,128)(2,1)S(1)} %get-tuple-element.75), channel_id=1, source_target_pairs={{0,2},{1,3},{2,4},{3,5},{4,6},{5,7},{6,0},{7,1},{8,10},{9,11},{10,... | collective-permute-start | bytes 24584 | tf_op jit(solution)/shard_map/ppermute | solution.py:368
  72.8 9.0 %collective-permute-start.16 = (bf16[8,512]{1,0:T(8,128)(2,1)S(1)}, bf16[8,512]{1,0:T(8,128)(2,1)S(1)}, u32[]{:S(2)}, u32[]{:S(2)}) collective-permute-start(bf16[8,512]{1,0:T(8,128)(2,1)S(1)} %get-tuple-element.76), channel_id=1, source_target_pairs={{0,4},{1,5},{2,6},{3,7},{4,0},{5,1},{6,2},{7,3},{8,12},{9,13},{10,... | collective-permute-start | bytes 24584 | tf_op jit(solution)/shard_map/ppermute | solution.py:368
  75.4 6.4 %collective-permute-start.17 = (bf16[8,512]{1,0:T(8,128)(2,1)S(1)}, bf16[8,512]{1,0:T(8,128)(2,1)S(1)}, u32[]{:S(2)}, u32[]{:S(2)}) collective-permute-start(bf16[8,512]{1,0:T(8,128)(2,1)S(1)} %get-tuple-element.77), channel_id=1, source_target_pairs={{0,6},{1,7},{2,0},{3,1},{4,2},{5,3},{6,4},{7,5},{8,14},{9,15},{10,... | collective-permute-start | bytes 24584 | tf_op jit(solution)/shard_map/ppermute | solution.py:368

commit v3 on v2

--- a/solution.py
+++ b/solution.py
@@ -10,10 +10,10 @@
 F32 = jnp.float32
 BF16 = jnp.bfloat16
 HD = 128
-ITEM_LANES = 1408
-RESULT_LANES = 1536
+STEP_LANES = 1408
 CARRY_LANES = 384
-BACK_LANES = RESULT_LANES + CARRY_LANES
+ITEM_LANES = STEP_LANES + CARRY_LANES
+BACK_LANES = 1536
 MASKED = -1e30
 MIB = 1024 * 1024
 
@@ -22,7 +22,7 @@
 HBM = pl.BlockSpec(memory_space=pltpu.HBM)
 
 
-def call(body, name, out_shape, in_specs, out_specs, scratch=(), flops=1000000, limit=32):
+def call(body, name, out_shape, in_specs, out_specs, scratch=(), flops=1000000, limit=16):
     return pl.pallas_call(
         body,
         name=name,
@@ -51,9 +51,10 @@
 
 
 def pack_body(*refs):
-    sources, (item, carry), wide, sems = refs[:6], refs[6:8], refs[14], refs[15]
-    q, kv, c, x, b, dt = refs[8:14]
-    copies = fetch(list(zip(sources, refs[8:14])), sems)
+    sources, item, wide, sems = refs[:6], refs[6], refs[13], refs[14]
+    q, kv, c, x, b, dt = refs[7:13]
+    copies = fetch(list(zip(sources, refs[7:13])), sems)
+    wide[:, STEP_LANES:] = jnp.zeros((8, CARRY_LANES), F32)
     for copy in copies:
         copy.wait()
     for t in range(2):
@@ -64,14 +65,12 @@
             wide[pl.ds(4 * t + s, 1), 1024:1152] = pair[0:1]
             wide[pl.ds(4 * t + s, 1), 1152:1280] = pair[1:2]
         wide[rows, 1280:1408] = c[t].astype(F32)
+    x0 = x[0].astype(F32)
+    wide[pl.ds(0, 4), 1408:1792] = x0[:, 0:384]
+    wide[pl.ds(4, 4), 1408:1536] = x0[:, 384:512]
+    wide[pl.ds(4, 4), 1536:1664] = b[0].astype(F32)
+    wide[pl.ds(4, 4), 1664:1672] = dt[0].astype(F32)
     item[...] = wide[...].astype(BF16)
-    wide[:, 0:CARRY_LANES] = jnp.zeros((8, CARRY_LANES), F32)
-    x0 = x[0].astype(F32)
-    wide[pl.ds(0, 4), 0:384] = x0[:, 0:384]
-    wide[pl.ds(4, 4), 0:128] = x0[:, 384:512]
-    wide[pl.ds(4, 4), 128:256] = b[0].astype(F32)
-    wide[pl.ds(4, 4), 256:264] = dt[0].astype(F32)
-    carry[...] = wide[:, 0:CARRY_LANES].astype(BF16)
 
 
 def table_body(parents, lengths, table):
@@ -101,6 +100,13 @@
         held[d] = ref[i]
 
 
+def stage_quarters_body(source, *refs):
+    outs, sems = refs[:4], refs[4]
+    pairs = [(source.at[:, pl.ds(1024 * y, 1024)], outs[y]) for y in range(4)]
+    for copy in fetch(pairs, sems):
+        copy.wait()
+
+
 def stage_body(*refs):
     half = (len(refs) - 1) // 2
     for copy in fetch(list(zip(refs[:half], refs[half : 2 * half])), refs[-1]):
@@ -111,12 +117,16 @@
     outs, held = refs[:4], refs[4]
     me = lax.axis_index("replica")
     hold(held, own, up, down)
-    first = first_rows((8, ITEM_LANES))
+    first = first_rows((8, STEP_LANES))
     for k in range(4):
         dest = (me + 8 * k) & 31
         for_child = held[(me - table[2, dest]) & 7].astype(F32)
         for_second = held[(me - table[3, dest]) & 7].astype(F32)
-        outs[k][...] = jnp.where(first, for_child, for_second).astype(BF16)
+        carry = held[(me - source_of(table, 1, dest)) & 7]
+        outs[k][:, 0:STEP_LANES] = jnp.where(
+            first, for_child[:, 0:STEP_LANES], for_second[:, 0:STEP_LANES]
+        ).astype(BF16)
+        outs[k][:, STEP_LANES:] = carry[:, STEP_LANES:]
 
 
 def bundle_back_body(own, one, two, three, out):
@@ -128,7 +138,7 @@
     outs, held = refs[:3], refs[3]
     me = lax.axis_index("replica")
     held[0], held[1], held[2] = own[...], up[...], down[...]
-    first = first_rows((8, RESULT_LANES))
+    first = first_rows((8, BACK_LANES))
     for k, step in enumerate((0, 3, 5)):
         dest = (me & 24) | ((me + step) & 7)
 
@@ -137,10 +147,9 @@
             ring = jnp.where(away == 1, 1, jnp.where(away == 7, 2, 0))
             return held[ring, column(me, source)].astype(F32)
 
-        one = pick(source_of(parents, 0, dest))[:, 0:RESULT_LANES]
-        two = pick(root_of(parents, dest))[:, 0:RESULT_LANES]
-        outs[k][:, 0:RESULT_LANES] = jnp.where(first, one, two).astype(BF16)
-        outs[k][:, RESULT_LANES:] = pick(source_of(parents, 1, dest))[:, RESULT_LANES:].astype(BF16)
+        one = pick(source_of(parents, 0, dest))
+        two = pick(root_of(parents, dest))
+        outs[k][...] = jnp.where(first, one, two).astype(BF16)
 
 
 def came_by(me, source):
@@ -168,7 +177,7 @@
 
 def attend_body(parents, *refs):
     blocks = refs[:4]
-    carry, keys, values, state, back, held = refs[4:10]
+    keys, values, state, back, carry, held = refs[4:10]
     me = lax.axis_index("replica")
     child = parents[2, me]
     second = parents[3, me]
@@ -176,8 +185,8 @@
         held[k] = blocks[k][...]
     one = held[column(me, child)].astype(F32)
     two = held[column(me, second)].astype(F32)
-    item = jnp.where(first_rows((8, ITEM_LANES)), one, two)
-    back[:, RESULT_LANES:] = carry[...]
+    item = jnp.where(first_rows((8, STEP_LANES)), one[:, 0:STEP_LANES], two[:, 0:STEP_LANES])
+    carry[...] = held[column(me, source_of(parents, 1, me))][:, STEP_LANES:]
 
     query = jnp.concatenate([item[:, h * HD : (h + 1) * HD] for h in range(8)], axis=0).astype(BF16)
     pads = jnp.zeros((120, HD), F32)
@@ -268,24 +277,23 @@
 
 def mamba_body(parents, a_rate, dt_bias, skip, *refs):
     blocks = refs[:3]
-    x_in, z_in, dt_in, b_in, c_in, gain, proj = refs[3:10]
-    attn, keep, send, carry, held, wide = refs[10:16]
+    carry, x_in, z_in, dt_in, b_in, c_in, gain = refs[3:10]
+    proj = refs[10:14]
+    attn, keep, send, held, wide = refs[14:19]
     me = lax.axis_index("replica")
     core = lax.axis_index("tensor") & 1
     for k in range(3):
         held[k] = blocks[k][...]
     one = held[came_by(me, source_of(parents, 0, me))].astype(F32)
     two = held[came_by(me, root_of(parents, me))].astype(F32)
-    mine = held[came_by(me, source_of(parents, 1, me))][:, RESULT_LANES:]
-    carry[...] = mine
     attn[0] = one[0:4, 0:1024].astype(BF16)
     attn[1] = two[4:8, 0:1024].astype(BF16)
     first = first_rows((8, 512))
-    read = jnp.where(first, one[:, 1024:RESULT_LANES], two[:, 1024:RESULT_LANES])
+    read = jnp.where(first, one[:, 1024:BACK_LANES], two[:, 1024:BACK_LANES])
 
     rate = per_head(a_rate)
     bias = per_head(dt_bias)
-    earlier = parent_rows(parents, me, mine, wide)
+    earlier = parent_rows(parents, me, carry[...], wide)
     decay_p, drive_p = step_terms(earlier[:, 640:768], earlier[:, 0:512], rate, bias)
     b_p = earlier[:, 512:640]
     wide[pl.ds(0, 8), 0:HD] = jnp.zeros((8, HD), F32)
@@ -304,8 +312,8 @@
     normed = (gated * lax.rsqrt(mean + 1e-05) * gain[...]).astype(BF16)
     for y in range(4):
         for target, parity in ((send, 1 - core), (keep, core)):
-            span = pl.ds(pl.multiple_of((2 * y + parity) * 512, 512), 512)
-            part = jnp.dot(normed, proj[:, span], preferred_element_type=F32)
+            span = pl.ds(pl.multiple_of(parity * 512, 512), 512)
+            part = jnp.dot(normed, proj[y][:, span], preferred_element_type=F32)
             target[y] = part.astype(BF16)
 
 
@@ -395,12 +403,12 @@
     gain,
     out_proj,
 ):
-    item, carry = call(
+    item = call(
         pack_body,
         "pack",
-        (struct((8, ITEM_LANES)), struct((8, CARRY_LANES))),
+        struct((8, ITEM_LANES)),
         [HBM] * 6,
-        (VMEM,) * 2,
+        VMEM,
         [
             pltpu.VMEM((2, 4, 1024), BF16),
             pltpu.VMEM((2, 4, 2, 128), BF16),
@@ -444,19 +452,34 @@
     blocks = [own_block] + list(blocks[1:])
     came = lax.all_to_all(moving.reshape(32, 16, 512), "replica", 0, 0, tiled=True)
     blocks = [blocks[0]] + [along_x(blocks[k], k) for k in range(1, 4)]
-    back = call(
+    back, carry = call(
         attend_body,
         "attend",
-        struct((8, BACK_LANES)),
-        [SMEM] + [VMEM] * 8,
-        VMEM,
+        (struct((8, BACK_LANES)), struct((8, CARRY_LANES))),
+        [SMEM] + [VMEM] * 7,
+        (VMEM,) * 2,
         [pltpu.VMEM((4, 8, ITEM_LANES), BF16)],
         flops=50000000000,
-    )(table, *blocks, carry, keys, values, state)
+    )(table, *blocks, keys, values, state)
+    back, weights = lax.optimization_barrier((back, out_proj))
+    weights = call(
+        stage_quarters_body,
+        "stage_proj",
+        (struct((512, 1024)),) * 4,
+        [HBM],
+        (VMEM,) * 4,
+        [pltpu.SemaphoreType.DMA((4,))],
+    )(weights)
+    others = [along_x(back, k) for k in range(1, 4)]
+    back, *weights = lax.optimization_barrier((back, *weights))
     rows = call(
         bundle_back_body, "bundle_back", struct((4, 8, BACK_LANES)), [VMEM] * 4, VMEM
-    )(back, *[along_x(back, k) for k in range(1, 4)])
+    )(back, *others)
     up, down = along_z(rows, 1), along_z(rows, 7)
+    regrouped = call(
+        regroup_body, "regroup", struct((32, 16, 512)), [SMEM, VMEM, HBM], VMEM
+    )(table, came, rows)
+    rows, regrouped = lax.optimization_barrier((rows, regrouped))
     blocks = call(
         sort_back_body,
         "sort_back",
@@ -465,39 +488,27 @@
         (VMEM,) * 3,
         [pltpu.VMEM((3, 4, 8, BACK_LANES), BF16)],
     )(table, rows, up, down)
-    regrouped = call(
-        regroup_body, "regroup", struct((32, 16, 512)), [SMEM, VMEM, HBM], VMEM
-    )(table, came, rows)
-    own_block, regrouped, weights = lax.optimization_barrier((blocks[0], regrouped, out_proj))
-    weights = call(
-        stage_body,
-        "stage_proj",
-        struct((512, 4096)),
-        [HBM],
-        VMEM,
-        [pltpu.SemaphoreType.DMA((1,))],
-    )(weights)
+    own_block, regrouped = lax.optimization_barrier((blocks[0], regrouped))
     arrived = lax.all_to_all(regrouped, "replica", 0, 0, tiled=True)
     blocks = [own_block, along_z(blocks[1], 3), along_z(blocks[2], 5)]
-    attn_out, keep, send, carry = call(
+    attn_out, keep, send = call(
         mamba_body,
         "mamba",
         (
             struct((2, 4, 1024)),
             struct((4, 8, 512)),
             struct((4, 8, 512)),
-            struct((8, CARRY_LANES)),
         ),
-        [SMEM] * 4 + [VMEM] * 10,
-        (VMEM,) * 4,
+        [SMEM] * 4 + [VMEM] * 14,
+        (VMEM,) * 3,
         [
             pltpu.VMEM((3, 8, BACK_LANES), BF16),
             pltpu.VMEM((16, 768), F32),
         ],
         flops=50000000000,
     )(
-        table, a_rate, dt_bias, skip, *blocks, x_in, z_in, dt_in, b_in, c_in,
-        gain.reshape(1, 512), weights,
+        table, a_rate, dt_bias, skip, *blocks, carry, x_in, z_in, dt_in, b_in, c_in,
+        gain.reshape(1, 512), *weights,
     )
     parts = call(
         core_sum_body,

time: 83 us -> 81.2 us (0.978)
  waiting for transfers between devices: 18.4 us -> 15.7 us
  local copies, waits for them, and re-layouts: 8.85 us -> 10.1 us
    ppermute x8, waiting for transfers between devices: 8.17 us -> 4.18 us  [along_z(): lax.ppermute(array, 'replica', [(r, r & 24 | r + k & 7) for r in range(32)])]
    all_to_all x1, waiting for transfers between devices: 0.01 us -> 3.6 us  [per_device(): lax.all_to_all(moving.reshape(32, 16, 512), 'replica', 0, 0, tiled=True)]
    ppermute x6, waiting for transfers between devices: 4.59 us -> 1.65 us  [along_x(): lax.ppermute(array, 'replica', [(r, r + 8 * k & 31) for r in range(32)])]
    unnamed x34 -> x40, local copies, waits for them, and re-layouts: 8.85 us -> 10.1 us
    ppermute x8, starting transfers between devices: 16.2 us -> 15.2 us  [along_z(): lax.ppermute(array, 'replica', [(r, r & 24 | r + k & 7) for r in range(32)])]
  transfers between devices with their start and end apart: 20 -> 20, of which waited for: 8 -> 6; matrix products, arithmetic and copies ran while one was open for 0% -> 0% of each run, Pallas kernels for 12% -> 12%
where the time goes in v3:
time: 81.2 us; the launch traced here: 80.6 us
  starting transfers between devices  41 us (50%)
  waiting for transfers between devices  15.7 us (19%)
  Pallas kernels  12.9 us (16%)
  local copies, waits for them, and re-layouts  10.1 us (12%)
  between operations  0.93 us (1%)
    ppermute x8, starting transfers between devices, along_z(): lax.ppermute(array, 'replica', [(r, r & 24 | r + k & 7) for r in range(32)])  15.2 us
    ppermute x6, starting transfers between devices, along_x(): lax.ppermute(array, 'replica', [(r, r + 8 * k & 31) for r in range(32)])  10.3 us
    unnamed x40, local copies, waits for them, and re-layouts  10.1 us
    all_to_all x1, starting transfers between devices, per_device(): arrived = lax.all_to_all(regrouped, 'replica', 0, 0, tiled=True)  7.75 us
    all_to_all x1, waiting for transfers between devices, per_device(): arrived = lax.all_to_all(regrouped, 'replica', 0, 0, tiled=True)  5.03 us
    all_to_all x1, starting transfers between devices, per_device(): lax.all_to_all(moving.reshape(32, 16, 512), 'replica', 0, 0, tiled=True)  4.84 us
    ppermute x8, waiting for transfers between devices, along_z(): lax.ppermute(array, 'replica', [(r, r & 24 | r + k & 7) for r in range(32)])  4.18 us
    all_to_all x1, waiting for transfers between devices, per_device(): lax.all_to_all(moving.reshape(32, 16, 512), 'replica', 0, 0, tiled=True)  3.6 us
  transfers between devices with their start and end apart: 20, of which 6 were waited for; matrix products, arithmetic and copies ran while one was open for 0% of the time, Pallas kernels for 12%

profile of v3, /device:TPU:56, one launch (start us, length us, event | category | flops | bytes accessed | tf_op | source)
XLA Modules:
  0.0 80.6 jit_solution(3647933870783956721)
XLA Ops:
  0.6 1.4 %pack.1.own = bf16[8,1792]{1,0:T(8,128)(2,1)} custom-call(bf16[2,4,1024]{2,1,0:T(4,128)(2,1)} %refs_0_.1, bf16[2,4,2,128]{3,2,1,0:T(2,128)(2,1)} %refs_1_.1, bf16[2,4,128]{2,1,0:T(4,128)(2,1)} %refs_8_.1, bf16[2,4,512]{2,1,0:T(4,128)(2,1)} %x_in.1, bf16[2,4,128]{2,1,0:T(4,128)(2,1)} %b_in.1, bf16[2,4,8]{2,1,0:T(4,128)(2,1)} %dt_in.1), custom_call_target="tpu_custom_call" | custom-call | flops 1000000 | tf_op jit(solution)/shard_map/pack/pallas_call | solution.py:406
  2.1 5.9 %collective-permute-start.1 = (bf16[8,1792]{1,0:T(8,128)(2,1)}, bf16[8,1792]{1,0:T(8,128)(2,1)S(1)}, u32[]{:S(2)}, u32[]{:S(2)}) collective-permute-start(bf16[8,1792]{1,0:T(8,128)(2,1)} %pack.1.own), channel_id=1, source_target_pairs={{0,40},{8,48},{16,56},{24,0},{32,8},{40,16},{48,24},{56,32},{64,10... | collective-permute-start | bytes 86024 | tf_op jit(solution)/shard_map/ppermute | solution.py:372
  8.0 0.1 collective-permute-start
  8.1 0.7 copy-done.9
  8.8 0.7 copy-done.12
  9.4 1.5 %table.1.parents = s32[8,128]{1,0:T(8,128)S(1)} custom-call(s32[2,128]{1,0:T(2,128)S(1)} %copy-done.9, s32[32]{0:T(128)S(1)} %copy-done.12), custom_call_target="tpu_custom_call" | custom-call | flops 1000000 | tf_op jit(solution)/shard_map/table/pallas_call | solution.py:425
  11.0 0.0 collective-permute-done.1.down
  11.0 4.1 %collective-permute-done.up = bf16[8,1792]{1,0:T(8,128)(2,1)S(1)} collective-permute-done((bf16[8,1792]{1,0:T(8,128)(2,1)}, bf16[8,1792]{1,0:T(8,128)(2,1)S(1)}, u32[]{:S(2)}, u32[]{:S(2)}) %collective-permute-start) | collective-permute-done | bytes 28704 | tf_op jit(solution)/shard_map/ppermute | solution.py:372
  15.1 0.7 copy-done.4
  15.9 1.3 %collective-permute-start.3 = (bf16[3,8,1792]{2,1,0:T(8,128)(2,1)S(1)}, bf16[3,8,1792]{2,1,0:T(8,128)(2,1)S(1)}, u32[]{:S(2)}, u32[]{:S(2)}) collective-permute-start(bf16[3,8,1792]{2,1,0:T(8,128)(2,1)S(1)} %bundle.1.own), channel_id=1, source_target_pairs={{0,56},{8,0},{16,8},{24,16},{32,24},{40,32},{48,40},{56,48},{64,12... | collective-permute-start | bytes 258056 | tf_op jit(solution)/shard_map/ppermute | solution.py:372
  17.2 0.7 collective-permute-start.2
  17.9 1.0 %copy-done.1 = bf16[4,128,512]{2,1,0:T(8,128)(2,1)S(1)} copy-done((bf16[4,128,512]{2,1,0:T(8,128)(2,1)S(1)}, bf16[4,128,512]{2,1,0:T(8,128)(2,1)}, u32[]{:S(2)}) %copy-start.1) | copy-done | bytes 524312
  18.9 1.2 %copy-done.2 = bf16[4,1024,128]{2,1,0:T(8,128)(2,1)S(1)} copy-done((bf16[4,1024,128]{2,1,0:T(8,128)(2,1)S(1)}, bf16[4,1024,128]{2,1,0:T(8,128)(2,1)}, u32[]{:S(2)}) %copy-start.2) | copy-done | bytes 1048600
  20.2 1.2 %copy-done.3 = bf16[4,1024,128]{2,1,0:T(8,128)(2,1)S(1)} copy-done((bf16[4,1024,128]{2,1,0:T(8,128)(2,1)S(1)}, bf16[4,1024,128]{2,1,0:T(8,128)(2,1)}, u32[]{:S(2)}) %copy-start.3) | copy-done | bytes 1048600
  21.4 0.2 stage.1
  21.6 0.0 collective-permute-done.3.down
  21.6 0.0 collective-permute-done.2.up
  21.7 0.6 sort_out.1
  22.3 1.6 %collective-permute-start.4 = (bf16[8,1792]{1,0:T(8,128)(2,1)S(1)}, bf16[8,1792]{1,0:T(8,128)(2,1)S(1)}, u32[]{:S(2)}, u32[]{:S(2)}) collective-permute-start(bf16[8,1792]{1,0:T(8,128)(2,1)S(1)} %get-tuple-element.65), channel_id=1, source_target_pairs={{0,64},{8,72},{16,80},{24,88},{32,96},{40,104},{48,112},{56,120},{... | collective-permute-start | bytes 86024 | tf_op jit(solution)/shard_map/ppermute | solution.py:368
  23.9 2.7 %collective-permute-start.5 = (bf16[8,1792]{1,0:T(8,128)(2,1)S(1)}, bf16[8,1792]{1,0:T(8,128)(2,1)S(1)}, u32[]{:S(2)}, u32[]{:S(2)}) collective-permute-start(bf16[8,1792]{1,0:T(8,128)(2,1)S(1)} %get-tuple-element.66), channel_id=1, source_target_pairs={{0,128},{8,136},{16,144},{24,152},{32,160},{40,168},{48,176},{56,1... | collective-permute-start | bytes 86024 | tf_op jit(solution)/shard_map/ppermute | solution.py:368
  26.6 1.4 %collective-permute-start.6 = (bf16[8,1792]{1,0:T(8,128)(2,1)S(1)}, bf16[8,1792]{1,0:T(8,128)(2,1)S(1)}, u32[]{:S(2)}, u32[]{:S(2)}) collective-permute-start(bf16[8,1792]{1,0:T(8,128)(2,1)S(1)} %get-tuple-element.67), channel_id=1, source_target_pairs={{0,192},{8,200},{16,208},{24,216},{32,224},{40,232},{48,240},{56,2... | collective-permute-start | bytes 86024 | tf_op jit(solution)/shard_map/ppermute | solution.py:368
  28.0 4.8 %all-to-all-start = ((bf16[32,16,512]{2,1,0:T(8,128)(2,1)}), bf16[32,16,512]{2,1,0:T(8,128)(2,1)S(1)}, u32[]{:S(2)}, u32[]{:S(2)}) async-start(bf16[32,16,512]{2,1,0:T(8,128)(2,1)} %bitcast.3), calls=%async_computation | async-start | bytes 1048576 | tf_op jit(solution)/shard_map/all_to_all | solution.py:453
  32.9 0.0 copy-start
  32.9 0.0 collective-permute-done.4.refs_1_
  32.9 0.0 collective-permute-done.5.refs_2_
  32.9 0.0 collective-permute-done.6.refs_3_
  32.9 1.5 %attend.1 = (bf16[8,1536]{1,0:T(8,128)(2,1)S(1)}, bf16[8,384]{1,0:T(8,128)(2,1)S(1)}) custom-call(s32[8,128]{1,0:T(8,128)S(1)} %table.1.parents, bf16[8,1792]{1,0:T(8,128)(2,1)S(1)} %get-tuple-element.64.refs_0_, bf16[8,1792]{1,0:T(8,128)(2,1)S(1)} %collective-permute-done.4.refs_1_, bf16[8,1792]{1,0:T(8,128)(2,1)S(1)} %collective-permute-done.5.refs_2_, ...), custom_call_target="tpu_custom_call" | custom-call | flops 49999998976 | tf_op jit(solution)/shard_map/attend/pallas_call | solution.py:455
  34.5 0.0 copy-start.8
  34.5 0.0 copy-start.10
  34.5 0.0 copy-start.11
  34.5 0.0 copy-start.17
  34.5 0.0 copy-start.18
  34.5 0.0 copy-start.19
  34.6 2.9 %collective-permute-start.9 = (bf16[8,1536]{1,0:T(8,128)(2,1)S(1)}, bf16[8,1536]{1,0:T(8,128)(2,1)S(1)}, u32[]{:S(2)}, u32[]{:S(2)}) collective-permute-start(bf16[8,1536]{1,0:T(8,128)(2,1)S(1)} %get-tuple-element.78.own), channel_id=1, source_target_pairs={{0,192},{8,200},{16,208},{24,216},{32,224},{40,232},{48,240},{56,2... | collective-permute-start | bytes 73736 | tf_op jit(solution)/shard_map/ppermute | solution.py:368
  37.5 0.7 collective-permute-start.8
  38.2 0.9 %collective-permute-start.7 = (bf16[8,1536]{1,0:T(8,128)(2,1)S(1)}, bf16[8,1536]{1,0:T(8,128)(2,1)S(1)}, u32[]{:S(2)}, u32[]{:S(2)}) collective-permute-start(bf16[8,1536]{1,0:T(8,128)(2,1)S(1)} %get-tuple-element.78.own), channel_id=1, source_target_pairs={{0,64},{8,72},{16,80},{24,88},{32,96},{40,104},{48,112},{56,120},{... | collective-permute-start | bytes 73736 | tf_op jit(solution)/shard_map/ppermute | solution.py:368
  39.1 0.7 stage_proj.1
  39.9 1.0 %copy-done.13 = bf16[512,1024]{1,0:T(8,128)(2,1)} copy-done((bf16[512,1024]{1,0:T(8,128)(2,1)}, bf16[512,1024]{1,0:T(8,128)(2,1)S(1)}, u32[]{:S(2)}) %copy-start.13) | copy-done | bytes 1048600
  40.9 1.0 %copy-done.15 = bf16[512,1024]{1,0:T(8,128)(2,1)} copy-done((bf16[512,1024]{1,0:T(8,128)(2,1)}, bf16[512,1024]{1,0:T(8,128)(2,1)S(1)}, u32[]{:S(2)}) %copy-start.15) | copy-done | bytes 1048600
  41.9 0.0 collective-permute-done.9.three
  41.9 1.3 %collective-permute-done.8.two = bf16[8,1536]{1,0:T(8,128)(2,1)S(1)} collective-permute-done((bf16[8,1536]{1,0:T(8,128)(2,1)S(1)}, bf16[8,1536]{1,0:T(8,128)(2,1)S(1)}, u32[]{:S(2)}, u32[]{:S(2)}) %collective-permute-start.8) | collective-permute-done | bytes 24608 | tf_op jit(solution)/shard_map/ppermute | solution.py:368
  43.2 0.3 collective-permute-done.7.one
  43.5 0.6 collective-permute-start.11
  44.1 1.5 %collective-permute-start.10 = (bf16[4,8,1536]{2,1,0:T(8,128)(2,1)S(1)}, bf16[4,8,1536]{2,1,0:T(8,128)(2,1)S(1)}, u32[]{:S(2)}, u32[]{:S(2)}) collective-permute-start(bf16[4,8,1536]{2,1,0:T(8,128)(2,1)S(1)} %bundle_back.1._.own), channel_id=1, source_target_pairs={{0,8},{8,16},{16,24},{24,32},{32,40},{40,48},{48,56},{56,0},{64,72... | collective-permute-start | bytes 294920 | tf_op jit(solution)/shard_map/ppermute | solution.py:372
  45.6 3.6 %all-to-all-done.came = bf16[32,16,512]{2,1,0:T(8,128)(2,1)S(1)} async-done(((bf16[32,16,512]{2,1,0:T(8,128)(2,1)}), bf16[32,16,512]{2,1,0:T(8,128)(2,1)S(1)}, u32[]{:S(2)}, u32[]{:S(2)}) %all-to-all-start) | async-done | bytes 524320 | tf_op jit(solution)/shard_map/all_to_all | solution.py:453
  49.2 1.5 %regroup.1 = bf16[32,16,512]{2,1,0:T(8,128)(2,1)} custom-call(s32[8,128]{1,0:T(8,128)S(1)} %table.1.parents, bf16[32,16,512]{2,1,0:T(8,128)(2,1)S(1)} %all-to-all-done.came, bf16[4,8,1536]{2,1,0:T(8,128)(2,1)S(1)} %bundle_back.1._.own), custom_call_target="tpu_custom_call" | custom-call | flops 1000000 | tf_op jit(solution)/shard_map/regroup/pallas_call | solution.py:479
  50.7 0.0 collective-permute-done.11.down
  50.7 0.0 collective-permute-done.10.up
  50.7 0.7 sort_back.1
  51.3 4.3 %collective-permute-start.12 = (bf16[8,1536]{1,0:T(8,128)(2,1)S(1)}, bf16[8,1536]{1,0:T(8,128)(2,1)S(1)}, u32[]{:S(2)}, u32[]{:S(2)}) collective-permute-start(bf16[8,1536]{1,0:T(8,128)(2,1)S(1)} %get-tuple-element.84), channel_id=1, source_target_pairs={{0,24},{8,32},{16,40},{24,48},{32,56},{40,0},{48,8},{56,16},{64,88... | collective-permute-start | bytes 73736 | tf_op jit(solution)/shard_map/ppermute | solution.py:372
  55.7 0.8 collective-permute-start.13
  56.5 7.7 %all-to-all-start.1 = ((bf16[32,16,512]{2,1,0:T(8,128)(2,1)}), bf16[32,16,512]{2,1,0:T(8,128)(2,1)S(1)}, u32[]{:S(2)}, u32[]{:S(2)}) async-start(bf16[32,16,512]{2,1,0:T(8,128)(2,1)} %regroup.1), calls=%async_computation.1 | async-start | bytes 1048576 | tf_op jit(solution)/shard_map/all_to_all | solution.py:492
  64.2 0.0 collective-permute-done.12.refs_1_
  64.3 1.2 %copy-done.14 = bf16[512,1024]{1,0:T(8,128)(2,1)S(1)} copy-done((bf16[512,1024]{1,0:T(8,128)(2,1)S(1)}, bf16[512,1024]{1,0:T(8,128)(2,1)}, u32[]{:S(2)}) %copy-start.14) | copy-done | bytes 1048600
  65.6 1.2 %copy-done.16 = bf16[512,1024]{1,0:T(8,128)(2,1)S(1)} copy-done((bf16[512,1024]{1,0:T(8,128)(2,1)S(1)}, bf16[512,1024]{1,0:T(8,128)(2,1)}, u32[]{:S(2)}) %copy-start.16) | copy-done | bytes 1048600
  66.8 2.1 %mamba.1 = (bf16[2,4,1024]{2,1,0:T(4,128)(2,1)}, bf16[4,8,512]{2,1,0:T(8,128)(2,1)S(1)}, bf16[4,8,512]{2,1,0:T(8,128)(2,1)S(1)}) custom-call(s32[8,128]{1,0:T(8,128)S(1)} %table.1.parents, f32[8]{0:T(128)S(1)} %copy-done.10, f32[8]{0:T(128)S(1)} %copy-done.11, f32[8]{0:T(128)S(1)} %copy-done.19, bf16[8,1536]{1,0:T(8,128)(2,1)S(1)} %get-tuple-element.83.refs_0_, ...), custom_call_target="tpu_custom_call" | custom-call | flops 49999998976 | tf_op jit(solution)/shard_map/mamba/pallas_call | solution.py:494
  68.8 1.2 %collective-permute-done.14.came = bf16[4,8,512]{2,1,0:T(8,128)(2,1)S(1)} collective-permute-done((bf16[4,8,512]{2,1,0:T(8,128)(2,1)S(1)}, bf16[4,8,512]{2,1,0:T(8,128)(2,1)S(1)}, u32[]{:S(2)}, u32[]{:S(2)}) %collective-permute-start.14) | collective-permute-done | bytes 32800 | tf_op jit(solution)/shard_map/ppermute | solution.py:380
  70.1 0.3 collective-permute-start.15
  70.4 2.6 %collective-permute-start.16 = (bf16[8,512]{1,0:T(8,128)(2,1)S(1)}, bf16[8,512]{1,0:T(8,128)(2,1)S(1)}, u32[]{:S(2)}, u32[]{:S(2)}) collective-permute-start(bf16[8,512]{1,0:T(8,128)(2,1)S(1)} %get-tuple-element.98), channel_id=1, source_target_pairs={{0,4},{1,5},{2,6},{3,7},{4,0},{5,1},{6,2},{7,3},{8,12},{9,13},{10,... | collective-permute-start | bytes 24584 | tf_op jit(solution)/shard_map/ppermute | solution.py:376
  73.0 0.0 collective-permute-start.17
  73.0 5.0 %all-to-all-done.1.state = bf16[32,16,512]{2,1,0:T(8,128)(2,1)S(1)} async-done(((bf16[32,16,512]{2,1,0:T(8,128)(2,1)}), bf16[32,16,512]{2,1,0:T(8,128)(2,1)S(1)}, u32[]{:S(2)}, u32[]{:S(2)}) %all-to-all-start.1) | async-done | bytes 524320 | tf_op jit(solution)/shard_map/all_to_all | solution.py:492
  78.0 1.9 %advance.1 = bf16[32,16,512]{2,1,0:T(8,128)(2,1)} custom-call(s32[8,128]{1,0:T(8,128)S(1)} %table.1.parents, f32[8]{0:T(128)S(1)} %copy-done.10, f32[8]{0:T(128)S(1)} %copy-done.11, bf16[32,16,512]{2,1,0:T(8,128)(2,1)S(1)} %all-to-all-done.1.state, bf16[8,384]{1,0:T(8,128)(2,1)S(1)} %get-tuple-element.86.refs_3_.carry, bf16[2,4,512]{2,1,0:T(4,128)(2,1)S(1)} %copy-done.5, ...), custom_call_target="tpu_custom_call" | custom-call | flops 1000000 | tf_op jit(solution)/shard_map/advance/pallas_call | solution.py:521
  79.9 0.0 collective-permute-done.17.d
  79.9 0.6 last_sum.1
  (30 shorter events, 0.1 us)
Async XLA Ops:
  2.1 8.9 %collective-permute-start.1 = (bf16[8,1792]{1,0:T(8,128)(2,1)}, bf16[8,1792]{1,0:T(8,128)(2,1)S(1)}, u32[]{:S(2)}, u32[]{:S(2)}) collective-permute-start(bf16[8,1792]{1,0:T(8,128)(2,1)} %pack.1.own), channel_id=1, source_target_pairs={{0,40},{8,48},{16,56},{24,0},{32,8},{40,16},{48,24},{56,32},{64,10... | collective-permute-start | bytes 86024 | tf_op jit(solution)/shard_map/ppermute | solution.py:372
  8.0 7.1 %collective-permute-start = (bf16[8,1792]{1,0:T(8,128)(2,1)}, bf16[8,1792]{1,0:T(8,128)(2,1)S(1)}, u32[]{:S(2)}, u32[]{:S(2)}) collective-permute-start(bf16[8,1792]{1,0:T(8,128)(2,1)} %pack.1.own), channel_id=1, source_target_pairs={{0,24},{8,32},{16,40},{24,48},{32,56},{40,0},{48,8},{56,16},{64,88... | collective-permute-start | bytes 86024 | tf_op jit(solution)/shard_map/ppermute | solution.py:372
  8.1 0.7 copy-start.9
  8.8 0.7 copy-start.12
  15.1 0.7 copy-start.4
  15.9 5.7 %collective-permute-start.3 = (bf16[3,8,1792]{2,1,0:T(8,128)(2,1)S(1)}, bf16[3,8,1792]{2,1,0:T(8,128)(2,1)S(1)}, u32[]{:S(2)}, u32[]{:S(2)}) collective-permute-start(bf16[3,8,1792]{2,1,0:T(8,128)(2,1)S(1)} %bundle.1.own), channel_id=1, source_target_pairs={{0,56},{8,0},{16,8},{24,16},{32,24},{40,32},{48,40},{56,48},{64,12... | collective-permute-start | bytes 258056 | tf_op jit(solution)/shard_map/ppermute | solution.py:372
  17.2 4.5 %collective-permute-start.2 = (bf16[3,8,1792]{2,1,0:T(8,128)(2,1)S(1)}, bf16[3,8,1792]{2,1,0:T(8,128)(2,1)S(1)}, u32[]{:S(2)}, u32[]{:S(2)}) collective-permute-start(bf16[3,8,1792]{2,1,0:T(8,128)(2,1)S(1)} %bundle.1.own), channel_id=1, source_target_pairs={{0,8},{8,16},{16,24},{24,32},{32,40},{40,48},{48,56},{56,0},{64,72... | collective-permute-start | bytes 258056 | tf_op jit(solution)/shard_map/ppermute | solution.py:372
  17.9 1.0 %copy-start.1 = (bf16[4,128,512]{2,1,0:T(8,128)(2,1)S(1)}, bf16[4,128,512]{2,1,0:T(8,128)(2,1)}, u32[]{:S(2)}) copy-start(bf16[4,128,512]{2,1,0:T(8,128)(2,1)} %refs_2_.2) | copy-start | bytes 1572868
  18.9 1.2 %copy-start.2 = (bf16[4,1024,128]{2,1,0:T(8,128)(2,1)S(1)}, bf16[4,1024,128]{2,1,0:T(8,128)(2,1)}, u32[]{:S(2)}) copy-start(bf16[4,1024,128]{2,1,0:T(8,128)(2,1)} %refs_0_.2) | copy-start | bytes 3145732
  20.2 1.2 %copy-start.3 = (bf16[4,1024,128]{2,1,0:T(8,128)(2,1)S(1)}, bf16[4,1024,128]{2,1,0:T(8,128)(2,1)}, u32[]{:S(2)}) copy-start(bf16[4,1024,128]{2,1,0:T(8,128)(2,1)} %refs_1_.2) | copy-start | bytes 3145732
  22.3 10.6 %collective-permute-start.4 = (bf16[8,1792]{1,0:T(8,128)(2,1)S(1)}, bf16[8,1792]{1,0:T(8,128)(2,1)S(1)}, u32[]{:S(2)}, u32[]{:S(2)}) collective-permute-start(bf16[8,1792]{1,0:T(8,128)(2,1)S(1)} %get-tuple-element.65), channel_id=1, source_target_pairs={{0,64},{8,72},{16,80},{24,88},{32,96},{40,104},{48,112},{56,120},{... | collective-permute-start | bytes 86024 | tf_op jit(solution)/shard_map/ppermute | solution.py:368
  23.9 9.0 %collective-permute-start.5 = (bf16[8,1792]{1,0:T(8,128)(2,1)S(1)}, bf16[8,1792]{1,0:T(8,128)(2,1)S(1)}, u32[]{:S(2)}, u32[]{:S(2)}) collective-permute-start(bf16[8,1792]{1,0:T(8,128)(2,1)S(1)} %get-tuple-element.66), channel_id=1, source_target_pairs={{0,128},{8,136},{16,144},{24,152},{32,160},{40,168},{48,176},{56,1... | collective-permute-start | bytes 86024 | tf_op jit(solution)/shard_map/ppermute | solution.py:368
  26.6 6.3 %collective-permute-start.6 = (bf16[8,1792]{1,0:T(8,128)(2,1)S(1)}, bf16[8,1792]{1,0:T(8,128)(2,1)S(1)}, u32[]{:S(2)}, u32[]{:S(2)}) collective-permute-start(bf16[8,1792]{1,0:T(8,128)(2,1)S(1)} %get-tuple-element.67), channel_id=1, source_target_pairs={{0,192},{8,200},{16,208},{24,216},{32,224},{40,232},{48,240},{56,2... | collective-permute-start | bytes 86024 | tf_op jit(solution)/shard_map/ppermute | solution.py:368
  28.0 21.2 %all-to-all-start = ((bf16[32,16,512]{2,1,0:T(8,128)(2,1)}), bf16[32,16,512]{2,1,0:T(8,128)(2,1)S(1)}, u32[]{:S(2)}, u32[]{:S(2)}) async-start(bf16[32,16,512]{2,1,0:T(8,128)(2,1)} %bitcast.3), calls=%async_computation | async-start | bytes 1048576 | tf_op jit(solution)/shard_map/all_to_all | solution.py:453
  32.9 6.2 %copy-start = (bf16[512,4096]{1,0:T(8,128)(2,1)S(1)}, bf16[512,4096]{1,0:T(8,128)(2,1)}, u32[]{:S(2)}) copy-start(bf16[512,4096]{1,0:T(8,128)(2,1)} %source) | copy-start | bytes 12582916
  34.5 29.8 %copy-start.5 = (bf16[2,4,512]{2,1,0:T(4,128)(2,1)S(1)}, bf16[2,4,512]{2,1,0:T(4,128)(2,1)}, u32[]{:S(2)}) copy-start(bf16[2,4,512]{2,1,0:T(4,128)(2,1)} %x_in.1) | copy-start | bytes 24580
  34.5 29.8 %copy-start.6 = (bf16[2,4,128]{2,1,0:T(4,128)(2,1)S(1)}, bf16[2,4,128]{2,1,0:T(4,128)(2,1)}, u32[]{:S(2)}) copy-start(bf16[2,4,128]{2,1,0:T(4,128)(2,1)} %b_in.1) | copy-start | bytes 6148
  34.5 29.8 %copy-start.7 = (bf16[2,4,8]{2,1,0:T(4,128)(2,1)S(1)}, bf16[2,4,8]{2,1,0:T(4,128)(2,1)}, u32[]{:S(2)}) copy-start(bf16[2,4,8]{2,1,0:T(4,128)(2,1)} %dt_in.1) | copy-start | bytes 388
  34.5 29.8 %copy-start.8 = (bf16[2,4,128]{2,1,0:T(4,128)(2,1)S(1)}, bf16[2,4,128]{2,1,0:T(4,128)(2,1)}, u32[]{:S(2)}) copy-start(bf16[2,4,128]{2,1,0:T(4,128)(2,1)} %refs_8_.1) | copy-start | bytes 6148
  34.5 29.8 %copy-start.10 = (f32[8]{0:T(128)S(1)}, f32[8]{0:T(128)}, u32[]{:S(2)}) copy-start(f32[8]{0:T(128)} %a_rate.3) | copy-start | bytes 100
  34.5 29.8 %copy-start.11 = (f32[8]{0:T(128)S(1)}, f32[8]{0:T(128)}, u32[]{:S(2)}) copy-start(f32[8]{0:T(128)} %dt_bias.3) | copy-start | bytes 100
  34.5 29.8 %copy-start.17 = (bf16[2,4,512]{2,1,0:T(4,128)(2,1)S(1)}, bf16[2,4,512]{2,1,0:T(4,128)(2,1)}, u32[]{:S(2)}) copy-start(bf16[2,4,512]{2,1,0:T(4,128)(2,1)} %refs_5_.3) | copy-start | bytes 24580
  34.5 29.8 %copy-start.18 = (f32[512]{0:T(512)S(1)}, f32[512]{0:T(512)}, u32[]{:S(2)}) copy-start(f32[512]{0:T(512)} %param.32) | copy-start | bytes 6148
  34.5 29.8 %copy-start.19 = (f32[8]{0:T(128)S(1)}, f32[8]{0:T(128)}, u32[]{:S(2)}) copy-start(f32[8]{0:T(128)} %skip.1) | copy-start | bytes 100
  34.6 7.3 %collective-permute-start.9 = (bf16[8,1536]{1,0:T(8,128)(2,1)S(1)}, bf16[8,1536]{1,0:T(8,128)(2,1)S(1)}, u32[]{:S(2)}, u32[]{:S(2)}) collective-permute-start(bf16[8,1536]{1,0:T(8,128)(2,1)S(1)} %get-tuple-element.78.own), channel_id=1, source_target_pairs={{0,192},{8,200},{16,208},{24,216},{32,224},{40,232},{48,240},{56,2... | collective-permute-start | bytes 73736 | tf_op jit(solution)/shard_map/ppermute | solution.py:368
  37.5 5.7 %collective-permute-start.8 = (bf16[8,1536]{1,0:T(8,128)(2,1)S(1)}, bf16[8,1536]{1,0:T(8,128)(2,1)S(1)}, u32[]{:S(2)}, u32[]{:S(2)}) collective-permute-start(bf16[8,1536]{1,0:T(8,128)(2,1)S(1)} %get-tuple-element.78.own), channel_id=1, source_target_pairs={{0,128},{8,136},{16,144},{24,152},{32,160},{40,168},{48,176},{56,1... | collective-permute-start | bytes 73736 | tf_op jit(solution)/shard_map/ppermute | solution.py:368
  38.2 5.3 %collective-permute-start.7 = (bf16[8,1536]{1,0:T(8,128)(2,1)S(1)}, bf16[8,1536]{1,0:T(8,128)(2,1)S(1)}, u32[]{:S(2)}, u32[]{:S(2)}) collective-permute-start(bf16[8,1536]{1,0:T(8,128)(2,1)S(1)} %get-tuple-element.78.own), channel_id=1, source_target_pairs={{0,64},{8,72},{16,80},{24,88},{32,96},{40,104},{48,112},{56,120},{... | collective-permute-start | bytes 73736 | tf_op jit(solution)/shard_map/ppermute | solution.py:368
  39.8 1.0 %copy-start.13 = (bf16[512,1024]{1,0:T(8,128)(2,1)}, bf16[512,1024]{1,0:T(8,128)(2,1)S(1)}, u32[]{:S(2)}) copy-start(bf16[512,1024]{1,0:T(8,128)(2,1)S(1)} %get-tuple-element.89.refs_12_) | copy-start | bytes 3145732
  40.9 1.0 %copy-start.15 = (bf16[512,1024]{1,0:T(8,128)(2,1)}, bf16[512,1024]{1,0:T(8,128)(2,1)S(1)}, u32[]{:S(2)}) copy-start(bf16[512,1024]{1,0:T(8,128)(2,1)S(1)} %get-tuple-element.90.refs_13_) | copy-start | bytes 3145732
  43.5 7.2 %collective-permute-start.11 = (bf16[4,8,1536]{2,1,0:T(8,128)(2,1)S(1)}, bf16[4,8,1536]{2,1,0:T(8,128)(2,1)S(1)}, u32[]{:S(2)}, u32[]{:S(2)}) collective-permute-start(bf16[4,8,1536]{2,1,0:T(8,128)(2,1)S(1)} %bundle_back.1._.own), channel_id=1, source_target_pairs={{0,56},{8,0},{16,8},{24,16},{32,24},{40,32},{48,40},{56,48},{64,12... | collective-permute-start | bytes 294920 | tf_op jit(solution)/shard_map/ppermute | solution.py:372
  44.1 6.6 %collective-permute-start.10 = (bf16[4,8,1536]{2,1,0:T(8,128)(2,1)S(1)}, bf16[4,8,1536]{2,1,0:T(8,128)(2,1)S(1)}, u32[]{:S(2)}, u32[]{:S(2)}) collective-permute-start(bf16[4,8,1536]{2,1,0:T(8,128)(2,1)S(1)} %bundle_back.1._.own), channel_id=1, source_target_pairs={{0,8},{8,16},{16,24},{24,32},{32,40},{40,48},{48,56},{56,0},{64,72... | collective-permute-start | bytes 294920 | tf_op jit(solution)/shard_map/ppermute | solution.py:372
  51.3 12.9 %collective-permute-start.12 = (bf16[8,1536]{1,0:T(8,128)(2,1)S(1)}, bf16[8,1536]{1,0:T(8,128)(2,1)S(1)}, u32[]{:S(2)}, u32[]{:S(2)}) collective-permute-start(bf16[8,1536]{1,0:T(8,128)(2,1)S(1)} %get-tuple-element.84), channel_id=1, source_target_pairs={{0,24},{8,32},{16,40},{24,48},{32,56},{40,0},{48,8},{56,16},{64,88... | collective-permute-start | bytes 73736 | tf_op jit(solution)/shard_map/ppermute | solution.py:372
  55.7 8.6 %collective-permute-start.13 = (bf16[8,1536]{1,0:T(8,128)(2,1)S(1)}, bf16[8,1536]{1,0:T(8,128)(2,1)S(1)}, u32[]{:S(2)}, u32[]{:S(2)}) collective-permute-start(bf16[8,1536]{1,0:T(8,128)(2,1)S(1)} %get-tuple-element.85), channel_id=1, source_target_pairs={{0,40},{8,48},{16,56},{24,0},{32,8},{40,16},{48,24},{56,32},{64,10... | collective-permute-start | bytes 73736 | tf_op jit(solution)/shard_map/ppermute | solution.py:372
  56.5 21.5 %all-to-all-start.1 = ((bf16[32,16,512]{2,1,0:T(8,128)(2,1)}), bf16[32,16,512]{2,1,0:T(8,128)(2,1)S(1)}, u32[]{:S(2)}, u32[]{:S(2)}) async-start(bf16[32,16,512]{2,1,0:T(8,128)(2,1)} %regroup.1), calls=%async_computation.1 | async-start | bytes 1048576 | tf_op jit(solution)/shard_map/all_to_all | solution.py:492
  64.3 1.2 %copy-start.14 = (bf16[512,1024]{1,0:T(8,128)(2,1)S(1)}, bf16[512,1024]{1,0:T(8,128)(2,1)}, u32[]{:S(2)}) copy-start(bf16[512,1024]{1,0:T(8,128)(2,1)} %copy-done.13) | copy-start | bytes 3145732
  65.6 1.2 %copy-start.16 = (bf16[512,1024]{1,0:T(8,128)(2,1)S(1)}, bf16[512,1024]{1,0:T(8,128)(2,1)}, u32[]{:S(2)}) copy-start(bf16[512,1024]{1,0:T(8,128)(2,1)} %copy-done.15) | copy-start | bytes 3145732
  68.8 1.2 %collective-permute-start.14 = (bf16[4,8,512]{2,1,0:T(8,128)(2,1)S(1)}, bf16[4,8,512]{2,1,0:T(8,128)(2,1)S(1)}, u32[]{:S(2)}, u32[]{:S(2)}) collective-permute-start(bf16[4,8,512]{2,1,0:T(8,128)(2,1)S(1)} %get-tuple-element.92), channel_id=1, source_target_pairs={{0,1},{1,0},{2,3},{3,2},{4,5},{5,4},{6,7},{7,6},{8,9},{9,8},{10,11... | collective-permute-start | bytes 98312 | tf_op jit(solution)/shard_map/ppermute | solution.py:380
  70.1 9.9 %collective-permute-start.15 = (bf16[8,512]{1,0:T(8,128)(2,1)S(1)}, bf16[8,512]{1,0:T(8,128)(2,1)S(1)}, u32[]{:S(2)}, u32[]{:S(2)}) collective-permute-start(bf16[8,512]{1,0:T(8,128)(2,1)S(1)} %get-tuple-element.97), channel_id=1, source_target_pairs={{0,2},{1,3},{2,4},{3,5},{4,6},{5,7},{6,0},{7,1},{8,10},{9,11},{10,... | collective-permute-start | bytes 24584 | tf_op jit(solution)/shard_map/ppermute | solution.py:376
  70.4 9.6 %collective-permute-start.16 = (bf16[8,512]{1,0:T(8,128)(2,1)S(1)}, bf16[8,512]{1,0:T(8,128)(2,1)S(1)}, u32[]{:S(2)}, u32[]{:S(2)}) collective-permute-start(bf16[8,512]{1,0:T(8,128)(2,1)S(1)} %get-tuple-element.98), channel_id=1, source_target_pairs={{0,4},{1,5},{2,6},{3,7},{4,0},{5,1},{6,2},{7,3},{8,12},{9,13},{10,... | collective-permute-start | bytes 24584 | tf_op jit(solution)/shard_map/ppermute | solution.py:376
  73.0 7.0 %collective-permute-start.17 = (bf16[8,512]{1,0:T(8,128)(2,1)S(1)}, bf16[8,512]{1,0:T(8,128)(2,1)S(1)}, u32[]{:S(2)}, u32[]{:S(2)}) collective-permute-start(bf16[8,512]{1,0:T(8,128)(2,1)S(1)} %get-tuple-element.99), channel_id=1, source_target_pairs={{0,6},{1,7},{2,0},{3,1},{4,2},{5,3},{6,4},{7,5},{8,14},{9,15},{10,... | collective-permute-start | bytes 24584 | tf_op jit(solution)/shard_map/ppermute | solution.py:376

commit v4 on v3

--- a/solution.py
+++ b/solution.py
@@ -279,7 +279,7 @@
     blocks = refs[:3]
     carry, x_in, z_in, dt_in, b_in, c_in, gain = refs[3:10]
     proj = refs[10:14]
-    attn, keep, send, held, wide = refs[14:19]
+    attn, keep, send, terms, columns, held, wide = refs[14:21]
     me = lax.axis_index("replica")
     core = lax.axis_index("tensor") & 1
     for k in range(3):
@@ -304,6 +304,10 @@
     b = stacked(b_in, wide, HD)
     c = stacked(c_in, wide, HD)
     decay, drive = step_terms(dt, x, rate, bias)
+    for i, term in enumerate((decay_p, drive_p, decay, drive)):
+        terms[i] = term
+    columns[0] = jnp.transpose(b_p)
+    columns[1] = jnp.transpose(b)
     inner = decay_p * read + drive_p * jnp.sum(b_p * c, axis=-1, keepdims=True)
     inner = jnp.where(first, read, inner)
     out = decay * inner + drive * jnp.sum(b * c, axis=-1, keepdims=True) + per_head(skip) * x
@@ -336,21 +340,10 @@
         out[prompt] = came[root_of(parents, prompt)]
 
 
-def advance_body(parents, a_rate, dt_bias, state, carry, x_in, dt_in, b_in, out, wide):
+def advance_body(parents, state, terms, columns, out):
     me = lax.axis_index("replica")
-    rate = per_head(a_rate)
-    bias = per_head(dt_bias)
-    earlier = parent_rows(parents, me, carry[...], wide)
-    decay_p, drive_p = step_terms(earlier[:, 640:768], earlier[:, 0:512], rate, bias)
-    b_p = earlier[:, 512:640]
-    wide[pl.ds(0, 8), 0:HD] = jnp.zeros((8, HD), F32)
-    stacked(dt_in, wide, 8)
-    dt = wide[pl.ds(0, 8), 0:HD]
-    x = stacked(x_in, wide, 512)
-    b = stacked(b_in, wide, HD)
-    decay, drive = step_terms(dt, x, rate, bias)
-    columns_p = jnp.transpose(b_p)
-    columns = jnp.transpose(b)
+    decay_p, drive_p, decay, drive = [terms[i] for i in range(4)]
+    columns_p, columns = columns[0], columns[1]
     source = source_of(parents, 1, me)
     for s in range(4):
         root = parents[0, source * 4 + (parents[1, me * 4 + s] & 3)] & 3
@@ -491,16 +484,18 @@
     own_block, regrouped = lax.optimization_barrier((blocks[0], regrouped))
     arrived = lax.all_to_all(regrouped, "replica", 0, 0, tiled=True)
     blocks = [own_block, along_z(blocks[1], 3), along_z(blocks[2], 5)]
-    attn_out, keep, send = call(
+    attn_out, keep, send, terms, columns = call(
         mamba_body,
         "mamba",
         (
             struct((2, 4, 1024)),
             struct((4, 8, 512)),
             struct((4, 8, 512)),
+            struct((4, 8, 512), F32),
+            struct((2, 128, 8), F32),
         ),
         [SMEM] * 4 + [VMEM] * 14,
-        (VMEM,) * 3,
+        (VMEM,) * 5,
         [
             pltpu.VMEM((3, 8, BACK_LANES), BF16),
             pltpu.VMEM((16, 768), F32),
@@ -522,10 +517,9 @@
         advance_body,
         "advance",
         struct((32, 16, 512)),
-        [SMEM] * 3 + [VMEM] * 5,
+        [SMEM] + [VMEM] * 3,
         VMEM,
-        [pltpu.VMEM((16, 768), F32)],
-    )(table, a_rate, dt_bias, arrived, carry, x_in, dt_in, b_in)
+    )(table, arrived, terms, columns)
     own_part, final_state = lax.optimization_barrier((parts[0], final_state))
     mamba_out = call(last_sum_body, "last_sum", struct((2, 4, 512)), [VMEM] * 4, VMEM)(
         own_part, *[along_y(parts[k], k) for k in range(1, 4)]

time: 81.2 us -> 81 us (level)
  no operation moved by 1% of the time
where the time goes in v4:
time: 81 us; the launch traced here: 80.4 us
  starting transfers between devices  41 us (51%)
  waiting for transfers between devices  15.6 us (19%)
  Pallas kernels  12.7 us (16%)
  local copies, waits for them, and re-layouts  10.1 us (12%)
  between operations  0.93 us (1%)
    ppermute x8, starting transfers between devices, along_z(): lax.ppermute(array, 'replica', [(r, r & 24 | r + k & 7) for r in range(32)])  15.2 us
    ppermute x6, starting transfers between devices, along_x(): lax.ppermute(array, 'replica', [(r, r + 8 * k & 31) for r in range(32)])  10.3 us
    unnamed x40, local copies, waits for them, and re-layouts  10.1 us
    all_to_all x1, starting transfers between devices, per_device(): arrived = lax.all_to_all(regrouped, 'replica', 0, 0, tiled=True)  7.75 us
    all_to_all x1, waiting for transfers between devices, per_device(): arrived = lax.all_to_all(regrouped, 'replica', 0, 0, tiled=True)  4.99 us
    all_to_all x1, starting transfers between devices, per_device(): lax.all_to_all(moving.reshape(32, 16, 512), 'replica', 0, 0, tiled=True)  4.84 us
    ppermute x8, waiting for transfers between devices, along_z(): lax.ppermute(array, 'replica', [(r, r & 24 | r + k & 7) for r in range(32)])  4.18 us
    all_to_all x1, waiting for transfers between devices, per_device(): lax.all_to_all(moving.reshape(32, 16, 512), 'replica', 0, 0, tiled=True)  3.6 us
  transfers between devices with their start and end apart: 20, of which 6 were waited for; matrix products, arithmetic and copies ran while one was open for 0% of the time, Pallas kernels for 12%

profile of v4, /device:TPU:56, one launch (start us, length us, event | category | flops | bytes accessed | tf_op | source)
XLA Modules:
  0.0 80.4 jit_solution(7099402587306393319)
XLA Ops:
  0.6 1.4 %pack.1.own = bf16[8,1792]{1,0:T(8,128)(2,1)} custom-call(bf16[2,4,1024]{2,1,0:T(4,128)(2,1)} %refs_0_.1, bf16[2,4,2,128]{3,2,1,0:T(2,128)(2,1)} %refs_1_.1, bf16[2,4,128]{2,1,0:T(4,128)(2,1)} %refs_8_.1, bf16[2,4,512]{2,1,0:T(4,128)(2,1)} %refs_4_.3, bf16[2,4,128]{2,1,0:T(4,128)(2,1)} %refs_7_.1, bf16[2,4,8]{2,1,0:T(4,128)(2,1)} %refs_6_.1), custom_call_target="tpu_custom_call" | custom-call | flops 1000000 | tf_op jit(solution)/shard_map/pack/pallas_call | solution.py:399
  2.1 5.9 %collective-permute-start.1 = (bf16[8,1792]{1,0:T(8,128)(2,1)}, bf16[8,1792]{1,0:T(8,128)(2,1)S(1)}, u32[]{:S(2)}, u32[]{:S(2)}) collective-permute-start(bf16[8,1792]{1,0:T(8,128)(2,1)} %pack.1.own), channel_id=1, source_target_pairs={{0,40},{8,48},{16,56},{24,0},{32,8},{40,16},{48,24},{56,32},{64,10... | collective-permute-start | bytes 86024 | tf_op jit(solution)/shard_map/ppermute | solution.py:365
  8.0 0.1 collective-permute-start
  8.1 0.7 copy-done.9
  8.8 0.7 copy-done.10
  9.4 1.5 %table.1.parents = s32[8,128]{1,0:T(8,128)S(1)} custom-call(s32[2,128]{1,0:T(2,128)S(1)} %copy-done.9, s32[32]{0:T(128)S(1)} %copy-done.10), custom_call_target="tpu_custom_call" | custom-call | flops 1000000 | tf_op jit(solution)/shard_map/table/pallas_call | solution.py:418
  11.0 0.0 collective-permute-done.1.down
  11.0 4.1 %collective-permute-done.up = bf16[8,1792]{1,0:T(8,128)(2,1)S(1)} collective-permute-done((bf16[8,1792]{1,0:T(8,128)(2,1)}, bf16[8,1792]{1,0:T(8,128)(2,1)S(1)}, u32[]{:S(2)}, u32[]{:S(2)}) %collective-permute-start) | collective-permute-done | bytes 28704 | tf_op jit(solution)/shard_map/ppermute | solution.py:365
  15.1 0.7 copy-done.4
  15.9 1.3 %collective-permute-start.3 = (bf16[3,8,1792]{2,1,0:T(8,128)(2,1)S(1)}, bf16[3,8,1792]{2,1,0:T(8,128)(2,1)S(1)}, u32[]{:S(2)}, u32[]{:S(2)}) collective-permute-start(bf16[3,8,1792]{2,1,0:T(8,128)(2,1)S(1)} %bundle.1.own), channel_id=1, source_target_pairs={{0,56},{8,0},{16,8},{24,16},{32,24},{40,32},{48,40},{56,48},{64,12... | collective-permute-start | bytes 258056 | tf_op jit(solution)/shard_map/ppermute | solution.py:365
  17.2 0.7 collective-permute-start.2
  17.9 1.0 %copy-done.1 = bf16[4,128,512]{2,1,0:T(8,128)(2,1)S(1)} copy-done((bf16[4,128,512]{2,1,0:T(8,128)(2,1)S(1)}, bf16[4,128,512]{2,1,0:T(8,128)(2,1)}, u32[]{:S(2)}) %copy-start.1) | copy-done | bytes 524312
  18.9 1.2 %copy-done.2 = bf16[4,1024,128]{2,1,0:T(8,128)(2,1)S(1)} copy-done((bf16[4,1024,128]{2,1,0:T(8,128)(2,1)S(1)}, bf16[4,1024,128]{2,1,0:T(8,128)(2,1)}, u32[]{:S(2)}) %copy-start.2) | copy-done | bytes 1048600
  20.2 1.2 %copy-done.3 = bf16[4,1024,128]{2,1,0:T(8,128)(2,1)S(1)} copy-done((bf16[4,1024,128]{2,1,0:T(8,128)(2,1)S(1)}, bf16[4,1024,128]{2,1,0:T(8,128)(2,1)}, u32[]{:S(2)}) %copy-start.3) | copy-done | bytes 1048600
  21.4 0.2 stage.1
  21.6 0.0 collective-permute-done.3.down
  21.6 0.0 collective-permute-done.2.up
  21.7 0.6 sort_out.1
  22.3 1.6 %collective-permute-start.4 = (bf16[8,1792]{1,0:T(8,128)(2,1)S(1)}, bf16[8,1792]{1,0:T(8,128)(2,1)S(1)}, u32[]{:S(2)}, u32[]{:S(2)}) collective-permute-start(bf16[8,1792]{1,0:T(8,128)(2,1)S(1)} %get-tuple-element.67), channel_id=1, source_target_pairs={{0,64},{8,72},{16,80},{24,88},{32,96},{40,104},{48,112},{56,120},{... | collective-permute-start | bytes 86024 | tf_op jit(solution)/shard_map/ppermute | solution.py:361
  23.9 2.7 %collective-permute-start.5 = (bf16[8,1792]{1,0:T(8,128)(2,1)S(1)}, bf16[8,1792]{1,0:T(8,128)(2,1)S(1)}, u32[]{:S(2)}, u32[]{:S(2)}) collective-permute-start(bf16[8,1792]{1,0:T(8,128)(2,1)S(1)} %get-tuple-element.68), channel_id=1, source_target_pairs={{0,128},{8,136},{16,144},{24,152},{32,160},{40,168},{48,176},{56,1... | collective-permute-start | bytes 86024 | tf_op jit(solution)/shard_map/ppermute | solution.py:361
  26.6 1.4 %collective-permute-start.6 = (bf16[8,1792]{1,0:T(8,128)(2,1)S(1)}, bf16[8,1792]{1,0:T(8,128)(2,1)S(1)}, u32[]{:S(2)}, u32[]{:S(2)}) collective-permute-start(bf16[8,1792]{1,0:T(8,128)(2,1)S(1)} %get-tuple-element.69), channel_id=1, source_target_pairs={{0,192},{8,200},{16,208},{24,216},{32,224},{40,232},{48,240},{56,2... | collective-permute-start | bytes 86024 | tf_op jit(solution)/shard_map/ppermute | solution.py:361
  28.0 4.8 %all-to-all-start = ((bf16[32,16,512]{2,1,0:T(8,128)(2,1)}), bf16[32,16,512]{2,1,0:T(8,128)(2,1)S(1)}, u32[]{:S(2)}, u32[]{:S(2)}) async-start(bf16[32,16,512]{2,1,0:T(8,128)(2,1)} %bitcast.3), calls=%async_computation | async-start | bytes 1048576 | tf_op jit(solution)/shard_map/all_to_all | solution.py:446
  32.9 0.0 copy-start
  32.9 0.0 collective-permute-done.4.refs_1_
  32.9 0.0 collective-permute-done.5.refs_2_
  32.9 1.5 %attend.1 = (bf16[8,1536]{1,0:T(8,128)(2,1)S(1)}, bf16[8,384]{1,0:T(8,128)(2,1)S(1)}) custom-call(s32[8,128]{1,0:T(8,128)S(1)} %table.1.parents, bf16[8,1792]{1,0:T(8,128)(2,1)S(1)} %get-tuple-element.66.refs_0_, bf16[8,1792]{1,0:T(8,128)(2,1)S(1)} %collective-permute-done.4.refs_1_, bf16[8,1792]{1,0:T(8,128)(2,1)S(1)} %collective-permute-done.5.refs_2_, ...), custom_call_target="tpu_custom_call" | custom-call | flops 49999998976 | tf_op jit(solution)/shard_map/attend/pallas_call | solution.py:448
  34.5 0.0 copy-start.8
  34.5 0.0 copy-start.15
  34.5 0.0 copy-start.16
  34.5 0.0 copy-start.17
  34.5 0.0 copy-start.18
  34.5 0.0 copy-start.19
  34.6 2.9 %collective-permute-start.9 = (bf16[8,1536]{1,0:T(8,128)(2,1)S(1)}, bf16[8,1536]{1,0:T(8,128)(2,1)S(1)}, u32[]{:S(2)}, u32[]{:S(2)}) collective-permute-start(bf16[8,1536]{1,0:T(8,128)(2,1)S(1)} %get-tuple-element.80.own), channel_id=1, source_target_pairs={{0,192},{8,200},{16,208},{24,216},{32,224},{40,232},{48,240},{56,2... | collective-permute-start | bytes 73736 | tf_op jit(solution)/shard_map/ppermute | solution.py:361
  37.5 0.7 collective-permute-start.8
  38.2 0.9 %collective-permute-start.7 = (bf16[8,1536]{1,0:T(8,128)(2,1)S(1)}, bf16[8,1536]{1,0:T(8,128)(2,1)S(1)}, u32[]{:S(2)}, u32[]{:S(2)}) collective-permute-start(bf16[8,1536]{1,0:T(8,128)(2,1)S(1)} %get-tuple-element.80.own), channel_id=1, source_target_pairs={{0,64},{8,72},{16,80},{24,88},{32,96},{40,104},{48,112},{56,120},{... | collective-permute-start | bytes 73736 | tf_op jit(solution)/shard_map/ppermute | solution.py:361
  39.1 0.7 stage_proj.1
  39.9 1.0 %copy-done.11 = bf16[512,1024]{1,0:T(8,128)(2,1)} copy-done((bf16[512,1024]{1,0:T(8,128)(2,1)}, bf16[512,1024]{1,0:T(8,128)(2,1)S(1)}, u32[]{:S(2)}) %copy-start.11) | copy-done | bytes 1048600
  40.9 1.0 %copy-done.13 = bf16[512,1024]{1,0:T(8,128)(2,1)} copy-done((bf16[512,1024]{1,0:T(8,128)(2,1)}, bf16[512,1024]{1,0:T(8,128)(2,1)S(1)}, u32[]{:S(2)}) %copy-start.13) | copy-done | bytes 1048600
  41.9 0.0 collective-permute-done.9.three
  41.9 1.3 %collective-permute-done.8.two = bf16[8,1536]{1,0:T(8,128)(2,1)S(1)} collective-permute-done((bf16[8,1536]{1,0:T(8,128)(2,1)S(1)}, bf16[8,1536]{1,0:T(8,128)(2,1)S(1)}, u32[]{:S(2)}, u32[]{:S(2)}) %collective-permute-start.8) | collective-permute-done | bytes 24608 | tf_op jit(solution)/shard_map/ppermute | solution.py:361
  43.2 0.3 collective-permute-done.7.one
  43.5 0.6 collective-permute-start.11
  44.1 1.5 %collective-permute-start.10 = (bf16[4,8,1536]{2,1,0:T(8,128)(2,1)S(1)}, bf16[4,8,1536]{2,1,0:T(8,128)(2,1)S(1)}, u32[]{:S(2)}, u32[]{:S(2)}) collective-permute-start(bf16[4,8,1536]{2,1,0:T(8,128)(2,1)S(1)} %bundle_back.1._.own), channel_id=1, source_target_pairs={{0,8},{8,16},{16,24},{24,32},{32,40},{40,48},{48,56},{56,0},{64,72... | collective-permute-start | bytes 294920 | tf_op jit(solution)/shard_map/ppermute | solution.py:365
  45.6 3.6 %all-to-all-done.came = bf16[32,16,512]{2,1,0:T(8,128)(2,1)S(1)} async-done(((bf16[32,16,512]{2,1,0:T(8,128)(2,1)}), bf16[32,16,512]{2,1,0:T(8,128)(2,1)S(1)}, u32[]{:S(2)}, u32[]{:S(2)}) %all-to-all-start) | async-done | bytes 524320 | tf_op jit(solution)/shard_map/all_to_all | solution.py:446
  49.2 1.5 %regroup.1 = bf16[32,16,512]{2,1,0:T(8,128)(2,1)} custom-call(s32[8,128]{1,0:T(8,128)S(1)} %table.1.parents, bf16[32,16,512]{2,1,0:T(8,128)(2,1)S(1)} %all-to-all-done.came, bf16[4,8,1536]{2,1,0:T(8,128)(2,1)S(1)} %bundle_back.1._.own), custom_call_target="tpu_custom_call" | custom-call | flops 1000000 | tf_op jit(solution)/shard_map/regroup/pallas_call | solution.py:472
  50.7 0.0 collective-permute-done.11.down
  50.7 0.0 collective-permute-done.10.up
  50.7 0.7 sort_back.1
  51.3 4.3 %collective-permute-start.12 = (bf16[8,1536]{1,0:T(8,128)(2,1)S(1)}, bf16[8,1536]{1,0:T(8,128)(2,1)S(1)}, u32[]{:S(2)}, u32[]{:S(2)}) collective-permute-start(bf16[8,1536]{1,0:T(8,128)(2,1)S(1)} %get-tuple-element.86), channel_id=1, source_target_pairs={{0,24},{8,32},{16,40},{24,48},{32,56},{40,0},{48,8},{56,16},{64,88... | collective-permute-start | bytes 73736 | tf_op jit(solution)/shard_map/ppermute | solution.py:365
  55.7 0.8 collective-permute-start.13
  56.5 7.7 %all-to-all-start.1 = ((bf16[32,16,512]{2,1,0:T(8,128)(2,1)}), bf16[32,16,512]{2,1,0:T(8,128)(2,1)S(1)}, u32[]{:S(2)}, u32[]{:S(2)}) async-start(bf16[32,16,512]{2,1,0:T(8,128)(2,1)} %regroup.1), calls=%async_computation.1 | async-start | bytes 1048576 | tf_op jit(solution)/shard_map/all_to_all | solution.py:485
  64.2 0.0 collective-permute-done.13.refs_2_
  64.3 1.2 %copy-done.12 = bf16[512,1024]{1,0:T(8,128)(2,1)S(1)} copy-done((bf16[512,1024]{1,0:T(8,128)(2,1)S(1)}, bf16[512,1024]{1,0:T(8,128)(2,1)}, u32[]{:S(2)}) %copy-start.12) | copy-done | bytes 1048600
  65.6 1.2 %copy-done.14 = bf16[512,1024]{1,0:T(8,128)(2,1)S(1)} copy-done((bf16[512,1024]{1,0:T(8,128)(2,1)S(1)}, bf16[512,1024]{1,0:T(8,128)(2,1)}, u32[]{:S(2)}) %copy-start.14) | copy-done | bytes 1048600
  66.8 2.1 %mamba.1 = (bf16[2,4,1024]{2,1,0:T(4,128)(2,1)}, bf16[4,8,512]{2,1,0:T(8,128)(2,1)S(1)}, bf16[4,8,512]{2,1,0:T(8,128)(2,1)S(1)}, f32[4,8,512]{2,1,0:T(8,128)S(1)}, f32[2,128,8]{2,1,0:T(8,128)S(1)}) custom-call(s32[8,128]{1,0:T(8,128)S(1)} %table.1.parents, f32[8]{0:T(128)S(1)} %copy-done.17, f32[8]{0:T(128)S(1)} %copy-done.18, f32[8]{0:T(128)S(1)} %copy-done.19, ...), custom_call_target="tpu_custom_call" | custom-call | flops 49999998976 | tf_op jit(solution)/shard_map/mamba/pallas_call | solution.py:487
  68.9 0.0 collective-permute-start.14
  68.9 1.2 %collective-permute-done.14.came = bf16[4,8,512]{2,1,0:T(8,128)(2,1)S(1)} collective-permute-done((bf16[4,8,512]{2,1,0:T(8,128)(2,1)S(1)}, bf16[4,8,512]{2,1,0:T(8,128)(2,1)S(1)}, u32[]{:S(2)}, u32[]{:S(2)}) %collective-permute-start.14) | collective-permute-done | bytes 32800 | tf_op jit(solution)/shard_map/ppermute | solution.py:373
  70.1 0.3 collective-permute-start.15
  70.4 2.6 %collective-permute-start.16 = (bf16[8,512]{1,0:T(8,128)(2,1)S(1)}, bf16[8,512]{1,0:T(8,128)(2,1)S(1)}, u32[]{:S(2)}, u32[]{:S(2)}) collective-permute-start(bf16[8,512]{1,0:T(8,128)(2,1)S(1)} %get-tuple-element.102), channel_id=1, source_target_pairs={{0,4},{1,5},{2,6},{3,7},{4,0},{5,1},{6,2},{7,3},{8,12},{9,13},{10,... | collective-permute-start | bytes 24584 | tf_op jit(solution)/shard_map/ppermute | solution.py:369
  73.0 0.0 collective-permute-start.17
  73.0 5.0 %all-to-all-done.1.state = bf16[32,16,512]{2,1,0:T(8,128)(2,1)S(1)} async-done(((bf16[32,16,512]{2,1,0:T(8,128)(2,1)}), bf16[32,16,512]{2,1,0:T(8,128)(2,1)S(1)}, u32[]{:S(2)}, u32[]{:S(2)}) %all-to-all-start.1) | async-done | bytes 524320 | tf_op jit(solution)/shard_map/all_to_all | solution.py:485
  78.0 1.8 %advance.1 = bf16[32,16,512]{2,1,0:T(8,128)(2,1)} custom-call(s32[8,128]{1,0:T(8,128)S(1)} %table.1.parents, bf16[32,16,512]{2,1,0:T(8,128)(2,1)S(1)} %all-to-all-done.1.state, f32[4,8,512]{2,1,0:T(8,128)S(1)} %get-tuple-element.97.terms, f32[2,128,8]{2,1,0:T(8,128)S(1)} %get-tuple-element.98.columns), custom_call_target="tpu_custom_call" | custom-call | flops 1000000 | tf_op jit(solution)/shard_map/advance/pallas_call | solution.py:516
  79.7 0.0 collective-permute-done.15.b
  79.7 0.6 last_sum.1
  (30 shorter events, 0.1 us)
Async XLA Ops:
  2.1 8.9 %collective-permute-start.1 = (bf16[8,1792]{1,0:T(8,128)(2,1)}, bf16[8,1792]{1,0:T(8,128)(2,1)S(1)}, u32[]{:S(2)}, u32[]{:S(2)}) collective-permute-start(bf16[8,1792]{1,0:T(8,128)(2,1)} %pack.1.own), channel_id=1, source_target_pairs={{0,40},{8,48},{16,56},{24,0},{32,8},{40,16},{48,24},{56,32},{64,10... | collective-permute-start | bytes 86024 | tf_op jit(solution)/shard_map/ppermute | solution.py:365
  8.0 7.1 %collective-permute-start = (bf16[8,1792]{1,0:T(8,128)(2,1)}, bf16[8,1792]{1,0:T(8,128)(2,1)S(1)}, u32[]{:S(2)}, u32[]{:S(2)}) collective-permute-start(bf16[8,1792]{1,0:T(8,128)(2,1)} %pack.1.own), channel_id=1, source_target_pairs={{0,24},{8,32},{16,40},{24,48},{32,56},{40,0},{48,8},{56,16},{64,88... | collective-permute-start | bytes 86024 | tf_op jit(solution)/shard_map/ppermute | solution.py:365
  8.1 0.7 copy-start.9
  8.8 0.7 copy-start.10
  15.1 0.7 copy-start.4
  15.9 5.7 %collective-permute-start.3 = (bf16[3,8,1792]{2,1,0:T(8,128)(2,1)S(1)}, bf16[3,8,1792]{2,1,0:T(8,128)(2,1)S(1)}, u32[]{:S(2)}, u32[]{:S(2)}) collective-permute-start(bf16[3,8,1792]{2,1,0:T(8,128)(2,1)S(1)} %bundle.1.own), channel_id=1, source_target_pairs={{0,56},{8,0},{16,8},{24,16},{32,24},{40,32},{48,40},{56,48},{64,12... | collective-permute-start | bytes 258056 | tf_op jit(solution)/shard_map/ppermute | solution.py:365
  17.2 4.5 %collective-permute-start.2 = (bf16[3,8,1792]{2,1,0:T(8,128)(2,1)S(1)}, bf16[3,8,1792]{2,1,0:T(8,128)(2,1)S(1)}, u32[]{:S(2)}, u32[]{:S(2)}) collective-permute-start(bf16[3,8,1792]{2,1,0:T(8,128)(2,1)S(1)} %bundle.1.own), channel_id=1, source_target_pairs={{0,8},{8,16},{16,24},{24,32},{32,40},{40,48},{48,56},{56,0},{64,72... | collective-permute-start | bytes 258056 | tf_op jit(solution)/shard_map/ppermute | solution.py:365
  17.9 1.0 %copy-start.1 = (bf16[4,128,512]{2,1,0:T(8,128)(2,1)S(1)}, bf16[4,128,512]{2,1,0:T(8,128)(2,1)}, u32[]{:S(2)}) copy-start(bf16[4,128,512]{2,1,0:T(8,128)(2,1)} %refs_2_.2) | copy-start | bytes 1572868
  18.9 1.2 %copy-start.2 = (bf16[4,1024,128]{2,1,0:T(8,128)(2,1)S(1)}, bf16[4,1024,128]{2,1,0:T(8,128)(2,1)}, u32[]{:S(2)}) copy-start(bf16[4,1024,128]{2,1,0:T(8,128)(2,1)} %refs_0_.2) | copy-start | bytes 3145732
  20.2 1.2 %copy-start.3 = (bf16[4,1024,128]{2,1,0:T(8,128)(2,1)S(1)}, bf16[4,1024,128]{2,1,0:T(8,128)(2,1)}, u32[]{:S(2)}) copy-start(bf16[4,1024,128]{2,1,0:T(8,128)(2,1)} %refs_1_.2) | copy-start | bytes 3145732
  22.3 10.6 %collective-permute-start.4 = (bf16[8,1792]{1,0:T(8,128)(2,1)S(1)}, bf16[8,1792]{1,0:T(8,128)(2,1)S(1)}, u32[]{:S(2)}, u32[]{:S(2)}) collective-permute-start(bf16[8,1792]{1,0:T(8,128)(2,1)S(1)} %get-tuple-element.67), channel_id=1, source_target_pairs={{0,64},{8,72},{16,80},{24,88},{32,96},{40,104},{48,112},{56,120},{... | collective-permute-start | bytes 86024 | tf_op jit(solution)/shard_map/ppermute | solution.py:361
  23.9 9.0 %collective-permute-start.5 = (bf16[8,1792]{1,0:T(8,128)(2,1)S(1)}, bf16[8,1792]{1,0:T(8,128)(2,1)S(1)}, u32[]{:S(2)}, u32[]{:S(2)}) collective-permute-start(bf16[8,1792]{1,0:T(8,128)(2,1)S(1)} %get-tuple-element.68), channel_id=1, source_target_pairs={{0,128},{8,136},{16,144},{24,152},{32,160},{40,168},{48,176},{56,1... | collective-permute-start | bytes 86024 | tf_op jit(solution)/shard_map/ppermute | solution.py:361
  26.6 6.3 %collective-permute-start.6 = (bf16[8,1792]{1,0:T(8,128)(2,1)S(1)}, bf16[8,1792]{1,0:T(8,128)(2,1)S(1)}, u32[]{:S(2)}, u32[]{:S(2)}) collective-permute-start(bf16[8,1792]{1,0:T(8,128)(2,1)S(1)} %get-tuple-element.69), channel_id=1, source_target_pairs={{0,192},{8,200},{16,208},{24,216},{32,224},{40,232},{48,240},{56,2... | collective-permute-start | bytes 86024 | tf_op jit(solution)/shard_map/ppermute | solution.py:361
  28.0 21.2 %all-to-all-start = ((bf16[32,16,512]{2,1,0:T(8,128)(2,1)}), bf16[32,16,512]{2,1,0:T(8,128)(2,1)S(1)}, u32[]{:S(2)}, u32[]{:S(2)}) async-start(bf16[32,16,512]{2,1,0:T(8,128)(2,1)} %bitcast.3), calls=%async_computation | async-start | bytes 1048576 | tf_op jit(solution)/shard_map/all_to_all | solution.py:446
  32.9 6.2 %copy-start = (bf16[512,4096]{1,0:T(8,128)(2,1)S(1)}, bf16[512,4096]{1,0:T(8,128)(2,1)}, u32[]{:S(2)}) copy-start(bf16[512,4096]{1,0:T(8,128)(2,1)} %source) | copy-start | bytes 12582916
  34.5 29.8 %copy-start.5 = (bf16[2,4,512]{2,1,0:T(4,128)(2,1)S(1)}, bf16[2,4,512]{2,1,0:T(4,128)(2,1)}, u32[]{:S(2)}) copy-start(bf16[2,4,512]{2,1,0:T(4,128)(2,1)} %refs_4_.3) | copy-start | bytes 24580
  34.5 29.8 %copy-start.6 = (bf16[2,4,128]{2,1,0:T(4,128)(2,1)S(1)}, bf16[2,4,128]{2,1,0:T(4,128)(2,1)}, u32[]{:S(2)}) copy-start(bf16[2,4,128]{2,1,0:T(4,128)(2,1)} %refs_8_.1) | copy-start | bytes 6148
  34.5 29.8 %copy-start.7 = (bf16[2,4,128]{2,1,0:T(4,128)(2,1)S(1)}, bf16[2,4,128]{2,1,0:T(4,128)(2,1)}, u32[]{:S(2)}) copy-start(bf16[2,4,128]{2,1,0:T(4,128)(2,1)} %refs_7_.1) | copy-start | bytes 6148
  34.5 29.8 %copy-start.8 = (bf16[2,4,8]{2,1,0:T(4,128)(2,1)S(1)}, bf16[2,4,8]{2,1,0:T(4,128)(2,1)}, u32[]{:S(2)}) copy-start(bf16[2,4,8]{2,1,0:T(4,128)(2,1)} %refs_6_.1) | copy-start | bytes 388
  34.5 29.8 %copy-start.15 = (bf16[2,4,512]{2,1,0:T(4,128)(2,1)S(1)}, bf16[2,4,512]{2,1,0:T(4,128)(2,1)}, u32[]{:S(2)}) copy-start(bf16[2,4,512]{2,1,0:T(4,128)(2,1)} %refs_5_.3) | copy-start | bytes 24580
  34.5 29.8 %copy-start.16 = (f32[512]{0:T(512)S(1)}, f32[512]{0:T(512)}, u32[]{:S(2)}) copy-start(f32[512]{0:T(512)} %param.32) | copy-start | bytes 6148
  34.5 29.8 %copy-start.17 = (f32[8]{0:T(128)S(1)}, f32[8]{0:T(128)}, u32[]{:S(2)}) copy-start(f32[8]{0:T(128)} %a_rate.1) | copy-start | bytes 100
  34.5 29.8 %copy-start.18 = (f32[8]{0:T(128)S(1)}, f32[8]{0:T(128)}, u32[]{:S(2)}) copy-start(f32[8]{0:T(128)} %dt_bias.1) | copy-start | bytes 100
  34.5 29.8 %copy-start.19 = (f32[8]{0:T(128)S(1)}, f32[8]{0:T(128)}, u32[]{:S(2)}) copy-start(f32[8]{0:T(128)} %skip.1) | copy-start | bytes 100
  34.6 7.3 %collective-permute-start.9 = (bf16[8,1536]{1,0:T(8,128)(2,1)S(1)}, bf16[8,1536]{1,0:T(8,128)(2,1)S(1)}, u32[]{:S(2)}, u32[]{:S(2)}) collective-permute-start(bf16[8,1536]{1,0:T(8,128)(2,1)S(1)} %get-tuple-element.80.own), channel_id=1, source_target_pairs={{0,192},{8,200},{16,208},{24,216},{32,224},{40,232},{48,240},{56,2... | collective-permute-start | bytes 73736 | tf_op jit(solution)/shard_map/ppermute | solution.py:361
  37.5 5.7 %collective-permute-start.8 = (bf16[8,1536]{1,0:T(8,128)(2,1)S(1)}, bf16[8,1536]{1,0:T(8,128)(2,1)S(1)}, u32[]{:S(2)}, u32[]{:S(2)}) collective-permute-start(bf16[8,1536]{1,0:T(8,128)(2,1)S(1)} %get-tuple-element.80.own), channel_id=1, source_target_pairs={{0,128},{8,136},{16,144},{24,152},{32,160},{40,168},{48,176},{56,1... | collective-permute-start | bytes 73736 | tf_op jit(solution)/shard_map/ppermute | solution.py:361
  38.2 5.3 %collective-permute-start.7 = (bf16[8,1536]{1,0:T(8,128)(2,1)S(1)}, bf16[8,1536]{1,0:T(8,128)(2,1)S(1)}, u32[]{:S(2)}, u32[]{:S(2)}) collective-permute-start(bf16[8,1536]{1,0:T(8,128)(2,1)S(1)} %get-tuple-element.80.own), channel_id=1, source_target_pairs={{0,64},{8,72},{16,80},{24,88},{32,96},{40,104},{48,112},{56,120},{... | collective-permute-start | bytes 73736 | tf_op jit(solution)/shard_map/ppermute | solution.py:361
  39.8 1.0 %copy-start.11 = (bf16[512,1024]{1,0:T(8,128)(2,1)}, bf16[512,1024]{1,0:T(8,128)(2,1)S(1)}, u32[]{:S(2)}) copy-start(bf16[512,1024]{1,0:T(8,128)(2,1)S(1)} %get-tuple-element.91.refs_12_) | copy-start | bytes 3145732
  40.9 1.0 %copy-start.13 = (bf16[512,1024]{1,0:T(8,128)(2,1)}, bf16[512,1024]{1,0:T(8,128)(2,1)S(1)}, u32[]{:S(2)}) copy-start(bf16[512,1024]{1,0:T(8,128)(2,1)S(1)} %get-tuple-element.92.refs_13_) | copy-start | bytes 3145732
  43.5 7.2 %collective-permute-start.11 = (bf16[4,8,1536]{2,1,0:T(8,128)(2,1)S(1)}, bf16[4,8,1536]{2,1,0:T(8,128)(2,1)S(1)}, u32[]{:S(2)}, u32[]{:S(2)}) collective-permute-start(bf16[4,8,1536]{2,1,0:T(8,128)(2,1)S(1)} %bundle_back.1._.own), channel_id=1, source_target_pairs={{0,56},{8,0},{16,8},{24,16},{32,24},{40,32},{48,40},{56,48},{64,12... | collective-permute-start | bytes 294920 | tf_op jit(solution)/shard_map/ppermute | solution.py:365
  44.1 6.6 %collective-permute-start.10 = (bf16[4,8,1536]{2,1,0:T(8,128)(2,1)S(1)}, bf16[4,8,1536]{2,1,0:T(8,128)(2,1)S(1)}, u32[]{:S(2)}, u32[]{:S(2)}) collective-permute-start(bf16[4,8,1536]{2,1,0:T(8,128)(2,1)S(1)} %bundle_back.1._.own), channel_id=1, source_target_pairs={{0,8},{8,16},{16,24},{24,32},{32,40},{40,48},{48,56},{56,0},{64,72... | collective-permute-start | bytes 294920 | tf_op jit(solution)/shard_map/ppermute | solution.py:365
  51.3 12.9 %collective-permute-start.12 = (bf16[8,1536]{1,0:T(8,128)(2,1)S(1)}, bf16[8,1536]{1,0:T(8,128)(2,1)S(1)}, u32[]{:S(2)}, u32[]{:S(2)}) collective-permute-start(bf16[8,1536]{1,0:T(8,128)(2,1)S(1)} %get-tuple-element.86), channel_id=1, source_target_pairs={{0,24},{8,32},{16,40},{24,48},{32,56},{40,0},{48,8},{56,16},{64,88... | collective-permute-start | bytes 73736 | tf_op jit(solution)/shard_map/ppermute | solution.py:365
  55.7 8.6 %collective-permute-start.13 = (bf16[8,1536]{1,0:T(8,128)(2,1)S(1)}, bf16[8,1536]{1,0:T(8,128)(2,1)S(1)}, u32[]{:S(2)}, u32[]{:S(2)}) collective-permute-start(bf16[8,1536]{1,0:T(8,128)(2,1)S(1)} %get-tuple-element.87), channel_id=1, source_target_pairs={{0,40},{8,48},{16,56},{24,0},{32,8},{40,16},{48,24},{56,32},{64,10... | collective-permute-start | bytes 73736 | tf_op jit(solution)/shard_map/ppermute | solution.py:365
  56.5 21.5 %all-to-all-start.1 = ((bf16[32,16,512]{2,1,0:T(8,128)(2,1)}), bf16[32,16,512]{2,1,0:T(8,128)(2,1)S(1)}, u32[]{:S(2)}, u32[]{:S(2)}) async-start(bf16[32,16,512]{2,1,0:T(8,128)(2,1)} %regroup.1), calls=%async_computation.1 | async-start | bytes 1048576 | tf_op jit(solution)/shard_map/all_to_all | solution.py:485
  64.3 1.2 %copy-start.12 = (bf16[512,1024]{1,0:T(8,128)(2,1)S(1)}, bf16[512,1024]{1,0:T(8,128)(2,1)}, u32[]{:S(2)}) copy-start(bf16[512,1024]{1,0:T(8,128)(2,1)} %copy-done.11) | copy-start | bytes 3145732
  65.6 1.2 %copy-start.14 = (bf16[512,1024]{1,0:T(8,128)(2,1)S(1)}, bf16[512,1024]{1,0:T(8,128)(2,1)}, u32[]{:S(2)}) copy-start(bf16[512,1024]{1,0:T(8,128)(2,1)} %copy-done.13) | copy-start | bytes 3145732
  68.9 1.2 %collective-permute-start.14 = (bf16[4,8,512]{2,1,0:T(8,128)(2,1)S(1)}, bf16[4,8,512]{2,1,0:T(8,128)(2,1)S(1)}, u32[]{:S(2)}, u32[]{:S(2)}) collective-permute-start(bf16[4,8,512]{2,1,0:T(8,128)(2,1)S(1)} %get-tuple-element.94), channel_id=1, source_target_pairs={{0,1},{1,0},{2,3},{3,2},{4,5},{5,4},{6,7},{7,6},{8,9},{9,8},{10,11... | collective-permute-start | bytes 98312 | tf_op jit(solution)/shard_map/ppermute | solution.py:373
  70.1 9.6 %collective-permute-start.15 = (bf16[8,512]{1,0:T(8,128)(2,1)S(1)}, bf16[8,512]{1,0:T(8,128)(2,1)S(1)}, u32[]{:S(2)}, u32[]{:S(2)}) collective-permute-start(bf16[8,512]{1,0:T(8,128)(2,1)S(1)} %get-tuple-element.101), channel_id=1, source_target_pairs={{0,2},{1,3},{2,4},{3,5},{4,6},{5,7},{6,0},{7,1},{8,10},{9,11},{10,... | collective-permute-start | bytes 24584 | tf_op jit(solution)/shard_map/ppermute | solution.py:369
  70.4 9.3 %collective-permute-start.16 = (bf16[8,512]{1,0:T(8,128)(2,1)S(1)}, bf16[8,512]{1,0:T(8,128)(2,1)S(1)}, u32[]{:S(2)}, u32[]{:S(2)}) collective-permute-start(bf16[8,512]{1,0:T(8,128)(2,1)S(1)} %get-tuple-element.102), channel_id=1, source_target_pairs={{0,4},{1,5},{2,6},{3,7},{4,0},{5,1},{6,2},{7,3},{8,12},{9,13},{10,... | collective-permute-start | bytes 24584 | tf_op jit(solution)/shard_map/ppermute | solution.py:369
  73.0 6.8 %collective-permute-start.17 = (bf16[8,512]{1,0:T(8,128)(2,1)S(1)}, bf16[8,512]{1,0:T(8,128)(2,1)S(1)}, u32[]{:S(2)}, u32[]{:S(2)}) collective-permute-start(bf16[8,512]{1,0:T(8,128)(2,1)S(1)} %get-tuple-element.103), channel_id=1, source_target_pairs={{0,6},{1,7},{2,0},{3,1},{4,2},{5,3},{6,4},{7,5},{8,14},{9,15},{10,... | collective-permute-start | bytes 24584 | tf_op jit(solution)/shard_map/ppermute | solution.py:369
